TPU v7x, 32 devices: a whole 2x2x4 slice. The times are simulated.
32 devices in a mesh: dp: 4 (over z), unit: 8 (over y, x, core).
Axes of the slice: x: 2, y: 2, z: 4, core: 2. Of those that a mesh axis runs over, the one named last changes fastest.
Arguments:
- token_ids: int32 [32, 1024], P(('dp', 'unit')), may hold values from 0 to 30719
- segment_ids: int32 [32, 1024], P(('dp', 'unit')), may hold values from 0 to 15, never falling along the last dimension, each value on 1 to 256 neighbouring positions
- real_mask: int32 [32, 1024], replicated, may hold values from 0 to 1, as said below
- positions: int32 [32, 64], P(('dp', 'unit')), may hold values from 0 to 1023
- targets: int32 [32, 64], replicated, may hold values from 0 to 30719
- teacher_states: bfloat16 [32, 1024, 768], P(('dp', 'unit')), may hold values from -6 to 6
- head_gate: float32 [2, 12], replicated, may hold values from 0.2 to 1
- layer_gate: float32 [2, 2], replicated, may hold values from 0.5 to 1
- hidden_gate: float32 [768], replicated, may hold values from 0.3 to 1
- unit_gate: float32 [2, 3072], replicated, may hold values from 0.2 to 1
- unit_keep: int32 [2, 3072], replicated, may hold values 0 or 1
- embedding: float32 [30720, 768], P('unit')
- attention: float32 [2, 4, 768, 768], replicated, may hold values from -0.21875 to 0.21875
- feed_forward: float32 [2, 2, 3072, 768], P(None, None, 'unit'), may hold values from -0.21875 to 0.21875
- map_weight: float32 [768, 768], replicated, may hold values from -0.21875 to 0.21875
- norm_params: float32 [10, 768], replicated, may hold values from 0.5 to 1.5
- embedding_rows: float32 [30720], P('unit'), may hold values from 1.7156695e-12 to 2.7450712e-11
- embedding_cols: float32 [768], replicated, may hold values from 4.2891737e-13 to 6.862678e-12
- attention_rows: float32 [2, 4, 768], P(None, None, 'unit'), may hold values from 1.7156695e-12 to 2.7450712e-11
- attention_cols: float32 [2, 4, 768], replicated, may hold values from 1.7156695e-12 to 2.7450712e-11
- feed_rows: float32 [2, 2, 3072], P(None, None, 'unit'), may hold values from 1.7156695e-12 to 2.7450712e-11
- feed_cols: float32 [2, 2, 768], replicated, may hold values from 1.7156695e-12 to 2.7450712e-11
- map_rows: float32 [768], P('unit'), may hold values from 1.7156695e-12 to 2.7450712e-11
- map_cols: float32 [768], replicated, may hold values from 1.7156695e-12 to 2.7450712e-11
- norm_moment: float32 [10, 768], replicated, may hold values from 2.7450712e-11 to 4.3463627e-10
Outputs:
- total_loss: float32 [], replicated
- real_count: float32 [], replicated
- grad_norm: float32 [], replicated
- new_embedding: float32 [30720, 768], P('unit')
- embedding_grad: float32 [30720, 768], P('unit')
- new_embedding_rows: float32 [30720], P('unit')
- new_embedding_cols: float32 [768], replicated
- new_attention: float32 [2, 4, 768, 768], P(None, None, 'unit')
- attention_grad: float32 [2, 4, 768, 768], P(None, None, 'unit')
- new_attention_rows: float32 [2, 4, 768], P(None, None, 'unit')
- new_attention_cols: float32 [2, 4, 768], replicated
- new_feed_forward: float32 [2, 2, 3072, 768], P(None, None, 'unit')
- feed_grad: float32 [2, 2, 3072, 768], P(None, None, 'unit')
- new_feed_rows: float32 [2, 2, 3072], P(None, None, 'unit')
- new_feed_cols: float32 [2, 2, 768], replicated
- new_map: float32 [768, 768], P('unit')
- map_grad: float32 [768, 768], P('unit')
- new_map_rows: float32 [768], P('unit')
- new_map_cols: float32 [768], replicated
- new_norm_params: float32 [10, 768], replicated
- norm_grad: float32 [10, 768], replicated
- new_norm_moment: float32 [10, 768], replicated
Inputs may be any that keep to these rules, and one draw needn't show every extreme that they name: `real_mask`: position 0 of every sequence is real.
All inputs are finite; a program needn't handle non-finite values.
Results may differ from a plain program's by a relative error of at most 0.0061.
Values may be sent and summed in bfloat16 or wider, within the bound.
No kernel may reach another device: no remote copies, remote signals or barrier semaphores. Data moves between devices by JAX's collectives and lax.ppermute only.
A program may use at most 640 MiB of HBM per device.

v0:
```python
import math

import jax
import jax.numpy as jnp
from jax import lax
from jax.sharding import PartitionSpec as P

H = 12
HD = 64


LN_EPS = 1e-06
ADA_EPS = 1e-30
DECAY_RATE = 0.95
LEARN_RATE = 0.015
CLIP_LIMIT = 0.05
MASK_FILL = 1e30


def shifted(value, axis, steps):
    count = lax.axis_size(axis)
    pairs = [(source, (source + steps) % count) for source in range(count)]
    return lax.ppermute(value, axis, pairs)


def combined_all(shard, axis, combine):
    everything = jax.tree.map(lambda part: lax.all_gather(part, axis), shard)
    initial = jax.tree.map(lambda part: part[0], everything)

    def turn(k, so_far):
        return combine(so_far, jax.tree.map(lambda part: part[k], everything))

    return lax.fori_loop(1, lax.axis_size(axis), turn, initial)


def norm_forward(value, gain, shift):
    centered = value - jnp.mean(value, axis=-1, keepdims=True)
    inverse = lax.rsqrt(jnp.mean(centered * centered, axis=-1, keepdims=True) + LN_EPS)
    normed = centered * inverse
    return (normed * gain + shift, (normed, inverse))


def norm_backward(stored, gain, upstream):
    normed, inverse = stored
    scaled = upstream * gain
    inner = (
        scaled
        - jnp.mean(scaled, axis=-1, keepdims=True)
        - normed * jnp.mean(scaled * normed, axis=-1, keepdims=True)
    )
    return (inverse * inner, jnp.sum(upstream * normed, axis=0), jnp.sum(upstream, axis=0))


def block_scores(query_block, keys, segments, real_rows, first_row, block_len, score_scale):
    raw_scores = (
        jnp.einsum("sqhd,skhd->shqk", query_block, keys, preferred_element_type=jnp.float32)
        * score_scale
    )
    seg_query = lax.dynamic_slice_in_dim(segments, first_row, block_len, 1)
    place_query = first_row + jnp.arange(block_len)
    place_key = jnp.arange(segments.shape[1])
    same_item = seg_query[:, :, None] == segments[:, None, :]
    key_usable = (real_rows[:, None, :] > 0.5) | (place_query[:, None] == place_key[None, :])[None]
    return jnp.where((same_item & key_usable)[:, None], raw_scores, -MASK_FILL)


def attend(query, keys, values, segments, real_rows, score_scale):
    seq_count, length = segments.shape
    block_len = min(512, length)

    def one_block(block_at):
        first_row = block_at * block_len
        query_block = lax.dynamic_slice_in_dim(query, first_row, block_len, 1)
        scores = block_scores(
            query_block, keys, segments, real_rows, first_row, block_len, score_scale
        )
        row_max = jnp.max(scores, axis=-1, keepdims=True)
        exponent = jnp.exp(scores - row_max)
        sum_exp = jnp.sum(exponent, axis=-1, keepdims=True)
        probability = (exponent / sum_exp).astype(jnp.bfloat16)
        result = jnp.einsum(
            "shqk,skhd->sqhd", probability, values, preferred_element_type=jnp.float32
        )
        return (result, (row_max + jnp.log(sum_exp))[..., 0])

    results, log_totals = lax.map(one_block, jnp.arange(length // block_len))
    result = jnp.moveaxis(results, 0, 1).reshape(query.shape)
    log_total = jnp.moveaxis(log_totals, 0, 2).reshape(seq_count, query.shape[2], length)
    return (result, log_total)


def attend_back(query, keys, values, grad_out, log_total, segments, real_rows, score_scale):
    seq_count, length = segments.shape
    block_len = min(512, length)

    def one_block(running, block_at):
        grad_keys, grad_values = running
        first_row = block_at * block_len
        query_block = lax.dynamic_slice_in_dim(query, first_row, block_len, 1)
        grad_block = lax.dynamic_slice_in_dim(grad_out, first_row, block_len, 1)
        total_block = lax.dynamic_slice_in_dim(log_total, first_row, block_len, 2)
        scores = block_scores(
            query_block, keys, segments, real_rows, first_row, block_len, score_scale
        )
        probability = jnp.exp(scores - total_block[..., None])
        grad_values = grad_values + jnp.einsum(
            "shqk,sqhd->skhd",
            probability.astype(jnp.bfloat16),
            grad_block,
            preferred_element_type=jnp.float32,
        )
        grad_prob = jnp.einsum(
            "sqhd,skhd->shqk", grad_block, values, preferred_element_type=jnp.float32
        )
        inner = jnp.sum(probability * grad_prob, axis=-1, keepdims=True)
        grad_scores = (probability * (grad_prob - inner)).astype(jnp.bfloat16)
        grad_query = (
            jnp.einsum("shqk,skhd->sqhd", grad_scores, keys, preferred_element_type=jnp.float32)
            * score_scale
        )
        grad_keys = (
            grad_keys
            + jnp.einsum(
                "shqk,sqhd->skhd", grad_scores, query_block, preferred_element_type=jnp.float32
            )
            * score_scale
        )
        return ((grad_keys, grad_values), grad_query)

    zeros_like_keys = jnp.zeros(keys.shape, jnp.float32)
    (grad_keys, grad_values), grad_queries = lax.scan(
        one_block, (zeros_like_keys, zeros_like_keys), jnp.arange(length // block_len)
    )
    grad_query = jnp.moveaxis(grad_queries, 0, 1).reshape(query.shape)
    return (grad_query, grad_keys, grad_values)


def attention_forward(hidden, weights, head_scale, segments, real_rows):
    seq_count, length = segments.shape
    hidden_low = hidden.astype(jnp.bfloat16)
    projected = jnp.einsum(
        "rd,jde->jre", hidden_low, weights[:3], preferred_element_type=jnp.float32
    ).astype(jnp.bfloat16)
    head_split = projected.reshape(3, seq_count, length, H, HD)
    mixed, log_total = attend(
        head_split[0], head_split[1], head_split[2], segments, real_rows, 1.0 / math.sqrt(HD)
    )
    gated_low = (mixed.reshape(hidden.shape) * head_scale).astype(jnp.bfloat16)
    branch = jnp.dot(gated_low, weights[3], preferred_element_type=jnp.float32)
    return (branch, (hidden_low, projected, gated_low, log_total))


def attention_backward(grad_branch, stored, weights, head_scale, segments, real_rows):
    hidden_low, projected, gated_low, log_total = stored
    seq_count, length = segments.shape
    grad_out_proj = jnp.einsum(
        "rd,re->de", gated_low, grad_branch, preferred_element_type=jnp.float32
    )
    grad_gated = jnp.einsum(
        "re,de->rd", grad_branch, weights[3], preferred_element_type=jnp.float32
    )
    grad_mixed = (grad_gated * head_scale).astype(jnp.bfloat16).reshape(seq_count, length, H, HD)
    head_split = projected.reshape(3, seq_count, length, H, HD)
    grad_query, grad_keys, grad_values = attend_back(
        head_split[0],
        head_split[1],
        head_split[2],
        grad_mixed,
        log_total,
        segments,
        real_rows,
        1.0 / math.sqrt(HD),
    )
    grad_proj = (
        jnp.stack([grad_query, grad_keys, grad_values])
        .astype(jnp.bfloat16)
        .reshape(projected.shape)
    )
    grad_in_proj = jnp.einsum(
        "rd,jre->jde", hidden_low, grad_proj, preferred_element_type=jnp.float32
    )
    grad_input = jnp.einsum(
        "jre,jde->rd", grad_proj, weights[:3], preferred_element_type=jnp.float32
    )
    return (grad_input, jnp.concatenate([grad_in_proj, grad_out_proj[None]], axis=0))


def feed_forward_pass(hidden_low, unit_weights, unit_scale):
    pre_act = jnp.einsum(
        "gd,fd->gf", hidden_low, unit_weights[0], preferred_element_type=jnp.float32
    )
    activated = (jax.nn.gelu(pre_act, approximate=False) * unit_scale).astype(jnp.bfloat16)
    result = jnp.dot(activated, unit_weights[1], preferred_element_type=jnp.float32)
    return (result, (hidden_low, pre_act, activated))


def feed_forward_back(grad_low, stored, unit_weights, unit_scale):
    gathered, pre_act, activated = stored
    grad_act = jnp.einsum(
        "gd,fd->gf", grad_low, unit_weights[1], preferred_element_type=jnp.float32
    )
    grad_down = jnp.einsum("gf,gd->fd", activated, grad_low, preferred_element_type=jnp.float32)
    _, gelu_pull = jax.vjp(lambda value: jax.nn.gelu(value, approximate=False), pre_act)
    grad_pre = gelu_pull(grad_act * unit_scale)[0].astype(jnp.bfloat16)
    grad_up = jnp.einsum("gf,gd->fd", grad_pre, gathered, preferred_element_type=jnp.float32)
    grad_input = jnp.dot(grad_pre, unit_weights[0], preferred_element_type=jnp.float32)
    return (grad_input, jnp.stack([grad_up, grad_down]))


def merge_softmax(first_part, second_part):
    row_max = jnp.maximum(first_part[0], second_part[0])
    sum_exp = first_part[1] * jnp.exp(first_part[0] - row_max) + second_part[1] * jnp.exp(
        second_part[0] - row_max
    )
    return (row_max, sum_exp, first_part[2] + second_part[2])


def factored(weight, gradient, row_stats, col_stats, col_total, row_total, clip_factor, height):
    squares = gradient * gradient + ADA_EPS
    new_rows = DECAY_RATE * row_stats + (1 - DECAY_RATE) * jnp.mean(squares, axis=-1)
    breadth = gradient.shape[-1]
    new_cols = DECAY_RATE * col_stats + (1 - DECAY_RATE) * (
        clip_factor * clip_factor * col_total / height + ADA_EPS
    )
    mean_rows = DECAY_RATE * row_total / height + (1 - DECAY_RATE) * (
        clip_factor * clip_factor * jnp.sum(col_total, axis=-1) / (height * breadth) + ADA_EPS
    )
    second = new_rows[..., :, None] * new_cols[..., None, :] / mean_rows[..., None, None]
    return (weight - LEARN_RATE * gradient * lax.rsqrt(second), new_rows, new_cols)


def local(
    token_ids,
    segment_ids,
    real_mask,
    positions,
    targets,
    teacher_states,
    head_gate,
    layer_gate,
    hidden_gate,
    unit_gate,
    unit_keep,
    embedding,
    attention,
    feed_forward,
    map_weight,
    norm_params,
    embedding_rows,
    embedding_cols,
    attention_rows,
    attention_cols,
    feed_rows,
    feed_cols,
    map_rows,
    map_cols,
    norm_moment,
):
    unit_count = lax.axis_size("unit")
    data_count = lax.axis_size("dp")
    unit_at = lax.axis_index("unit")
    data_at = lax.axis_index("dp")
    seq_count, length = token_ids.shape
    rows_dev = seq_count * length
    pick_count = positions.shape[1]
    breadth = embedding.shape[1]
    vocab_dev = embedding.shape[0]
    units_dev = feed_forward.shape[2]
    layer_count = attention.shape[0]
    slab_rows = breadth // unit_count
    group_first = data_at * unit_count * seq_count
    real_rows = lax.dynamic_slice_in_dim(
        real_mask, group_first + unit_at * seq_count, seq_count, 0
    ).astype(jnp.float32)
    real_flat = real_rows.reshape(rows_dev)
    count = jnp.sum(real_mask).astype(jnp.float32)
    scale_all = unit_gate * unit_keep.astype(jnp.float32)
    feed_low = lax.all_gather(feed_forward.astype(jnp.bfloat16), "unit", axis=2, tiled=True)
    teacher = (
        shifted(teacher_states, "unit", unit_count // 2)
        .astype(jnp.float32)
        .reshape(rows_dev, breadth)
    )
    table_low = embedding.astype(jnp.bfloat16)
    token_flat = token_ids.reshape(rows_dev)
    portion = lax.all_gather(table_low, "unit", axis=0, tiled=True)
    relative = token_flat
    inside = (relative >= 0) & (relative < portion.shape[0])
    picked = jnp.take(portion, jnp.where(inside, relative, 0), axis=0).astype(jnp.float32)
    looked = jnp.where(inside[:, None], picked, 0.0)
    normed, embed_stored = norm_forward(looked, norm_params[0], norm_params[1])
    hidden = normed * hidden_gate
    head_scale = jnp.repeat(head_gate, HD, axis=1)
    attention_low = attention.astype(jnp.bfloat16)
    stored_layers = []
    for layer_at in range(layer_count):
        branch, attn_stored = attention_forward(
            hidden, attention_low[layer_at], head_scale[layer_at], segment_ids, real_rows
        )
        middle, norm_first = norm_forward(
            hidden + branch * layer_gate[layer_at, 0] * hidden_gate,
            norm_params[2 + 4 * layer_at],
            norm_params[3 + 4 * layer_at],
        )
        result, feed_stored = feed_forward_pass(
            middle.astype(jnp.bfloat16), feed_low[layer_at], scale_all[layer_at]
        )
        hidden, norm_second = norm_forward(
            middle + result * layer_gate[layer_at, 1] * hidden_gate,
            norm_params[4 + 4 * layer_at],
            norm_params[5 + 4 * layer_at],
        )
        stored_layers.append((attn_stored, norm_first, feed_stored, norm_second))
    final = hidden.astype(jnp.bfloat16)
    map_low = map_weight.astype(jnp.bfloat16)
    mapped = jnp.dot(final, map_low, preferred_element_type=jnp.float32)
    diff = mapped - teacher
    error_part = jnp.sum(jnp.sum(diff * diff, axis=-1) * real_flat) / breadth
    grad_mapped = (diff * (2.0 / (breadth * count)) * real_flat[:, None]).astype(jnp.bfloat16)
    grad_map = jnp.einsum("rd,re->de", final, grad_mapped, preferred_element_type=jnp.float32)
    grad_final = jnp.einsum("re,de->rd", grad_mapped, map_low, preferred_element_type=jnp.float32)
    flat_pos = (positions + jnp.arange(seq_count)[:, None] * length).reshape(-1)
    picked_rows = lax.all_gather(jnp.take(final, flat_pos, axis=0), "unit", axis=0, tiled=True)
    target_all = lax.dynamic_slice_in_dim(targets, group_first, unit_count * seq_count, 0).reshape(
        -1
    )
    logits = jnp.einsum("pd,vd->pv", picked_rows, table_low, preferred_element_type=jnp.float32)
    is_target = (target_all - unit_at * vocab_dev)[:, None] == jnp.arange(vocab_dev)[None, :]
    row_max = jnp.max(logits, axis=1)
    sum_exp = jnp.sum(jnp.exp(logits - row_max[:, None]), axis=1)
    target_logit = jnp.sum(jnp.where(is_target, logits, 0.0), axis=1)
    row_max, sum_exp, target_logit = combined_all(
        (row_max, sum_exp, target_logit), "unit", merge_softmax
    )
    log_total = row_max + jnp.log(sum_exp)
    own_terms = lax.dynamic_slice_in_dim(
        log_total - target_logit, unit_at * seq_count * pick_count, seq_count * pick_count, 0
    )
    loss_part = error_part + jnp.sum(own_terms)
    grad_logits = (
        (jnp.exp(logits - log_total[:, None]) - is_target.astype(jnp.float32)) / count
    ).astype(jnp.bfloat16)
    grad_table = jnp.einsum(
        "pv,pd->vd", grad_logits, picked_rows, preferred_element_type=jnp.float32
    )
    grad_picked = lax.psum_scatter(
        jnp.einsum("pv,vd->pd", grad_logits, table_low, preferred_element_type=jnp.float32),
        "unit",
        scatter_dimension=0,
        tiled=True,
    )
    grad_hidden = grad_final.at[flat_pos].add(grad_picked)
    gain_rows = [None] * norm_params.shape[0]
    attn_grads = [None] * layer_count
    feed_grads = [None] * layer_count
    for layer_at in reversed(range(layer_count)):
        attn_stored, norm_first, feed_stored, norm_second = stored_layers[layer_at]
        grad_second, gain_rows[4 + 4 * layer_at], gain_rows[5 + 4 * layer_at] = norm_backward(
            norm_second, norm_params[4 + 4 * layer_at], grad_hidden
        )
        grad_result = (grad_second * layer_gate[layer_at, 1] * hidden_gate).astype(jnp.bfloat16)
        grad_middle, feed_grads[layer_at] = feed_forward_back(
            grad_result, feed_stored, feed_low[layer_at], scale_all[layer_at]
        )
        grad_first, gain_rows[2 + 4 * layer_at], gain_rows[3 + 4 * layer_at] = norm_backward(
            norm_first, norm_params[2 + 4 * layer_at], grad_second + grad_middle
        )
        grad_branch = (grad_first * layer_gate[layer_at, 0] * hidden_gate).astype(jnp.bfloat16)
        grad_input, attn_grads[layer_at] = attention_backward(
            grad_branch,
            attn_stored,
            attention_low[layer_at],
            head_scale[layer_at],
            segment_ids,
            real_rows,
        )
        grad_hidden = grad_first + grad_input
    grad_looked, gain_rows[0], gain_rows[1] = norm_backward(
        embed_stored, norm_params[0], grad_hidden * hidden_gate
    )
    grad_norms = jnp.stack(gain_rows)
    grad_attention = jnp.stack(attn_grads)
    grad_feed = jnp.stack(feed_grads)
    block_rows = vocab_dev + layer_count * 4 * slab_rows + slab_rows + layer_count * 2 * units_dev

    def owner_rows(owner_at):
        portions = []
        relative = token_flat - owner_at * vocab_dev
        inside = (relative >= 0) & (relative < vocab_dev)
        portions.append(
            jax.ops.segment_sum(
                grad_looked, jnp.where(inside, relative, vocab_dev), num_segments=vocab_dev
            )
        )
        portions.append(
            lax.dynamic_slice_in_dim(grad_attention, owner_at * slab_rows, slab_rows, 2).reshape(
                -1, breadth
            )
        )
        portions.append(lax.dynamic_slice_in_dim(grad_map, owner_at * slab_rows, slab_rows, 0))
        portions.append(
            lax.dynamic_slice_in_dim(grad_feed, owner_at * units_dev, units_dev, 2).reshape(
                -1, breadth
            )
        )
        return jnp.concatenate(portions, axis=0)

    owners = jnp.arange(lax.axis_size("unit") * block_rows // block_rows)
    reduced = lax.psum_scatter(
        lax.map(owner_rows, owners)
        .reshape(lax.axis_size("unit") * block_rows, breadth)
        .astype(jnp.bfloat16),
        "unit",
        scatter_dimension=0,
        tiled=True,
    ).astype(jnp.float32)
    embed_grad = reduced[:vocab_dev] + grad_table
    cursor = vocab_dev
    attn_grad = reduced[cursor : cursor + layer_count * 4 * slab_rows].reshape(
        layer_count, 4, slab_rows, breadth
    )
    cursor = cursor + layer_count * 4 * slab_rows
    map_grad = reduced[cursor : cursor + slab_rows]
    cursor = cursor + slab_rows
    feed_grad = reduced[cursor : cursor + layer_count * 2 * units_dev].reshape(
        layer_count, 2, units_dev, breadth
    )
    embed_grad, attn_grad, map_grad, feed_grad = lax.psum(
        (embed_grad, attn_grad, map_grad, feed_grad), "dp"
    )
    square_part = (
        jnp.sum(embed_grad * embed_grad)
        + jnp.sum(attn_grad * attn_grad)
        + jnp.sum(map_grad * map_grad)
        + jnp.sum(feed_grad * feed_grad)
    ) / data_count
    (
        grad_norms,
        total_loss,
        square_sum,
        embed_colsum,
        attn_colsum,
        map_colsum,
        feed_colsum,
        embed_rowsum,
        attn_rowsum,
        map_rowsum,
        feed_rowsum,
    ) = lax.psum(
        (
            grad_norms,
            loss_part,
            square_part,
            jnp.sum(embed_grad * embed_grad, axis=0) / data_count,
            jnp.sum(attn_grad * attn_grad, axis=2) / data_count,
            jnp.sum(map_grad * map_grad, axis=0) / data_count,
            jnp.sum(feed_grad * feed_grad, axis=2) / data_count,
            jnp.sum(embedding_rows) / data_count,
            jnp.sum(attention_rows, axis=-1) / data_count,
            jnp.sum(map_rows) / data_count,
            jnp.sum(feed_rows, axis=-1) / data_count,
        ),
        ("dp", "unit"),
    )
    grad_norm = jnp.sqrt(square_sum + jnp.sum(grad_norms * grad_norms))
    clip_factor = jnp.minimum(1.0, CLIP_LIMIT / grad_norm)
    embed_grad = embed_grad * clip_factor
    attn_grad = attn_grad * clip_factor
    map_grad = map_grad * clip_factor
    feed_grad = feed_grad * clip_factor
    norm_grad = grad_norms * clip_factor
    new_embedding, new_embedding_rows, new_embedding_cols = factored(
        embedding,
        embed_grad,
        embedding_rows,
        embedding_cols,
        embed_colsum,
        embed_rowsum,
        clip_factor,
        vocab_dev * unit_count,
    )
    attn_mine = lax.dynamic_slice_in_dim(attention, unit_at * slab_rows, slab_rows, 2)
    new_attention, new_attention_rows, new_attention_cols = factored(
        attn_mine,
        attn_grad,
        attention_rows,
        attention_cols,
        attn_colsum,
        attn_rowsum,
        clip_factor,
        breadth,
    )
    new_feed_forward, new_feed_rows, new_feed_cols = factored(
        feed_forward,
        feed_grad,
        feed_rows,
        feed_cols,
        feed_colsum,
        feed_rowsum,
        clip_factor,
        units_dev * unit_count,
    )
    map_mine = lax.dynamic_slice_in_dim(map_weight, unit_at * slab_rows, slab_rows, 0)
    new_map, new_map_rows, new_map_cols = factored(
        map_mine, map_grad, map_rows, map_cols, map_colsum, map_rowsum, clip_factor, breadth
    )
    new_norm_moment = DECAY_RATE * norm_moment + (1 - DECAY_RATE) * (
        norm_grad * norm_grad + ADA_EPS
    )
    new_norm_params = norm_params - LEARN_RATE * norm_grad * lax.rsqrt(new_norm_moment)
    return (
        total_loss,
        count,
        grad_norm,
        new_embedding,
        embed_grad,
        new_embedding_rows,
        new_embedding_cols,
        new_attention,
        attn_grad,
        new_attention_rows,
        new_attention_cols,
        new_feed_forward,
        feed_grad,
        new_feed_rows,
        new_feed_cols,
        new_map,
        map_grad,
        new_map_rows,
        new_map_cols,
        new_norm_params,
        norm_grad,
        new_norm_moment,
    )


def solution(mesh):
    placed = (
        P(("dp", "unit"), None),
        P(("dp", "unit"), None),
        P(),
        P(("dp", "unit"), None),
        P(),
        P(("dp", "unit"), None, None),
        P(),
        P(),
        P(),
        P(),
        P(),
        P("unit", None),
        P(),
        P(None, None, "unit", None),
        P(),
        P(),
        P("unit"),
        P(),
        P(None, None, "unit"),
        P(),
        P(None, None, "unit"),
        P(),
        P("unit"),
        P(),
        P(),
    )
    return jax.shard_map(
        local,
        mesh=mesh,
        in_specs=placed,
        out_specs=(
            P(),
            P(),
            P(),
            P("unit", None),
            P("unit", None),
            P("unit"),
            P(),
            P(None, None, "unit", None),
            P(None, None, "unit", None),
            P(None, None, "unit"),
            P(),
            P(None, None, "unit", None),
            P(None, None, "unit", None),
            P(None, None, "unit"),
            P(),
            P("unit", None),
            P("unit", None),
            P("unit"),
            P(),
            P(),
            P(),
            P(),
        ),
        check_vma=False,
    )
```

profile of v0, /device:TPU:0, one launch (start us, length us, event | category | flops | bytes accessed | tf_op | source)
XLA Modules:
  0.0 2735.5 jit_solution(16106571580219344286)
XLA Ops:
  26.4 16.0 copy.118
  46.2 215.4 %all-gather.9.cloned.1.call-done = bf16[30720,768]{1,0:T(8,128)(2,1)} async-done(((bf16[3840,768]{1,0:T(8,128)(2,1)}), bf16[30720,768]{1,0:T(8,128)(2,1)}) %all-gather.9.cloned.1.call-update) | async-done | bytes 47185936 | tf_op jit(solution)/shard_map/all_gather | solution.py:286
  261.5 14.0 gather_fusion
  288.0 77.3 %while.83 = (s32[]{:T(128)}, f32[2,1,512,12,64]{2,4,3,1,0:T(8,128)}, f32[2,1,12,512]{3,2,1,0:T(8,128)S(1)}, s32[2]{0:T(128)S(1)}, s32[1,1024]{1,0:T(1,128)S(1)},...) while((s32[]{:T(128)}, ...), condition=%wide.region_5.6_spmd, body=%wide.region_2.5_spmd.sunk | while | flops 1688202752 | bytes 190296336 | solution.py:86
  301.0 14.4 fusion.218
  376.0 37.8 %multiply_convert_fusion.3 = (bf16[1024,3072]{1,0:T(8,128)(2,1)}, f32[1024,3072]{1,0:T(8,128)}, f32[1024,3072]{1,0:T(8,128)}) fusion(f32[3072]{0:T(1024)S(1)} %bitcast.555, bf16[2,2,3072,768]{3,2,1,0:T(8,128)(2,1)} %all-gather.11.cloned.1.call-done, f32[1024,768]{0,1:T(8,128)S(1)} %get-tuple-element.856, f32[768]{0:T(1024)S(1)} %copy-done.134, ...), kind=kOutput, calls=%fused_computation.156 | convolution fusion | flops 5043388416 | bytes 39348224 | tf_op jit(solution)/shard_map/gd,fd->gf/dot_general | solution.py:189
  433.8 73.3 %while.84 = (s32[]{:T(128)}, f32[2,1,512,12,64]{2,4,3,1,0:T(8,128)}, f32[2,1,12,512]{3,2,1,0:T(8,128)S(1)}, s32[2]{0:T(128)S(1)}, s32[1,1024]{1,0:T(1,128)S(1)},...) while((s32[]{:T(128)}, ...), condition=%wide.region_13.14_spmd, body=%wide.region_10.13_spmd.sunk | while | flops 1688202752 | bytes 190296336 | solution.py:86
  517.5 37.3 %multiply_convert_fusion.2 = (bf16[1024,3072]{1,0:T(8,128)(2,1)S(1)}, f32[1024,3072]{1,0:T(8,128)}, f32[1024,3072]{1,0:T(8,128)}) fusion(f32[3072]{0:T(1024)S(1)} %bitcast.557, bf16[2,2,3072,768]{3,2,1,0:T(8,128)(2,1)} %all-gather.11.cloned.1.call-done, f32[1024,768]{0,1:T(8,128)S(1)} %get-tuple-element.861, f32[768]{0:T(1024)S(1)} %copy-done.139, ...), kind=kOutput, calls=%fused_computation.143 | convolution fusion | flops 5043388416 | bytes 39348224 | tf_op jit(solution)/shard_map/gd,fd->gf/dot_general | solution.py:189
  692.2 20.4 add_convert_fusion.1
  738.2 171.0 %while.87 = (s32[]{:T(128)}, f32[1,1024,12,64]{1,3,2,0:T(8,128)}, f32[1,1024,12,64]{1,3,2,0:T(8,128)}, bf16[2,1,512,12,64]{2,4,3,1,0:T(8,128)(2,1)}, s32[2]{0:T(...) while((s32[]{:T(128)}, f32[1,1024,12,64]{1,3,2,0:T(8,128)}, ...), condition=%wide.region_36.37_spmd.clone, body=%wide.region_34.36_spmd.clone.sunk | while | flops 4127321600 | bytes 225644848 | solution.py:131
  752.0 13.4 bitcast_add_fusion.11
  765.4 18.2 multiply_reduce_fusion.35
  783.6 21.3 multiply_convert_fusion.27
  836.3 14.3 bitcast_add_fusion.11
  850.6 18.2 multiply_reduce_fusion.35
  868.7 21.3 multiply_convert_fusion.27
  955.1 20.5 add_convert_fusion
  1001.2 170.8 %while.88 = (s32[]{:T(128)}, f32[1,1024,12,64]{1,3,2,0:T(8,128)}, f32[1,1024,12,64]{1,3,2,0:T(8,128)}, bf16[2,1,512,12,64]{2,4,3,1,0:T(8,128)(2,1)}, s32[2]{0:T(...) while((s32[]{:T(128)}, f32[1,1024,12,64]{1,3,2,0:T(8,128)}, ...), condition=%wide.region_43.44_spmd.clone, body=%wide.region_41.43_spmd.clone.sunk | while | flops 4127321600 | bytes 225644848 | solution.py:131
  1014.8 13.3 bitcast_add_fusion.13
  1028.1 18.2 multiply_reduce_fusion.36
  1046.2 21.2 multiply_convert_fusion.28
  1098.9 14.2 bitcast_add_fusion.13
  1113.2 18.2 multiply_reduce_fusion.36
  1131.3 21.2 multiply_convert_fusion.28
  1262.4 16.9 pad_maximum_fusion
  1279.3 240.2 %while.86 = (s32[]{:T(128)}, bf16[8,6240,768]{2,1,0:T(8,128)(2,1)}, s32[8]{0:T(128)S(1)}, s32[1024]{0:T(1024)S(1)}, f32[1024,768]{1,0:T(8,128)}, /*index=5*/bf16...) while((s32[]{:T(128)}, bf16[8,6240,768]{2,1,0:T(8,128)(2,1)}, ...), condition=%wide.region_48.49_spmd, body=%wide.region_46.48_spmd.sunk | while | flops 39130120 | bytes 44253988 | solution.py:410
  1286.7 13.2 scatter_custom_fusion.6
  1316.6 13.2 scatter_custom_fusion.6
  1519.8 431.0 %reduce-scatter.5.cloned.1.call-done = bf16[6240,768]{1,0:T(8,128)(2,1)} async-done(((bf16[49920,768]{1,0:T(8,128)(2,1)}), bf16[6240,768]{1,0:T(8,128)(2,1)}) %reduce-scatter.5.cloned.1.call-update) | async-done | bytes 9584656 | tf_op jit(solution)/shard_map/reduce_scatter | solution.py:409
  1962.6 13.5 slice_add_fusion
  1988.2 635.1 %all-reduce.5.cloned.1.call-done = (f32[3840,768]{1,0:T(8,128)}, f32[2,4,96,768]{3,2,1,0:T(8,128)}, f32[96,768]{1,0:T(8,128)}, f32[2,2,384,768]{3,2,1,0:T(8,128)}) async-done(((f32[3840,768]{1,0:T(8,128)}, f32[2,4,96,768]{3,2,1,0:T(8,128)}, f32[96,768]{1,0:T(8,128)}, f32[2,2,384,768]{3,2,1,0:T(8,128)}), (f32[3840,768]{1,0:T(8,128)}, f32[2,4,96,768]{3,2,1,0:T(8,128)}, f32[96,768]{1,0:T(8,128)}, ...) | async-done | bytes 19169296 | tf_op jit(solution)/shard_map/psum | solution.py:428
  2637.9 41.2 %all-reduce.6 = (f32[]{:T(128)}, f32[]{:T(128)}, f32[10,768]{1,0:T(8,128)S(1)}, f32[]{:T(128)}, f32[768]{0:T(1024)S(1)}, /*index=5*/f32[2,4,768]{2,1,0:T(4,128)S...) all-reduce(f32[]{:T(128)S(6)} %add.542, ...), channel_id=1, replica_groups=mesh['dp'=4,'unit'=8] {'dp','unit'}, use_global_device_ids=true, to_apply=%region_26.27 | all-reduce | flops 18448 | bytes 147584 | tf_op jit(solution)/shard_map/psum | solution.py:449
  (762 shorter events, 931.0 us)
Async XLA Ops:
  7.2 254.4 %all-gather.9.cloned.1.call-start = ((), (), s32[]{:S(2)}) async-start(), calls=%async_computation.2 | async-start | bytes 53084160 | tf_op jit(solution)/shard_map/all_gather | solution.py:286
  14.8 360.8 %all-gather.11.cloned.1.call-start = ((), (), s32[]{:S(2)}) async-start(), calls=%async_computation.3 | async-start | bytes 21233664 | tf_op jit(solution)/shard_map/all_gather | solution.py:278
  19.0 651.3 %reduce-scatter.3.cloned.1.call-start = ((), (), s32[]{:S(2)}) async-start(), calls=%async_computation.4 | async-start | bytes 1769472 | tf_op jit(solution)/shard_map/reduce_scatter | solution.py:346
  20.6 635.0 %collective-permute-start = (bf16[1,1024,768]{1,2,0:T(8,128)(2,1)}, bf16[1,1024,768]{1,2,0:T(8,128)(2,1)}, u32[]{:S(2)}, u32[]{:S(2)}) collective-permute-start(bf16[1,1024,768]{1,2,0:T(8,128)(2,1)} %copy.123), channel_id=1, source_target_pairs={{0,4},{1,5},{2,6},{3,7},{4,0},{5,1},{6,2},{7,3},{8,12},{9,13},{10,... | collective-permute-start | bytes 4718600 | tf_op jit(solution)/shard_map/ppermute | solution.py:23
  26.3 19.1 copy-start.67
  26.4 19.2 copy-start.88
  26.4 19.2 copy-start.89
  44.4 233.1 %copy-start.99 = (f32[768]{0:T(1024)}, f32[768]{0:T(1024)S(1)}, u32[]{:S(2)}) copy-start(f32[768]{0:T(1024)S(1)} %get-tuple-element.667) | copy-start | bytes 9220
  44.4 233.1 %copy-start.131 = (f32[768]{0:T(1024)}, f32[768]{0:T(1024)S(1)}, u32[]{:S(2)}) copy-start(f32[768]{0:T(1024)S(1)} %get-tuple-element.666) | copy-start | bytes 9220
  45.5 232.0 %copy-start.93 = (pred[1024]{0:T(1024)(128)(4,1)}, pred[1024]{0:T(1024)(128)(4,1)S(1)}, u32[]{:S(2)}) copy-start(pred[1024]{0:T(1024)(128)(4,1)S(1)} %get-tuple-element.847) | copy-start | bytes 3076
  45.5 232.0 %copy-start.96 = (pred[1024]{0:T(1024)(128)(4,1)}, pred[1024]{0:T(1024)(128)(4,1)S(1)}, u32[]{:S(2)}) copy-start(pred[1024]{0:T(1024)(128)(4,1)S(1)} %get-tuple-element.848) | copy-start | bytes 3076
  288.0 77.4 %copy-start.126 = (f32[12]{0:T(128)S(1)}, f32[12]{0:T(128)}, u32[]{:S(2)}) copy-start(f32[12]{0:T(128)} %get-tuple-element.854) | copy-start | bytes 148
  290.4 25.1 copy-start.12
  330.1 23.5 copy-start.12
  375.1 38.7 %copy-start.25 = (f32[1024,768]{0,1:T(8,128)}, f32[1024,768]{0,1:T(8,128)S(1)}, u32[]{:S(2)}) copy-start(f32[1024,768]{0,1:T(8,128)S(1)} %get-tuple-element.856) | copy-start | bytes 9437188
  375.2 38.6 %copy-start.81 = (f32[1024]{0:T(1024)}, f32[1024]{0:T(1024)S(1)}, u32[]{:S(2)}) copy-start(f32[1024]{0:T(1024)S(1)} %broadcast_multiply_fusion.22) | copy-start | bytes 12292
  375.6 38.2 %copy-start.116 = (f32[1024]{0:T(1024)}, f32[1024]{0:T(1024)S(1)}, u32[]{:S(2)}) copy-start(f32[1024]{0:T(1024)S(1)} %add_rsqrt_fusion.3) | copy-start | bytes 12292
  433.8 73.3 %copy-start.128 = (f32[12]{0:T(128)S(1)}, f32[12]{0:T(128)}, u32[]{:S(2)}) copy-start(f32[12]{0:T(128)} %get-tuple-element.853) | copy-start | bytes 148
  436.2 22.9 copy-start.13
  472.6 22.9 copy-start.13
  516.6 38.1 %copy-start.30 = (f32[1024,768]{0,1:T(8,128)}, f32[1024,768]{0,1:T(8,128)S(1)}, u32[]{:S(2)}) copy-start(f32[1024,768]{0,1:T(8,128)S(1)} %get-tuple-element.861) | copy-start | bytes 9437188
  631.5 1319.4 %reduce-scatter.5.cloned.1.call-start = ((), (), s32[]{:S(2)}) async-start(), calls=%async_computation.5 | async-start | bytes 86261760 | tf_op jit(solution)/shard_map/reduce_scatter | solution.py:409
  632.2 100.4 %copy-start.142 = (f32[768]{0:T(1024)}, f32[768]{0:T(1024)S(1)}, u32[]{:S(2)}) copy-start(f32[768]{0:T(1024)S(1)} %broadcast_in_dim.155) | copy-start | bytes 9220
  692.2 20.4 copy-start.31
  955.0 20.5 copy-start.26
  955.0 20.5 copy-start.82
  955.0 20.5 copy-start.103
  955.0 20.5 copy-start.117
  955.1 20.5 copy-start.135
  1519.5 443.1 %copy-start.52 = (bf16[512,768]{1,0:T(8,128)(2,1)S(1)}, bf16[512,768]{1,0:T(8,128)(2,1)}, u32[]{:S(2)}) copy-start(bf16[512,768]{1,0:T(8,128)(2,1)} %copy-done.51) | copy-start | bytes 2359300
  1519.6 1103.7 %all-reduce.5.cloned.1.call-start = ((), (), s32[]{:S(2)}) async-start(), calls=%async_computation.6 | async-start | bytes 38338560 | tf_op jit(solution)/shard_map/psum | solution.py:428
  2681.2 21.8 copy-start.63
  (163 other events, 1079.8 us)
Sparse Core Ops, SparseCore 0:
  14.9 246.5 all-gather.8
  264.0 98.7 all-gather.10
  631.6 38.6 reduce-scatter.2
  1519.7 431.1 reduce-scatter.4
  1981.2 642.0 all-reduce.4
where the time goes:
time: 2750 us; the launch traced here: 2740 us
  waiting for transfers between devices  1290 us (47%)
  matrix products  617 us (22%)
  other arithmetic  499 us (18%)
  local copies, waits for them, and re-layouts  200 us (7%)
  blocking collectives  76.4 us (3%)
  between operations  28.5 us (1%)
    psum x1, waiting for transfers between devices, local(): lax.psum((embed_grad, attn_grad, map_grad, feed_grad), 'dp')  635 us
    reduce_scatter x1, waiting for transfers between devices, local(): lax.psum_scatter(lax.map(owner_rows, owners).reshape(lax.axis_size('unit'...  431 us
    all_gather x1, waiting for transfers between devices, local(): portion = lax.all_gather(table_low, 'unit', axis=0, tiled=True)  215 us
    scatter-add x8, other arithmetic, owner_rows(): jax.ops.segment_sum(grad_looked, jnp.where(inside, relative, vocab_dev),...  106 us
    dot_general x8, matrix products, block_scores(): jnp.einsum('sqhd,skhd->shqk', query_block, keys, preferred_element_type=j...  88.2 us
    convert_element_type x4, other arithmetic, one_block(): grad_scores = (probability * (grad_prob - inner)).astype(jnp.bfloat16)  85.1 us
    dynamic_update_slice x8, other arithmetic, local(): lax.map(owner_rows, owners)  75.9 us
    dot_general x2, matrix products, feed_forward_pass(): jnp.einsum('gd,fd->gf', hidden_low, unit_weights[0], preferred_element_ty...  75.2 us
  transfers between devices with their start and end apart: 6, of which 4 were waited for; matrix products, arithmetic and copies ran while one was open for 14% of the time, Pallas kernels for 0%

commit v1 on v0

v1 whole, which is shorter than its diff:
```python
import functools
import math

import jax
import jax.numpy as jnp
from jax import lax
from jax.experimental import pallas as pl
from jax.experimental.pallas import tpu as pltpu
from jax.sharding import PartitionSpec as P

H = 12
HD = 64
PAIR = 2 * HD
KEY_BLOCK = 128
QUERY_BLOCK = 256
ROW_BLOCK = 512
UNIT_BLOCK = 768

LN_EPS = 1e-06
ADA_EPS = 1e-30
DECAY_RATE = 0.95
LEARN_RATE = 0.015
CLIP_LIMIT = 0.05
MASK_FILL = 1e30

B = jnp.bfloat16
F = jnp.float32
NT = (((1,), (1,)), ((), ()))
TN = (((0,), (0,)), ((), ()))
TT = (((0,), (1,)), ((), ()))
VMEM_MOST = 58 * 2**20


def dot(left, right):
    return jnp.dot(left, right, preferred_element_type=F)


def contract(left, right, dims):
    return lax.dot_general(left, right, dims, preferred_element_type=F)


def query_windows(segments, block):
    first = segments[::block]
    last = segments[block - 1 :: block]
    start = jnp.sum((segments[None, :] < first[:, None]).astype(jnp.int32), axis=1)
    stop = jnp.sum((segments[None, :] <= last[:, None]).astype(jnp.int32), axis=1)
    low = start // KEY_BLOCK
    high = (stop + KEY_BLOCK - 1) // KEY_BLOCK
    return jnp.concatenate([low, high - low]).astype(jnp.int32)


def most_blocks(length, block):
    return min(length // KEY_BLOCK, block // KEY_BLOCK + 4)


def window_mask(segk_ref, segq_ref, start, width, first_query, block):
    key_seg = segk_ref[pl.ds(start, width), :]
    if block > KEY_BLOCK:
        key_seg = jnp.concatenate([key_seg] * (block // KEY_BLOCK), axis=1)
    query_seg = segq_ref[0:1, pl.ds(first_query, block)]
    key_at = start + lax.broadcasted_iota(jnp.int32, (width, block), 0)
    query_at = first_query + lax.broadcasted_iota(jnp.int32, (width, block), 1)
    return (key_seg == query_seg) | (key_at == query_at)


def head_rows(block, head):
    empty = jnp.zeros((HD, block.shape[1]), block.dtype)
    parts = [block[:HD], empty] if head == 0 else [empty, block[HD:]]
    return jnp.concatenate(parts, axis=0)


def head_lanes(block):
    lane = lax.broadcasted_iota(jnp.int32, block.shape, 1)
    empty = jnp.zeros_like(block)
    return jnp.concatenate(
        [jnp.where(lane < HD, block, empty), jnp.where(lane < HD, empty, block)], axis=0
    )


def attend_kernel(
    window_ref, gate_ref, k_ref, qt_ref, vt_ref, segk_ref, segq_ref, ot_ref, lse_ref, *, block
):
    pair = pl.program_id(0)
    length = k_ref.shape[1]
    count = length // block
    lse_ref[...] = jnp.zeros_like(lse_ref)
    for i in range(count):
        low = window_ref[i]
        number = window_ref[count + i]
        columns = pl.ds(i * block, block)
        for n in range(1, most_blocks(length, block) + 1):

            @pl.when(number == n)
            def _():
                width = n * KEY_BLOCK
                start = pl.multiple_of(low * KEY_BLOCK, KEY_BLOCK)
                keys = k_ref[0, pl.ds(start, width), :]
                mask = window_mask(segk_ref, segq_ref, start, width, i * block, block)
                queries = qt_ref[0, :, columns]
                for head in range(2):
                    rows = slice(head * HD, (head + 1) * HD)
                    scores = jnp.where(mask, dot(keys, head_rows(queries, head)), -MASK_FILL)
                    top = jnp.max(scores, axis=0, keepdims=True)
                    exponent = jnp.exp(scores - top)
                    total = jnp.sum(exponent, axis=0, keepdims=True)
                    mixed = dot(vt_ref[0, rows, pl.ds(start, width)], exponent.astype(B))
                    gated = mixed * (gate_ref[2 * pair + head] / total)
                    ot_ref[rows, columns] = gated.astype(B)
                    lse_ref[0, head : head + 1, columns] = top + jnp.log(total)


def attend(windows, gates, tokens, features, key_segments, query_segments):
    _, length, breadth = tokens.shape
    pairs = breadth // PAIR
    return pl.pallas_call(
        functools.partial(attend_kernel, block=QUERY_BLOCK),
        grid_spec=pltpu.PrefetchScalarGridSpec(
            num_scalar_prefetch=2,
            grid=(pairs,),
            in_specs=[
                pl.BlockSpec((1, length, PAIR), lambda p, *_: (1, 0, p)),
                pl.BlockSpec((1, PAIR, length), lambda p, *_: (0, p, 0)),
                pl.BlockSpec((1, PAIR, length), lambda p, *_: (2, p, 0)),
                pl.BlockSpec((length, KEY_BLOCK), lambda p, *_: (0, 0)),
                pl.BlockSpec((8, length), lambda p, *_: (0, 0)),
            ],
            out_specs=[
                pl.BlockSpec((PAIR, length), lambda p, *_: (p, 0)),
                pl.BlockSpec((1, 8, length), lambda p, *_: (p, 0, 0)),
            ],
        ),
        out_shape=[
            jax.ShapeDtypeStruct((breadth, length), B),
            jax.ShapeDtypeStruct((pairs, 8, length), F),
        ],
        compiler_params=pltpu.CompilerParams(vmem_limit_bytes=VMEM_MOST),
        cost_estimate=pl.CostEstimate(
            flops=2 * 2 * 2 * length * 512 * breadth,
            bytes_accessed=8 * length * breadth,
            transcendentals=length * 512 * 12,
        ),
        name="attend",
    )(windows, gates, tokens, features, features, key_segments, query_segments)


def attend_back_kernel(
    window_ref,
    k_ref,
    kt_ref,
    q_ref,
    qt_ref,
    v_ref,
    do_ref,
    dot_ref,
    segk_ref,
    segq_ref,
    lse_ref,
    grad_ref,
    dq_sum,
    dk_sum,
    dv_sum,
    *,
    block,
    score_scale,
):
    length = k_ref.shape[1]
    count = length // block
    dk_sum[...] = jnp.zeros_like(dk_sum)
    dv_sum[...] = jnp.zeros_like(dv_sum)
    for i in range(count):
        low = window_ref[i]
        number = window_ref[count + i]
        columns = pl.ds(i * block, block)
        for n in range(1, most_blocks(length, block) + 1):

            @pl.when(number == n)
            def _():
                width = n * KEY_BLOCK
                start = pl.multiple_of(low * KEY_BLOCK, KEY_BLOCK)
                window = pl.ds(start, width)
                keys = k_ref[0, window, :]
                values = v_ref[0, window, :]
                mask = window_mask(segk_ref, segq_ref, start, width, i * block, block)
                queries_t = qt_ref[0, :, columns]
                grads_t = dot_ref[:, columns]
                all_prob = []
                all_grad = []
                for head in range(2):
                    rows = slice(head * HD, (head + 1) * HD)
                    scores = jnp.where(mask, dot(keys, head_rows(queries_t, head)), -MASK_FILL)
                    prob = jnp.exp(scores - lse_ref[0, head : head + 1, columns])
                    weighted = prob * dot(values, head_rows(grads_t, head))
                    inner = jnp.sum(weighted, axis=0, keepdims=True)
                    grad = (weighted - prob * inner).astype(B)
                    dq_sum[rows, columns] = dot(kt_ref[0, rows, window], grad) * score_scale
                    all_prob.append(prob.astype(B))
                    all_grad.append(grad)
                dv_sum[window, :] += dot(
                    jnp.concatenate(all_prob, axis=1), head_lanes(do_ref[columns, :])
                )
                dk_sum[window, :] += dot(
                    jnp.concatenate(all_grad, axis=1), head_lanes(q_ref[0, columns, :])
                )

    grad_ref[0] = jnp.transpose(dq_sum[...]).astype(B)
    grad_ref[1] = dk_sum[...].astype(B)
    grad_ref[2] = dv_sum[...].astype(B)


def attend_back(
    windows, tokens, features, grads, grads_t, key_segments, query_segments, log_total
):
    _, length, breadth = tokens.shape
    pairs = breadth // PAIR

    def token_spec(which):
        return pl.BlockSpec((1, length, PAIR), lambda p, *_: (which, 0, p))

    def feature_spec(which):
        return pl.BlockSpec((1, PAIR, length), lambda p, *_: (which, p, 0))

    return pl.pallas_call(
        functools.partial(
            attend_back_kernel, block=QUERY_BLOCK, score_scale=1.0 / math.sqrt(HD)
        ),
        grid_spec=pltpu.PrefetchScalarGridSpec(
            num_scalar_prefetch=1,
            grid=(pairs,),
            in_specs=[
                token_spec(1),
                feature_spec(1),
                token_spec(0),
                feature_spec(0),
                token_spec(2),
                pl.BlockSpec((length, PAIR), lambda p, *_: (0, p)),
                pl.BlockSpec((PAIR, length), lambda p, *_: (p, 0)),
                pl.BlockSpec((length, KEY_BLOCK), lambda p, *_: (0, 0)),
                pl.BlockSpec((8, length), lambda p, *_: (0, 0)),
                pl.BlockSpec((1, 8, length), lambda p, *_: (p, 0, 0)),
            ],
            out_specs=pl.BlockSpec((3, length, PAIR), lambda p, *_: (0, 0, p)),
            scratch_shapes=[
                pltpu.VMEM((PAIR, length), F),
                pltpu.VMEM((length, PAIR), F),
                pltpu.VMEM((length, PAIR), F),
            ],
        ),
        out_shape=jax.ShapeDtypeStruct((3, length, breadth), B),
        compiler_params=pltpu.CompilerParams(vmem_limit_bytes=VMEM_MOST),
        cost_estimate=pl.CostEstimate(
            flops=5 * 2 * 2 * length * 512 * breadth,
            bytes_accessed=20 * length * breadth,
            transcendentals=length * 512 * 12,
        ),
        name="attend_back",
    )(
        windows,
        tokens,
        features,
        tokens,
        features,
        tokens,
        grads,
        grads_t,
        key_segments,
        query_segments,
        log_total,
    )


def project_kernel(x_ref, weight_ref, tokens_ref, features_ref, *, score_scale):
    scale = jnp.where(pl.program_id(0) == 0, score_scale, 1.0).astype(F)
    tokens = dot(x_ref[...], weight_ref[...]).astype(B).astype(F)
    tokens_ref[0] = (tokens * scale).astype(B)
    features = contract(weight_ref[...], x_ref[...], TT).astype(B).astype(F)
    features_ref[0] = (features * scale).astype(B)


def project(x, weights, layer):
    length, breadth = x.shape
    return pl.pallas_call(
        functools.partial(project_kernel, score_scale=1.0 / math.sqrt(HD)),
        grid=(3,),
        in_specs=[
            pl.BlockSpec((length, breadth), lambda j: (0, 0)),
            pl.BlockSpec((None, None, breadth, breadth), lambda j: (layer, j, 0, 0)),
        ],
        out_specs=[
            pl.BlockSpec((1, length, breadth), lambda j: (j, 0, 0)),
            pl.BlockSpec((1, breadth, length), lambda j: (j, 0, 0)),
        ],
        out_shape=[
            jax.ShapeDtypeStruct((3, length, breadth), B),
            jax.ShapeDtypeStruct((3, breadth, length), B),
        ],
        compiler_params=pltpu.CompilerParams(vmem_limit_bytes=VMEM_MOST),
        cost_estimate=pl.CostEstimate(
            flops=12 * length * breadth * breadth,
            bytes_accessed=14 * length * breadth + 6 * breadth * breadth,
            transcendentals=0,
        ),
        name="project",
    )(x, weights)


def gelu_and_slope(value):
    density = jnp.exp(value * value * -0.5)
    ratio = pl.reciprocal(1.0 + jnp.abs(value) * (0.3275911 * math.sqrt(0.5)))
    series = ratio * (
        0.127414796
        + ratio
        * (-0.142248368 + ratio * (0.7107068705 + ratio * (-0.7265760135 + ratio * 0.5307027145)))
    )
    tail = series * density
    below = jnp.where(value >= 0, 1.0 - tail, tail)
    return value * below, below + value * density * (1.0 / math.sqrt(2.0 * math.pi))


def feed_kernel(x_ref, up_ref, down_ref, scale_ref, act_ref, slope_ref, out_ref):
    first = pl.program_id(0) == 0
    scale = scale_ref[0]
    act, slope = gelu_and_slope(contract(x_ref[...], up_ref[...], NT))
    act = (act * scale).astype(B)
    act_ref[...] = act
    slope_ref[...] = (slope * scale).astype(B)
    part = dot(act, down_ref[...])

    @pl.when(first)
    def _():
        out_ref[...] = part

    @pl.when(jnp.logical_not(first))
    def _():
        out_ref[...] += part


def feed(x, weights, scale):
    length, breadth = x.shape
    units = weights.shape[1]
    block = UNIT_BLOCK
    return pl.pallas_call(
        feed_kernel,
        grid=(units // block,),
        in_specs=[
            pl.BlockSpec((length, breadth), lambda j: (0, 0)),
            pl.BlockSpec((None, block, breadth), lambda j: (0, j, 0)),
            pl.BlockSpec((None, block, breadth), lambda j: (1, j, 0)),
            pl.BlockSpec((1, 1, block), lambda j: (0, 0, j)),
        ],
        out_specs=[
            pl.BlockSpec((length, block), lambda j: (0, j)),
            pl.BlockSpec((length, block), lambda j: (0, j)),
            pl.BlockSpec((length, breadth), lambda j: (0, 0)),
        ],
        out_shape=[
            jax.ShapeDtypeStruct((length, units), B),
            jax.ShapeDtypeStruct((length, units), B),
            jax.ShapeDtypeStruct((length, breadth), F),
        ],
        compiler_params=pltpu.CompilerParams(vmem_limit_bytes=VMEM_MOST),
        cost_estimate=pl.CostEstimate(
            flops=4 * length * breadth * units,
            bytes_accessed=4 * (length + breadth) * units + 6 * length * breadth,
            transcendentals=2 * length * units,
        ),
        name="feed",
    )(x, weights, weights, scale.reshape(1, 1, units))


def feed_back_kernel(
    grad_ref, x_ref, act_ref, slope_ref, up_ref, down_ref, out_ref, owned_ref, pre_grad
):
    first = pl.program_id(0) == 0
    grad_act = contract(grad_ref[...], down_ref[...], NT)
    grad_pre = (grad_act * slope_ref[...].astype(F)).astype(B)
    pre_grad[...] = grad_pre
    part = dot(grad_pre, up_ref[...])

    @pl.when(first)
    def _():
        out_ref[...] = part

    @pl.when(jnp.logical_not(first))
    def _():
        out_ref[...] += part

    grads = (
        contract(pre_grad[...], x_ref[...], TN).astype(B),
        contract(act_ref[...], grad_ref[...], TN).astype(B),
    )
    owners, _, share, _ = owned_ref.shape
    for which in range(2):
        for owner in range(owners):
            owned_ref[owner, which] = grads[which][owner * share : (owner + 1) * share]


def feed_back(grad, x, act, slope, weights, owners):
    length, breadth = x.shape
    units = weights.shape[1]
    share = units // owners
    block = UNIT_BLOCK
    lanes = pl.BlockSpec((length, block), lambda j: (0, j))
    whole = pl.BlockSpec((length, breadth), lambda j: (0, 0))
    return pl.pallas_call(
        feed_back_kernel,
        grid=(units // block,),
        in_specs=[
            whole,
            whole,
            lanes,
            lanes,
            pl.BlockSpec((None, block, breadth), lambda j: (0, j, 0)),
            pl.BlockSpec((None, block, breadth), lambda j: (1, j, 0)),
        ],
        out_specs=[
            whole,
            pl.BlockSpec((block // share, 2, share, breadth), lambda j: (j, 0, 0, 0)),
        ],
        scratch_shapes=[pltpu.VMEM((length, block), B)],
        out_shape=[
            jax.ShapeDtypeStruct((length, breadth), F),
            jax.ShapeDtypeStruct((owners, 2, share, breadth), B),
        ],
        compiler_params=pltpu.CompilerParams(vmem_limit_bytes=VMEM_MOST),
        cost_estimate=pl.CostEstimate(
            flops=8 * length * breadth * units,
            bytes_accessed=4 * (length + 2 * breadth) * units + 8 * length * breadth,
            transcendentals=0,
        ),
        name="feed_back",
    )(grad, x, act, slope, weights, weights)


def scan_kernel(ids, place, found, ends, *, vocab):
    base = place[0]
    blocks = ends.shape[0]
    streams = math.gcd(blocks, 8)
    for first in range(0, blocks, streams):

        def scan(t, counts):
            after = []
            for k, count in enumerate(counts):
                at = (first + k) * ROW_BLOCK + t
                relative = (ids[at] - base).astype(jnp.uint32)
                found[count] = at
                after.append(count + jnp.where(relative < jnp.uint32(vocab), 1, 0))
            return tuple(after)

        begin = tuple(jnp.int32((first + k) * ROW_BLOCK) for k in range(streams))
        counts = lax.fori_loop(0, ROW_BLOCK, scan, begin, unroll=4)
        for k, count in enumerate(counts):
            ends[first + k] = count


def scan_ids(ids, place, vocab):
    smem = pl.BlockSpec(memory_space=pltpu.SMEM)
    return pl.pallas_call(
        functools.partial(scan_kernel, vocab=vocab),
        in_specs=[smem, smem],
        out_specs=[smem, smem],
        out_shape=[
            jax.ShapeDtypeStruct(ids.shape, jnp.int32),
            jax.ShapeDtypeStruct((ids.shape[0] // ROW_BLOCK,), jnp.int32),
        ],
        name="scan_ids",
    )(ids, place)


def lookup_kernel(ids, place, found, ends, own, other, *rest, blocks, vocab):
    outs = rest[:blocks]
    table, rows, stage, table_sem, out_sem = rest[blocks:]
    base = place[0]
    core = place[1]
    mine = pl.multiple_of(core * vocab, 8)
    theirs = pl.multiple_of((1 - core) * vocab, 8)
    loads = [
        pltpu.make_async_copy(own, table.at[pl.ds(mine, vocab)], table_sem.at[0]),
        pltpu.make_async_copy(other, table.at[pl.ds(theirs, vocab)], table_sem.at[1]),
    ]
    for load in loads:
        load.start()
    for load in loads:
        load.wait()
    copies = [None, None]
    for k in range(blocks):
        rows[...] = jnp.zeros_like(rows)

        def put(entry, carry):
            t = found[entry]
            rows[pl.ds(t - k * ROW_BLOCK, 1), :] = table[pl.ds(ids[t] - base, 1), :]
            return carry

        each_entry(k * ROW_BLOCK, ends[k], put)
        slot = k % 2
        if copies[slot] is not None:
            copies[slot].wait()
        stage[slot] = rows[...].astype(B)
        copies[slot] = pltpu.make_async_copy(stage.at[slot], outs[k], out_sem.at[slot])
        copies[slot].start()
    for copy in copies:
        copy.wait()


def each_entry(low, high, body):
    quads = lax.div(high - low, 4)

    def four(e, carry):
        for j in range(4):
            body(low + e * 4 + j, 0)
        return carry

    lax.fori_loop(0, quads, four, 0)
    lax.fori_loop(low + quads * 4, high, body, 0)


def lookup(ids, place, found, ends, own, other):
    vocab, breadth = own.shape
    blocks = ids.shape[0] // ROW_BLOCK
    hbm = pl.BlockSpec(memory_space=pl.ANY)
    smem = pl.BlockSpec(memory_space=pltpu.SMEM)
    return pl.pallas_call(
        functools.partial(lookup_kernel, blocks=blocks, vocab=vocab),
        in_specs=[smem] * 4 + [hbm] * 2,
        out_specs=[hbm] * blocks,
        out_shape=[jax.ShapeDtypeStruct((ROW_BLOCK, breadth), B)] * blocks,
        scratch_shapes=[
            pltpu.VMEM((2 * vocab, breadth), F),
            pltpu.VMEM((ROW_BLOCK, breadth), F),
            pltpu.VMEM((2, ROW_BLOCK, breadth), B),
            pltpu.SemaphoreType.DMA((2,)),
            pltpu.SemaphoreType.DMA((2,)),
        ],
        compiler_params=pltpu.CompilerParams(vmem_limit_bytes=VMEM_MOST),
        cost_estimate=pl.CostEstimate(
            flops=0,
            bytes_accessed=8 * vocab * breadth + 2 * ids.shape[0] * breadth,
            transcendentals=0,
        ),
        name="lookup",
    )(ids, place, found, ends, own, other)


def spread_kernel(
    ids, other_ids, place, found, ends, other_found, other_ends, begin, *rest, pieces
):
    blocks = len(pieces)
    arrays = max(which for which, _ in pieces) + 1
    grads = [rest[which].at[pl.ds(at, ROW_BLOCK)] for which, at in pieces]
    out, total, rows, stage, half, sem, in_sem, out_sem = rest[arrays:]
    base = place[0]
    vocab = total.shape[0]
    fill = pltpu.make_async_copy(begin, total, sem.at[0])
    fill.start()

    def load(k):
        copy = pltpu.make_async_copy(grads[k], stage.at[k % 2], in_sem.at[k % 2])
        copy.start()
        return copy

    coming = load(0)
    fill.wait()
    for k in range(blocks):
        coming.wait()
        if k + 1 < blocks:
            coming = load(k + 1)
        rows[...] = stage[k % 2].astype(F)

        lists = (ids, found, ends) if k < blocks // 2 else (other_ids, other_found, other_ends)
        first = k % (blocks // 2) * ROW_BLOCK

        def add(entry, carry):
            t = lists[1][entry]
            at = pl.ds(lists[0][t] - base, 1)
            total[at, :] += rows[pl.ds(t - first, 1), :]
            return carry

        each_entry(first, lists[2][k % (blocks // 2)], add)
    step = half.shape[1]
    copies = [None, None]
    for j in range(vocab // step):
        slot = j % 2
        if copies[slot] is not None:
            copies[slot].wait()
        half[slot] = total[j * step : (j + 1) * step, :].astype(B)
        copies[slot] = pltpu.make_async_copy(
            half.at[slot], out.at[pl.ds(j * step, step)], out_sem.at[slot]
        )
        copies[slot].start()
    for copy in copies:
        copy.wait()


def spread(ids, other_ids, place, lists, begin, grads):
    vocab, breadth = begin.shape
    arrays = []
    pieces = []
    for array, at in grads:
        known = [k for k, other in enumerate(arrays) if other is array]
        if not known:
            known = [len(arrays)]
            arrays.append(array)
        pieces.append((known[0], at))
    hbm = pl.BlockSpec(memory_space=pl.ANY)
    smem = pl.BlockSpec(memory_space=pltpu.SMEM)
    return pl.pallas_call(
        functools.partial(spread_kernel, pieces=tuple(pieces)),
        in_specs=[smem] * 7 + [hbm] * (1 + len(arrays)),
        out_specs=hbm,
        out_shape=jax.ShapeDtypeStruct((vocab, breadth), B),
        scratch_shapes=[
            pltpu.VMEM((vocab, breadth), F),
            pltpu.VMEM((ROW_BLOCK, breadth), F),
            pltpu.VMEM((2, ROW_BLOCK, breadth), B),
            pltpu.VMEM((2, vocab // 4, breadth), B),
            pltpu.SemaphoreType.DMA((1,)),
            pltpu.SemaphoreType.DMA((2,)),
            pltpu.SemaphoreType.DMA((2,)),
        ],
        compiler_params=pltpu.CompilerParams(vmem_limit_bytes=VMEM_MOST),
        cost_estimate=pl.CostEstimate(
            flops=0,
            bytes_accessed=6 * vocab * breadth + 2 * len(grads) * ROW_BLOCK * breadth,
            transcendentals=0,
        ),
        name="spread",
    )(ids, other_ids, place, *lists, begin, *arrays)


def stats_kernel(small_ref, row_sums_ref, embed_ref, *rest, layers):
    attn = rest[:layers]
    feeds = rest[layers : 2 * layers]
    out_ref = rest[2 * layers]
    norms = small_ref.shape[0]
    cols = jnp.sum(jnp.square(embed_ref[...].astype(F)), axis=0, keepdims=True)

    @pl.when(pl.program_id(0) == 0)
    def _():
        def put(row, value):
            out_ref[row : row + 1, :] = jnp.sum(
                jnp.square(value.astype(F)), axis=0, keepdims=True
            )

        out_ref[:norms, :] = small_ref[...]
        row = norms
        for parts, count in ((attn, 4), (feeds, 2)):
            for part in parts:
                for k in range(count):
                    put(row, part[k])
                    row += 1
        put(row, attn[layers - 1][4])
        out_ref[row + 1 : row + 2, :] = cols
        row += 2
        out_ref[row : row + 1, :] = row_sums_ref[...]

    @pl.when(pl.program_id(0) > 0)
    def _():
        at = norms + 6 * layers + 1
        out_ref[at : at + 1, :] += cols


def stats(small, row_sums, embed, attn, feeds):
    height, breadth = embed.shape
    block = math.gcd(height, 480)
    rows = small.shape[0] + 3 + 6 * len(attn)
    vmem = pl.BlockSpec(memory_space=pltpu.VMEM)
    return pl.pallas_call(
        functools.partial(stats_kernel, layers=len(attn)),
        grid=(height // block,),
        in_specs=[vmem, vmem, pl.BlockSpec((block, breadth), lambda j: (j, 0))]
        + [vmem] * (2 * len(attn)),
        out_specs=pl.BlockSpec((rows, breadth), lambda j: (0, 0)),
        out_shape=jax.ShapeDtypeStruct((rows, breadth), F),
        compiler_params=pltpu.CompilerParams(vmem_limit_bytes=VMEM_MOST),
        name="stats",
    )(small, row_sums, embed, *attn, *feeds)


def factors_kernel(
    parts_ref,
    cols_ref,
    heights_ref,
    params_ref,
    moment_ref,
    scalars_ref,
    new_cols_ref,
    factor_ref,
    norm_grad_ref,
    new_params_ref,
    new_moment_ref,
):
    packed = parts_ref[0]
    for k in range(1, parts_ref.shape[0]):
        packed = packed + parts_ref[k]
    norms = params_ref.shape[0]
    mats, breadth = cols_ref.shape
    norm_grads = packed[:norms]
    col_sums = packed[norms + 1 : norms + 1 + mats]
    lane = lax.broadcasted_iota(jnp.int32, (mats, breadth), 1)
    row = lax.broadcasted_iota(jnp.int32, (mats, breadth), 0)
    row_sums = jnp.sum(
        jnp.where(lane == row, packed[norms + 1 + mats :], 0.0), axis=1, keepdims=True
    )
    heights = heights_ref[...]
    mat_sums = jnp.sum(col_sums, axis=1, keepdims=True)
    square = jnp.sum(mat_sums, axis=0, keepdims=True) + jnp.sum(
        jnp.sum(norm_grads * norm_grads, axis=1, keepdims=True), axis=0, keepdims=True
    )
    norm = jnp.sqrt(square)
    clip = jnp.minimum(1.0, CLIP_LIMIT / norm)
    scalars_ref[0] = packed[norms, 0]
    scalars_ref[1] = norm[0, 0]
    scalars_ref[2] = clip[0, 0]
    new_cols = DECAY_RATE * cols_ref[...] + (1 - DECAY_RATE) * (
        clip * clip * col_sums / heights + ADA_EPS
    )
    mean_rows = DECAY_RATE * row_sums / heights + (1 - DECAY_RATE) * (
        clip * clip * mat_sums / (heights * breadth) + ADA_EPS
    )
    new_cols_ref[...] = new_cols
    factor_ref[...] = LEARN_RATE * jnp.sqrt(mean_rows) * lax.rsqrt(new_cols)
    norm_grad = norm_grads * clip
    moment = DECAY_RATE * moment_ref[...] + (1 - DECAY_RATE) * (norm_grad * norm_grad + ADA_EPS)
    norm_grad_ref[...] = norm_grad
    new_moment_ref[...] = moment
    new_params_ref[...] = params_ref[...] - LEARN_RATE * norm_grad * lax.rsqrt(moment)


def factors(parts, cols, heights, params, moment):
    vmem = pl.BlockSpec(memory_space=pltpu.VMEM)
    like = [jax.ShapeDtypeStruct(x.shape, F) for x in (cols, cols, params, params, params)]
    return pl.pallas_call(
        factors_kernel,
        in_specs=[vmem] * 5,
        out_specs=[pl.BlockSpec(memory_space=pltpu.SMEM)] + [vmem] * 5,
        out_shape=[jax.ShapeDtypeStruct((3,), F)] + like,
        compiler_params=pltpu.CompilerParams(vmem_limit_bytes=VMEM_MOST),
        name="factors",
    )(parts, cols, heights, params, moment)


def renew_kernel(
    scalars_ref, at_ref, factor_ref, rows_ref, weight_ref, sum_ref, new_ref, grad_ref, new_rows_ref
):
    for m in range(sum_ref.shape[0]):
        grad = sum_ref[m].astype(F) * scalars_ref[2]
        mean = jnp.mean(grad * grad, axis=1, keepdims=True) + ADA_EPS
        new_rows = DECAY_RATE * rows_ref[m] + (1 - DECAY_RATE) * mean
        wide = jnp.broadcast_to(new_rows, (new_rows.shape[0], 128))
        new_rows_ref[m, 0] = jnp.transpose(wide)[:1]
        grad_ref[m] = grad
        new_ref[m] = weight_ref[m] - grad * lax.rsqrt(new_rows) * factor_ref[m]


def renew(scalars, at, factor, first, rows, weight, total, group, most):
    mats, height, breadth = total.shape
    block = math.gcd(height, most)
    per = height // block
    wide = pl.BlockSpec((group, block, breadth), lambda m, j, *_: (m, j, 0))
    new, grad, new_rows = pl.pallas_call(
        renew_kernel,
        grid_spec=pltpu.PrefetchScalarGridSpec(
            num_scalar_prefetch=2,
            grid=(mats // group, per),
            in_specs=[
                pl.BlockSpec((group, 1, breadth), lambda m, j, *_: (first // group + m, 0, 0)),
                pl.BlockSpec((group, block, 1), lambda m, j, *_: (m, j, 0)),
                pl.BlockSpec(
                    (group, block, breadth), lambda m, j, scalars, at: (m, at[0] * per + j, 0)
                ),
                wide,
            ],
            out_specs=[
                wide,
                wide,
                pl.BlockSpec((group, 1, 1, block), lambda m, j, *_: (m, j, 0, 0)),
            ],
        ),
        out_shape=[
            jax.ShapeDtypeStruct((mats, height, breadth), F),
            jax.ShapeDtypeStruct((mats, height, breadth), F),
            jax.ShapeDtypeStruct((mats, per, 1, block), F),
        ],
        compiler_params=pltpu.CompilerParams(vmem_limit_bytes=VMEM_MOST),
        name="renew",
    )(scalars, at, factor, rows[..., None], weight, total)
    return new, grad, new_rows.reshape(rows.shape)


def across(value, step):
    pairs = [(u, ((u // 2) ^ step) * 2 + u % 2) for u in range(lax.axis_size("unit"))]
    return lax.ppermute(value, "unit", pairs)


def swapped(value):
    return lax.ppermute(value, "unit", [(u, u ^ 1) for u in range(lax.axis_size("unit"))])


def gathered(value, beside_core, beside_chip):
    other, *beside_core = together(swapped(value), *beside_core)
    both = jnp.stack([value, other])
    chips = lax.axis_size("unit") // 2
    parts = [across(both, step) for step in range(1, chips)]
    if beside_chip:
        parts[0], *beside_chip = together(parts[0], *beside_chip(*beside_core))
    return jnp.stack([both] + parts), beside_core, beside_chip


def dp_scatter(value):
    size = lax.axis_size("dp")
    at = lax.axis_index("dp")
    share = value.shape[0] // size
    parts = [lax.dynamic_slice_in_dim(value, at * share, share, 0)]
    for step in range(1, size):
        away = lax.dynamic_slice_in_dim(value, (at + step) % size * share, share, 0)
        parts.append(lax.ppermute(away, "dp", [(d, (d + step) % size) for d in range(size)]))
    return parts


def dp_gather(parts):
    size = lax.axis_size("dp")
    at = lax.axis_index("dp")
    total = parts[0].astype(F)
    for part in parts[1:]:
        total = total + part.astype(F)
    total = total.astype(B)
    share = total.shape[0]
    found = [total] + [
        lax.ppermute(total, "dp", [(d, (d + step) % size) for d in range(size)])
        for step in range(1, size)
    ]
    return found, share, at, size


def dp_placed(found, share, at, size):
    result = jnp.zeros((size * share,) + found[0].shape[1:], found[0].dtype)
    for step, part in enumerate(found):
        result = lax.dynamic_update_slice_in_dim(result, part, (at - step) % size * share, 0)
    return result


def dp_sum(value):
    size = lax.axis_size("dp")
    if size & (size - 1):
        return lax.psum(value, "dp")
    step = 1
    while step < size:
        value = value + lax.ppermute(value, "dp", [(d, d ^ step) for d in range(size)])
        step = 2 * step
    return value


def together(*values):
    return lax.optimization_barrier(values)


def chip_sum(mine, swapped_theirs):
    return (mine.astype(F) + swapped_theirs.astype(F)).astype(B)


def sent_to_owners(total, chip, steps):
    return [
        across(lax.dynamic_index_in_dim(total, chip ^ step, 0, keepdims=False), step)
        for step in steps
    ]


def owner_total(total, received, chip):
    result = lax.dynamic_index_in_dim(total, chip, 0, keepdims=False).astype(F)
    for part in received:
        result = result + part.astype(F)
    return result.astype(B)


def rows_of_tokens(served, chips, beside, beside_last):
    halves = len(served[0])
    total = [part.astype(F) for part in served[0]]
    if chips != 4 or halves != 2:
        for step in range(1, chips):
            for k in range(halves):
                total[k] = total[k] + across(served[step][k], step).astype(F)
        return jnp.concatenate(total, axis=0), *beside, *beside_last()
    passing = [across(served[3][0], 2), across(served[3][1], 1)]
    direct = [across(served[2][0], 2), across(served[1][1], 1)]
    passing[0], passing[1], direct[0], direct[1], *beside = together(*passing, *direct, *beside)
    last = [
        across(served[1][0] + passing[0], 1),
        across(served[2][1] + passing[1], 2),
    ]
    last[0], last[1], *after = together(*last, *beside_last())
    total = [a + b.astype(F) + c.astype(F) for a, b, c in zip(total, direct, last)]
    return jnp.concatenate(total, axis=0), *beside, *after


def norm_forward(value, gain, shift):
    centered = value - jnp.mean(value, axis=-1, keepdims=True)
    inverse = lax.rsqrt(jnp.mean(centered * centered, axis=-1, keepdims=True) + LN_EPS)
    normed = centered * inverse
    return (normed * gain + shift, (normed, inverse))


def norm_backward(stored, gain, upstream):
    normed, inverse = stored
    scaled = upstream * gain
    inner = (
        scaled
        - jnp.mean(scaled, axis=-1, keepdims=True)
        - normed * jnp.mean(scaled * normed, axis=-1, keepdims=True)
    )
    return (inverse * inner, jnp.sum(upstream * normed, axis=0), jnp.sum(upstream, axis=0))


def local(
    token_ids,
    segment_ids,
    real_mask,
    positions,
    targets,
    teacher_states,
    head_gate,
    layer_gate,
    hidden_gate,
    unit_gate,
    unit_keep,
    embedding,
    attention,
    feed_forward,
    map_weight,
    norm_params,
    embedding_rows,
    embedding_cols,
    attention_rows,
    attention_cols,
    feed_rows,
    feed_cols,
    map_rows,
    map_cols,
    norm_moment,
):
    unit_count = lax.axis_size("unit")
    chips = unit_count // 2
    unit_at = lax.axis_index("unit")
    data_at = lax.axis_index("dp")
    chip = unit_at // 2
    core = unit_at % 2
    length = token_ids.shape[1]
    pick_count = positions.shape[1]
    breadth = embedding.shape[1]
    vocab_dev = embedding.shape[0]
    units_dev = feed_forward.shape[2]
    layer_count = attention.shape[0]
    slab_rows = breadth // unit_count
    group_first = data_at * unit_count
    place = jnp.stack([chip * 2 * vocab_dev, core]).astype(jnp.int32)

    other_table = swapped(embedding)
    all_ids = jnp.concatenate(
        [token_ids[0]] + [across(token_ids[0], step) for step in range(1, chips)]
    )
    found, ends = scan_ids(all_ids, place, 2 * vocab_dev)
    served = list(lookup(all_ids, place, found, ends, embedding, other_table))
    halves = length // ROW_BLOCK
    own_place = jnp.stack([unit_at * vocab_dev, core]).astype(jnp.int32)
    other_ids = swapped(all_ids)
    table_low = embedding.astype(B)
    attention_low = attention.astype(B)
    map_low = map_weight.astype(B)
    looked, *lows = rows_of_tokens(
        [served[step * halves : (step + 1) * halves] for step in range(chips)],
        chips,
        [table_low, attention_low, map_low, *scan_ids(all_ids, own_place, vocab_dev)],
        lambda: scan_ids(other_ids, own_place, vocab_dev),
    )
    table_low, attention_low, map_low, *lists = lows
    feed_low = []
    for layer_at in range(layer_count):
        own = feed_forward[layer_at].astype(B)
        if layer_at > 0:
            looked, own = together(looked, own)
        feed_low.append(lax.all_gather(own, "unit", axis=1, tiled=True))
    teacher = lax.ppermute(
        teacher_states[0],
        "unit",
        [(u, (u + unit_count // 2) % unit_count) for u in range(unit_count)],
    )
    real_row = lax.dynamic_index_in_dim(real_mask, group_first + unit_at, 0, keepdims=False)
    real_flat = real_row.astype(F)
    count = jnp.sum(real_mask).astype(F)
    scale_all = unit_gate * unit_keep.astype(F)
    segments = segment_ids[0]
    windows = query_windows(segments, QUERY_BLOCK)
    key_segments = jnp.broadcast_to(
        jnp.where(real_row > 0, segments, -1)[:, None], (length, KEY_BLOCK)
    )
    query_segments = jnp.broadcast_to(segments[None, :], (8, length))
    head_scale = jnp.repeat(head_gate, HD, axis=1)

    normed, embed_stored = norm_forward(looked, norm_params[0], norm_params[1])
    hidden = normed * hidden_gate
    stored_layers = []
    for layer_at in range(layer_count):
        hidden_low = hidden.astype(B)
        weights = attention_low[layer_at]
        tokens, features = project(hidden_low, attention_low, layer_at)
        gated_t, log_total = attend(
            windows, head_gate[layer_at], tokens, features, key_segments, query_segments
        )
        branch = jnp.einsum("dr,de->re", gated_t, weights[3], preferred_element_type=F)
        middle, norm_first = norm_forward(
            hidden + branch * layer_gate[layer_at, 0] * hidden_gate,
            norm_params[2 + 4 * layer_at],
            norm_params[3 + 4 * layer_at],
        )
        middle_low = middle.astype(B)
        act, slope, result = feed(middle_low, feed_low[layer_at], scale_all[layer_at])
        if layer_at == 0:
            result, teacher = together(result, teacher)
        hidden, norm_second = norm_forward(
            middle + result * layer_gate[layer_at, 1] * hidden_gate,
            norm_params[4 + 4 * layer_at],
            norm_params[5 + 4 * layer_at],
        )
        stored_layers.append(
            (
                (hidden_low, tokens, features, gated_t, log_total),
                norm_first,
                (middle_low, act, slope),
                norm_second,
            )
        )

    final = hidden.astype(B)
    pick_hot = (positions[0][:, None] == jnp.arange(length)[None, :]).astype(B)
    picked_own = dot(pick_hot, final).astype(B)

    def map_loss(mapped):
        diff = mapped - teacher.astype(F)
        error = jnp.sum(jnp.sum(diff * diff, axis=-1) * real_flat) / breadth
        return error, (diff * (2.0 / (breadth * count)) * real_flat[:, None]).astype(B)

    picked_rows, _, (error_part, grad_mapped) = gathered(
        picked_own, [dot(final, map_low)], map_loss
    )
    picked_rows = picked_rows.reshape(unit_count * pick_count, breadth)
    target_all = jnp.concatenate(
        [
            lax.dynamic_index_in_dim(targets, group_first + (unit_at ^ other), 0, keepdims=False)
            for other in range(unit_count)
        ]
    )
    logits = contract(picked_rows, table_low, NT)
    is_target = (target_all - unit_at * vocab_dev)[:, None] == jnp.arange(vocab_dev)[None, :]
    row_max = jnp.max(logits, axis=1)
    sum_exp = jnp.sum(jnp.exp(logits - row_max[:, None]), axis=1)
    target_logit = jnp.sum(jnp.where(is_target, logits, 0.0), axis=1)
    shares, (grad_map,), (grad_final,) = gathered(
        jnp.stack([row_max, sum_exp, target_logit]).reshape(3, unit_count, pick_count),
        [contract(final, grad_mapped, TN).astype(B)],
        lambda _: (contract(grad_mapped, map_low, NT),),
    )
    shares = shares.reshape(unit_count, 3, unit_count, pick_count)
    shares = jnp.stack(
        [
            jnp.stack([shares[a, :, a ^ b] for a in range(unit_count)])
            for b in range(unit_count)
        ],
        axis=2,
    ).reshape(unit_count, 3, unit_count * pick_count)
    top = jnp.max(shares[:, 0], axis=0)
    log_sum = top + jnp.log(jnp.sum(shares[:, 1] * jnp.exp(shares[:, 0] - top), axis=0))
    own_terms = (log_sum - jnp.sum(shares[:, 2], axis=0))[:pick_count]
    grad_logits = (
        (jnp.exp(logits - log_sum[:, None]) - is_target.astype(F)) / count
    ).astype(B)
    grad_parts = dot(grad_logits, table_low).reshape(chips, 2, pick_count, breadth)
    both = grad_parts[:, 0] + swapped(grad_parts[:, 1])
    grad_picked = both[0]
    for step in range(1, chips):
        grad_picked = grad_picked + across(both[step], step)
    grad_table = contract(grad_logits, picked_rows, TN)

    loss_part = error_part + jnp.sum(own_terms)
    grad_hidden = grad_final + lax.dot_general(
        pick_hot.astype(F),
        grad_picked,
        TN,
        precision=lax.Precision.HIGHEST,
        preferred_element_type=F,
    )

    gain_rows = [None] * norm_params.shape[0]
    feed_parts = [None] * layer_count
    attn_parts = [None] * layer_count
    for layer_at in reversed(range(layer_count)):
        attn_stored, norm_first, feed_stored, norm_second = stored_layers[layer_at]
        hidden_low, tokens, features, gated_t, log_total = attn_stored
        middle_low, act, slope = feed_stored
        weights = attention_low[layer_at]
        grad_second, gain_rows[4 + 4 * layer_at], gain_rows[5 + 4 * layer_at] = norm_backward(
            norm_second, norm_params[4 + 4 * layer_at], grad_hidden
        )
        grad_result = (grad_second * layer_gate[layer_at, 1] * hidden_gate).astype(B)
        if layer_at < layer_count - 1:
            grad_result, attn_owned = together(grad_result, attn_owned)
            attn_parts[layer_at + 1] = lax.psum_scatter(attn_owned, "unit")
        grad_middle, feed_owned = feed_back(
            grad_result, middle_low, act, slope, feed_low[layer_at], unit_count
        )
        feed_parts[layer_at] = lax.psum_scatter(feed_owned, "unit")
        grad_first, gain_rows[2 + 4 * layer_at], gain_rows[3 + 4 * layer_at] = norm_backward(
            norm_first, norm_params[2 + 4 * layer_at], grad_second + grad_middle
        )
        grad_branch = (grad_first * layer_gate[layer_at, 0] * hidden_gate).astype(B)
        scale = head_scale[layer_at]
        grad_mixed = (contract(grad_branch, weights[3], NT) * scale).astype(B)
        grad_mixed_t = (contract(weights[3], grad_branch, NT) * scale[:, None]).astype(B)
        grad_proj = attend_back(
            windows,
            tokens,
            features,
            grad_mixed,
            grad_mixed_t,
            key_segments,
            query_segments,
            log_total,
        )
        grad_input = jnp.einsum("jre,jde->rd", grad_proj, weights[:3], preferred_element_type=F)
        grad_hidden = grad_first + grad_input
        grad_hidden, grad_proj = together(grad_hidden, grad_proj)
        grad_in = jnp.einsum(
            "rd,jre->jde", hidden_low, grad_proj, preferred_element_type=F
        ).astype(B)
        grad_out = dot(gated_t, grad_branch).astype(B)
        stack = [grad_in, grad_out[None]]
        if layer_at == layer_count - 1:
            stack.append(grad_map[None])
        stack = jnp.concatenate(stack, axis=0)
        if layer_at > 0:
            attn_owned = jnp.moveaxis(
                stack.reshape(-1, unit_count, slab_rows, breadth), 1, 0
            )
        else:
            stack = stack.reshape(-1, chips, 2, slab_rows, breadth)
            attn_mine = jnp.moveaxis(
                lax.dynamic_index_in_dim(stack, core, 2, keepdims=False), 1, 0
            )
            attn_theirs = jnp.moveaxis(
                lax.dynamic_index_in_dim(stack, 1 - core, 2, keepdims=False), 1, 0
            )

    grad_looked, gain_rows[0], gain_rows[1] = norm_backward(
        embed_stored, norm_params[0], grad_hidden * hidden_gate
    )
    sent = grad_looked.astype(B)
    small = jnp.concatenate(
        [jnp.stack(gain_rows), jnp.broadcast_to(loss_part, (1, breadth))], axis=0
    )
    pieces = [part.reshape(-1, breadth) for part in feed_parts[1:] + attn_parts[1:]]
    early = jnp.concatenate(pieces, axis=0)
    same = [(sent, 0), (sent, ROW_BLOCK)]
    other = swapped(sent)
    crossed = [(other, 0), (other, ROW_BLOCK)]
    if chips == 4 and length == 2 * ROW_BLOCK:
        near = [across(sent, 1), across(sent, 2)]
        near, early, grad_table, attn_theirs = together(near, early, grad_table, attn_theirs)
        last = [across(near[0][:ROW_BLOCK], 2), across(near[1][ROW_BLOCK:], 1)]
        near_other = [swapped(part) for part in near]
        attn_chip = chip_sum(attn_mine, swapped(attn_theirs))
        early = dp_scatter(early)
        last, near_other, attn_chip, early = together(last, near_other, attn_chip, early)
        early, *early_place = dp_gather(early)
        small = dp_sum(small)
        attn_received = sent_to_owners(attn_chip, chip, range(1, chips))
        last_other = [swapped(part) for part in last]
        for home, parts, ends in ((same, near, last), (crossed, near_other, last_other)):
            home += [(part, at) for part in parts for at in (0, ROW_BLOCK)]
            home += [(part, 0) for part in ends]
    else:
        early, *early_place = dp_gather(dp_scatter(early))
        small = dp_sum(small)
        attn_chip = chip_sum(attn_mine, swapped(attn_theirs))
        attn_received = sent_to_owners(attn_chip, chip, range(1, chips))
        for step in range(1, chips):
            part = across(sent, step)
            for home, part in ((same, part), (crossed, swapped(part))):
                home += [(part, at) for at in range(0, length, ROW_BLOCK)]
    embed_part = spread(all_ids, other_ids, own_place, lists, grad_table, same + crossed)
    embed_part, attn_received, early, small = together(embed_part, attn_received, early, small)
    attn_parts[0] = owner_total(attn_chip, attn_received, chip)
    early = dp_placed(early, *early_place)
    embed_sum, feed_first, attn_first = lax.psum((embed_part, feed_parts[0], attn_parts[0]), "dp")
    feed_sums, attn_sums = [feed_first], [attn_first]
    cursor = 0
    for parts, sums in ((feed_parts, feed_sums), (attn_parts, attn_sums)):
        for part in parts[1:]:
            rows = part.shape[0] * part.shape[1]
            sums.append(early[cursor : cursor + rows].reshape(part.shape))
            cursor += rows

    row_sums = jnp.concatenate(
        [
            jnp.sum(attention_rows, axis=-1).reshape(-1),
            jnp.sum(feed_rows, axis=-1).reshape(-1),
            jnp.sum(map_rows)[None],
            jnp.sum(embedding_rows)[None],
        ]
    )
    row_sums = jnp.pad(row_sums, (0, breadth - row_sums.shape[0]))[None]
    old_cols = jnp.concatenate(
        [
            attention_cols.reshape(-1, breadth),
            feed_cols.reshape(-1, breadth),
            map_cols[None],
            embedding_cols[None],
        ],
        axis=0,
    )
    mats = layer_count * 4
    heights = jnp.array(
        [breadth] * mats
        + [units_dev * unit_count] * (layer_count * 2)
        + [breadth, vocab_dev * unit_count],
        F,
    )[:, None]
    packed = stats(small, row_sums, embed_sum, attn_sums, feed_sums)
    scalars, new_cols, factor, norm_grad, new_norm_params, new_norm_moment = factors(
        lax.all_gather(packed, "unit"), old_cols, heights, norm_params, norm_moment
    )
    total_loss, grad_norm = scalars[0], scalars[1]
    factor = factor[:, None]
    feeds = layer_count * 2
    here = jnp.zeros((1,), jnp.int32)
    slab = jnp.full((1,), unit_at, jnp.int32)
    new_embedding, embed_grad, new_embedding_rows = (
        value[0]
        for value in renew(
            scalars,
            here,
            factor,
            mats + feeds + 1,
            embedding_rows[None],
            embedding[None],
            embed_sum[None],
            1,
            640,
        )
    )
    new_map, map_grad, new_map_rows = (
        value[0]
        for value in renew(
            scalars,
            slab,
            factor,
            mats + feeds,
            map_rows[None],
            map_weight[None],
            attn_sums[layer_count - 1][4:],
            1,
            slab_rows,
        )
    )
    new_attention, attn_grad, new_attention_rows = (
        value.reshape((layer_count, 4) + value.shape[1:])
        for value in renew(
            scalars,
            slab,
            factor,
            0,
            attention_rows.reshape(mats, slab_rows),
            attention.reshape(mats, breadth, breadth),
            jnp.concatenate([part[:4] for part in attn_sums], axis=0),
            4,
            slab_rows,
        )
    )
    new_feed_forward, feed_grad, new_feed_rows = (
        value.reshape((layer_count, 2) + value.shape[1:])
        for value in renew(
            scalars,
            here,
            factor,
            mats,
            feed_rows.reshape(feeds, units_dev),
            feed_forward.reshape(feeds, units_dev, breadth),
            jnp.concatenate(feed_sums, axis=0),
            1,
            units_dev,
        )
    )
    new_attention_cols = new_cols[:mats].reshape(layer_count, 4, breadth)
    new_feed_cols = new_cols[mats : mats + feeds].reshape(layer_count, 2, breadth)
    new_map_cols = new_cols[mats + feeds]
    new_embedding_cols = new_cols[mats + feeds + 1]
    return (
        total_loss,
        count,
        grad_norm,
        new_embedding,
        embed_grad,
        new_embedding_rows,
        new_embedding_cols,
        new_attention,
        attn_grad,
        new_attention_rows,
        new_attention_cols,
        new_feed_forward,
        feed_grad,
        new_feed_rows,
        new_feed_cols,
        new_map,
        map_grad,
        new_map_rows,
        new_map_cols,
        new_norm_params,
        norm_grad,
        new_norm_moment,
    )


def solution(mesh):
    placed = (
        P(("dp", "unit"), None),
        P(("dp", "unit"), None),
        P(),
        P(("dp", "unit"), None),
        P(),
        P(("dp", "unit"), None, None),
        P(),
        P(),
        P(),
        P(),
        P(),
        P("unit", None),
        P(),
        P(None, None, "unit", None),
        P(),
        P(),
        P("unit"),
        P(),
        P(None, None, "unit"),
        P(),
        P(None, None, "unit"),
        P(),
        P("unit"),
        P(),
        P(),
    )
    return jax.shard_map(
        local,
        mesh=mesh,
        in_specs=placed,
        out_specs=(
            P(),
            P(),
            P(),
            P("unit", None),
            P("unit", None),
            P("unit"),
            P(),
            P(None, None, "unit", None),
            P(None, None, "unit", None),
            P(None, None, "unit"),
            P(),
            P(None, None, "unit", None),
            P(None, None, "unit", None),
            P(None, None, "unit"),
            P(),
            P("unit", None),
            P("unit", None),
            P("unit"),
            P(),
            P(),
            P(),
            P(),
        ),
        check_vma=False,
    )
```

time: 2750 us -> 1130 us (0.41)
  waiting for transfers between devices: 1290 us -> 425 us
  matrix products: 617 us -> 90.6 us
  other arithmetic: 499 us -> 115 us
  Pallas kernels: 0 us -> 373 us
  local copies, waits for them, and re-layouts: 200 us -> 44.7 us
  blocking collectives: 76.4 us -> 12.3 us
  starting transfers between devices: 3.85 us -> 43.2 us
    dot_general x58 -> x20, matrix products: 617 us -> 90.6 us  [the longest x8 42.2 us: contract(): return lax.dot_general(left, right, dims, preferred_element_type=F)]
    psum x1, waiting for transfers between devices: 635 us -> 253 us  [local(): lax.psum((embed_part, feed_parts[0], attn_parts[0]), 'dp')]
    reduce_scatter x2 -> x3, waiting for transfers between devices: 436 us -> 56.3 us  [the longest x2 56.3 us: local(): feed_parts[layer_at] = lax.psum_scatter(feed_owned, 'unit')]
    pallas_call x0 -> x21, Pallas kernels: none -> 373 us  [the longest x2 69.9 us: attend_back(): pl.pallas_call(functools.partial(attend_back_kernel, block=QUERY_BLOCK, s...]
    all_gather x2, waiting for transfers between devices: 215 us -> 0.01 us  [local(): feed_low.append(lax.all_gather(own, 'unit', axis=1, tiled=True))]
    ppermute x1 -> x45, waiting for transfers between devices: 0.01 us -> 115 us  [the longest x25 64.5 us: across(): return lax.ppermute(value, 'unit', pairs)]
    scatter-add x9 -> x0, other arithmetic: 111 us -> none  [the longest x8 106 us: owner_rows(): jax.ops.segment_sum(grad_looked, jnp.where(inside, relative, vocab_dev),...]
    reduce_sum x21 -> x10, other arithmetic: 87.5 us -> 7.36 us  [the longest x1 4.39 us: local(): sum_exp = jnp.sum(jnp.exp(logits - row_max[:, None]), axis=1)]
  transfers between devices with their start and end apart: 6 -> 51, of which waited for: 4 -> 23; matrix products, arithmetic and copies ran while one was open for 14% -> 13% of each run, Pallas kernels for 0% -> 22%
where the time goes in v1:
time: 1130 us; the launch traced here: 1120 us
  waiting for transfers between devices  425 us (38%)
  Pallas kernels  373 us (33%)
  other arithmetic  115 us (10%)
  matrix products  90.6 us (8%)
  local copies, waits for them, and re-layouts  44.7 us (4%)
  starting transfers between devices  43.2 us (4%)
  between operations  19.3 us (2%)
  blocking collectives  12.3 us (1%)
    psum x1, waiting for transfers between devices, local(): lax.psum((embed_part, feed_parts[0], attn_parts[0]), 'dp')  253 us
    pallas_call x2, Pallas kernels, attend_back(): pl.pallas_call(functools.partial(attend_back_kernel, block=QUERY_BLOCK, s...  69.9 us
    ppermute x25, waiting for transfers between devices, across(): return lax.ppermute(value, 'unit', pairs)  64.5 us
    pallas_call x2, Pallas kernels, feed_back(): pl.pallas_call(feed_back_kernel, grid=(units // block,), in_specs=[whole,...  57.4 us
    reduce_scatter x2, waiting for transfers between devices, local(): feed_parts[layer_at] = lax.psum_scatter(feed_owned, 'unit')  56.3 us
    pallas_call x2, Pallas kernels, feed(): pl.pallas_call(feed_kernel, grid=(units // block,), in_specs=[pl.BlockSpe...  52.3 us
    pallas_call x2, Pallas kernels, attend(): pl.pallas_call(functools.partial(attend_kernel, block=QUERY_BLOCK), grid_...  51.3 us
    dot_general x8, matrix products, contract(): return lax.dot_general(left, right, dims, preferred_element_type=F)  42.2 us
  transfers between devices with their start and end apart: 51, of which 23 were waited for; matrix products, arithmetic and copies ran while one was open for 13% of the time, Pallas kernels for 22%

profile of v1, /device:TPU:0, one launch (start us, length us, event | category | flops | bytes accessed | tf_op | source)
XLA Modules:
  0.0 1123.2 jit_solution(294932347345797472)
XLA Ops:
  20.3 12.3 %scan_ids.3 = (s32[4096]{0:T(1024)}, s32[8]{0:T(128)}) custom-call(s32[4096]{0:T(1024)} %pad_add_fusion.ids, s32[2]{0:T(128)} %pad_add_fusion.2.place), custom_call_target="tpu_custom_call" | custom-call | tf_op jit(solution)/shard_map/scan_ids/pallas_call | solution.py:457
  32.6 15.8 %lookup.1 = (bf16[512,768]{1,0:T(8,128)(2,1)}, bf16[512,768]{1,0:T(8,128)(2,1)}, bf16[512,768]{1,0:T(8,128)(2,1)}, bf16[512,768]{1,0:T(8,128)(2,1)}, bf16[512,76...) custom-call(s32[4096]{0:T(1024)} %pad_add_fusion.ids, ...), custom_call_target="tpu_custom_call" | custom-call | bytes 29884416 | tf_op jit(solution)/shard_map/lookup/pallas_call | solution.py:521
  54.6 7.4 convert_element_type.187
  62.1 9.9 convert_element_type.188.weight_ref
  73.8 12.3 %scan_ids.4 = (s32[4096]{0:T(1024)}, s32[8]{0:T(128)}) custom-call(s32[4096]{0:T(1024)} %pad_add_fusion.ids, s32[2]{0:T(128)} %pad_add_fusion.1.place), custom_call_target="tpu_custom_call" | custom-call | tf_op jit(solution)/shard_map/scan_ids/pallas_call | solution.py:457
  88.1 16.8 %collective-permute-done.7 = bf16[512,768]{1,0:T(8,128)(2,1)} collective-permute-done((bf16[512,768]{1,0:T(8,128)(2,1)}, bf16[512,768]{1,0:T(8,128)(2,1)}, u32[]{:S(2)}, u32[]{:S(2)}) %collective-permute-start.7) | collective-permute-done | bytes 786464 | tf_op jit(solution)/shard_map/ppermute | solution.py:791
  110.0 12.3 %scan_ids.5 = (s32[4096]{0:T(1024)}, s32[8]{0:T(128)}) custom-call(s32[4096]{0:T(1024)} %copy-done.50, s32[2]{0:T(128)} %pad_add_fusion.1.place), custom_call_target="tpu_custom_call" | custom-call | tf_op jit(solution)/shard_map/scan_ids/pallas_call | solution.py:457
  139.4 10.8 project.2
  151.9 25.7 %attend.2 = (bf16[768,1024]{1,0:T(8,128)(2,1)}, f32[6,8,1024]{2,1,0:T(8,128)}) custom-call(s32[8]{0:T(128)} %pad_add_fusion.3.window_ref, f32[12]{0:T(128)} %get-tuple-element.389.gate_ref, bf16[3,1024,768]{2,1,0:T(8,128)(2,1)} %get-tuple-element.153.k_ref.q_ref.v_ref, bf16[3,768,1024]{2,1,0:T(8,128)(2,1)} %get-tuple-element.154.qt_ref.vt_ref.kt_ref, ...), custom_call_target="tpu_custom_call" | custom-call | flops 3221225472 | bytes 6291456 | tf_op jit(solution)/shard_map/attend/pallas_call | solution.py:115
  185.6 26.0 %feed.2 = (bf16[1024,3072]{1,0:T(8,128)(2,1)}, bf16[1024,3072]{1,0:T(8,128)(2,1)}, f32[1024,768]{1,0:T(8,128)}) custom-call(bf16[1024,768]{1,0:T(8,128)(2,1)} %fusion.8.x_ref, bf16[2,3072,768]{2,1,0:T(8,128)(2,1)} %bitcast.447, bf16[2,3072,768]{2,1,0:T(8,128)(2,1)} %bitcast.448, f32[1,1,3072]{2,1,0:T(1,128)} %get-tuple-element.375.scale_ref), custom_call_target="tpu_custom_call" | custom-call | flops 9663676416 | bytes 26738688 | tf_op jit(solution)/shard_map/feed/pallas_call | solution.py:341
  218.6 10.8 project.3
  229.5 25.6 %attend.3 = (bf16[768,1024]{1,0:T(8,128)(2,1)}, f32[6,8,1024]{2,1,0:T(8,128)}) custom-call(s32[8]{0:T(128)} %pad_add_fusion.3.window_ref, f32[12]{0:T(128)} %get-tuple-element.388.gate_ref, bf16[3,1024,768]{2,1,0:T(8,128)(2,1)} %get-tuple-element.158.k_ref.q_ref.v_ref, bf16[3,768,1024]{2,1,0:T(8,128)(2,1)} %get-tuple-element.159.qt_ref.vt_ref.kt_ref, ...), custom_call_target="tpu_custom_call" | custom-call | flops 3221225472 | bytes 6291456 | tf_op jit(solution)/shard_map/attend/pallas_call | solution.py:115
  263.0 26.3 %feed.3 = (bf16[1024,3072]{1,0:T(8,128)(2,1)}, bf16[1024,3072]{1,0:T(8,128)(2,1)}, f32[1024,768]{1,0:T(8,128)}) custom-call(bf16[1024,768]{1,0:T(8,128)(2,1)} %fusion.10.x_ref, bf16[2,3072,768]{2,1,0:T(8,128)(2,1)} %all-gather.6.cloned.1.call-done.up_ref.down_ref, bf16[2,3072,768]{2,1,0:T(8,128)(2,1)} %all-gather.6.cloned.1.call-done.up_ref.down_ref, ...), custom_call_target="tpu_custom_call" | custom-call | flops 9663676416 | bytes 26738688 | tf_op jit(solution)/shard_map/feed/pallas_call | solution.py:341
  312.4 8.5 fusion.65
  346.6 7.3 fusion.68
  380.5 28.7 %feed_back.2 = (f32[1024,768]{1,0:T(8,128)}, bf16[8,2,384,768]{3,2,1,0:T(8,128)(2,1)}) custom-call(bf16[1024,768]{1,0:T(8,128)(2,1)} %get-tuple-element.283.grad_ref, bf16[1024,768]{1,0:T(8,128)(2,1)} %fusion.10.x_ref, bf16[1024,3072]{1,0:T(8,128)(2,1)} %get-tuple-element.173.act_ref, bf16[1024,3072]{1,0:T(8,128)(2,1)} %get-tuple-element.174.slope_ref, ...), custom_call_target="tpu_custom_call" | custom-call | flops 19327352832 | bytes 37748736 | tf_op jit(solution)/shard_map/feed_back/pallas_call | solution.py:404
  426.9 34.9 %attend_back.2 = bf16[3,1024,768]{2,1,0:T(8,128)(2,1)} custom-call(s32[8]{0:T(128)} %pad_add_fusion.3.window_ref, bf16[3,1024,768]{2,1,0:T(8,128)(2,1)} %get-tuple-element.158.k_ref.q_ref.v_ref, bf16[3,768,1024]{2,1,0:T(8,128)(2,1)} %get-tuple-element.159.qt_ref.vt_ref.kt_ref, bf16[3,1024,768]{2,1,0:T(8,128)(2,1)} %get-tuple-element.158.k_ref.q_ref.v_ref, ...), custom_call_target="tpu_custom_call" | custom-call | flops 8053063680 | bytes 15728640 | tf_op jit(solution)/shard_map/attend_back/pallas_call | solution.py:222
  461.8 8.2 bitcast_add_fusion.1
  484.5 28.7 %feed_back.3 = (f32[1024,768]{1,0:T(8,128)}, bf16[8,2,384,768]{3,2,1,0:T(8,128)(2,1)}) custom-call(bf16[1024,768]{1,0:T(8,128)(2,1)} %get-tuple-element.180.grad_ref, bf16[1024,768]{1,0:T(8,128)(2,1)} %fusion.8.x_ref, bf16[1024,3072]{1,0:T(8,128)(2,1)} %get-tuple-element.181.act_ref, bf16[1024,3072]{1,0:T(8,128)(2,1)} %get-tuple-element.182.slope_ref, ...), custom_call_target="tpu_custom_call" | custom-call | flops 19327352832 | bytes 37748736 | tf_op jit(solution)/shard_map/feed_back/pallas_call | solution.py:404
  514.3 10.2 fusion.69.begin
  536.4 35.0 %attend_back.3 = bf16[3,1024,768]{2,1,0:T(8,128)(2,1)} custom-call(s32[8]{0:T(128)} %pad_add_fusion.3.window_ref, bf16[3,1024,768]{2,1,0:T(8,128)(2,1)} %get-tuple-element.153.k_ref.q_ref.v_ref, bf16[3,768,1024]{2,1,0:T(8,128)(2,1)} %get-tuple-element.154.qt_ref.vt_ref.kt_ref, bf16[3,1024,768]{2,1,0:T(8,128)(2,1)} %get-tuple-element.153.k_ref.q_ref.v_ref, ...), custom_call_target="tpu_custom_call" | custom-call | flops 8053063680 | bytes 15728640 | tf_op jit(solution)/shard_map/attend_back/pallas_call | solution.py:222
  571.4 7.8 bitcast_add_fusion
  592.5 56.2 %reduce-scatter.4.cloned.1.call-done = bf16[1,2,384,768]{3,2,1,0:T(8,128)(2,1)} async-done(((bf16[8,2,384,768]{3,2,1,0:T(8,128)(2,1)}), bf16[1,2,384,768]{3,2,1,0:T(8,128)(2,1)}) %reduce-scatter.4.cloned.1.call-update) | async-done | bytes 1179664 | tf_op jit(solution)/shard_map/reduce_scatter | solution.py:1108
  657.7 11.3 %collective-permute-done.31 = bf16[312,768]{1,0:T(8,128)(2,1)S(1)} collective-permute-done((bf16[312,768]{1,0:T(8,128)(2,1)S(1)}, bf16[312,768]{1,0:T(8,128)(2,1)S(1)}, u32[]{:S(2)}, u32[]{:S(2)}) %collective-permute-start.31) | collective-permute-done | bytes 479264 | tf_op jit(solution)/shard_map/ppermute | solution.py:815
  670.1 18.9 %collective-permute-done.32 = bf16[312,768]{1,0:T(8,128)(2,1)S(1)} collective-permute-done((bf16[312,768]{1,0:T(8,128)(2,1)S(1)}, bf16[312,768]{1,0:T(8,128)(2,1)S(1)}, u32[]{:S(2)}, u32[]{:S(2)}) %collective-permute-start.32) | collective-permute-done | bytes 479264 | tf_op jit(solution)/shard_map/ppermute | solution.py:815
  700.5 23.6 %collective-permute-done.26.rest_3_ = bf16[512,768]{1,0:T(8,128)(2,1)} collective-permute-done((bf16[512,768]{1,0:T(8,128)(2,1)S(1)}, bf16[512,768]{1,0:T(8,128)(2,1)}, u32[]{:S(2)}, u32[]{:S(2)}) %collective-permute-start.26) | collective-permute-done | bytes 786464 | tf_op jit(solution)/shard_map/ppermute | solution.py:791
  730.4 10.4 collective-permute-done.43
  752.2 26.8 %spread.1 = bf16[3840,768]{1,0:T(8,128)(2,1)} custom-call(s32[4096]{0:T(1024)} %pad_add_fusion.ids, s32[4096]{0:T(1024)} %copy-done.50, s32[2]{0:T(128)} %pad_add_fusion.1.place, s32[4096]{0:T(1024)} %get-tuple-element.135.found, s32[8]{0:T(128)} %get-tuple-element.136.ends, s32[4096]{0:T(1024)} %get-tuple-element.143.other_found, ...), custom_call_target="tpu_custom_call" | custom-call | bytes 30277632 | tf_op jit(solution)/shard_map/spread/pallas_call | solution.py:605
  797.7 253.0 %all-reduce.4.cloned.1.call-done = (bf16[3840,768]{1,0:T(8,128)(2,1)}, bf16[4,96,768]{2,1,0:T(8,128)(2,1)}, bf16[2,384,768]{2,1,0:T(8,128)(2,1)}) async-done(((bf16[3840,768]{1,0:T(8,128)(2,1)}, bf16[4,96,768]{2,1,0:T(8,128)(2,1)}, bf16[2,384,768]{2,1,0:T(8,128)(2,1)}), (bf16[3840,768]{1,0:T(8,128)(2,1)}, bf16[4,96,768]{2,1,0:T(8,128)(2,1)}, bf16[2,384,768]{2,1,0:T(8,128)(2,1)})) %all-reduce.4.cloned.1.call-update) | async-done | bytes 7667728 | tf_op jit(solution)/shard_map/psum | solution.py:1190
  1057.9 12.3 %all-gather.2.parts_ref = f32[8,26,768]{2,1,0:T(8,128)} all-gather(f32[1,26,768]{2,1,0:T(8,128)} %bitcast.409), channel_id=3, replica_groups=mesh['dp'=4,'unit'=8] {'unit'}, dimensions={0}, use_global_device_ids=true | all-gather | bytes 718848 | tf_op jit(solution)/shard_map/all_gather | solution.py:1226
  1078.1 16.5 %renew.4 = (f32[1,3840,768]{2,1,0:T(8,128)}, f32[1,3840,768]{2,1,0:T(8,128)}, f32[1,6,1,640]{3,2,1,0:T(1,128)}) custom-call(f32[3]{0:T(128)} %get-tuple-element.214.scalars_ref, s32[1]{0:T(128)} %constant.194.clone.1.at_ref, f32[14,1,768]{2,1,0:T(1,128)} %broadcast_in_dim.62.factor_ref, f32[1,3840,1]{2,1,0:T(8,128)} %broadcast_in_dim_broadcast_in_dim.8.rows_ref, ...), custom_call_target="tpu_custom_call" | custom-call | tf_op jit(solution)/shard_map/renew/pallas_call | solution.py:759
  1097.7 7.9 renew.6
  (480 shorter events, 285.7 us)
Async XLA Ops:
  7.2 178.4 %all-gather.8.cloned.1.call-start = ((), (), s32[]{:S(2)}) async-start(), calls=%async_computation.7 | async-start | bytes 10616832 | tf_op jit(solution)/shard_map/all_gather | solution.py:979
  11.5 251.6 %all-gather.6.cloned.1.call-start = ((), (), s32[]{:S(2)}) async-start(), calls=%async_computation.3 | async-start | bytes 10616832 | tf_op jit(solution)/shard_map/all_gather | solution.py:979
  11.5 21.1 %collective-permute-start.4 = (f32[3840,768]{1,0:T(8,128)}, f32[3840,768]{1,0:T(8,128)}, u32[]{:S(2)}, u32[]{:S(2)}) collective-permute-start(f32[3840,768]{1,0:T(8,128)} %own.1), channel_id=1, source_target_pairs={{0,1},{1,0},{2,3},{3,2},{4,5},{5,4},{6,7},{7,6},{8,9},{9,8},{10,11... | collective-permute-start | bytes 35389448 | tf_op jit(solution)/shard_map/ppermute | solution.py:795
  48.4 37.7 %collective-permute-start.5 = (bf16[512,768]{1,0:T(8,128)(2,1)}, bf16[512,768]{1,0:T(8,128)(2,1)S(1)}, u32[]{:S(2)}, u32[]{:S(2)}) collective-permute-start(bf16[512,768]{1,0:T(8,128)(2,1)} %get-tuple-element.129), channel_id=1, source_target_pairs={{0,4},{1,5},{2,6},{3,7},{4,0},{5,1},{6,2},{7,3},{8,12},{9,13},{10,... | collective-permute-start | bytes 2359304 | tf_op jit(solution)/shard_map/ppermute | solution.py:791
  49.7 38.4 %collective-permute-start.6 = (bf16[512,768]{1,0:T(8,128)(2,1)}, bf16[512,768]{1,0:T(8,128)(2,1)S(1)}, u32[]{:S(2)}, u32[]{:S(2)}) collective-permute-start(bf16[512,768]{1,0:T(8,128)(2,1)} %get-tuple-element.130), channel_id=1, source_target_pairs={{0,2},{1,3},{2,0},{3,1},{4,6},{5,7},{6,4},{7,5},{8,10},{9,11},{10,... | collective-permute-start | bytes 2359304 | tf_op jit(solution)/shard_map/ppermute | solution.py:791
  54.5 50.4 %collective-permute-start.7 = (bf16[512,768]{1,0:T(8,128)(2,1)}, bf16[512,768]{1,0:T(8,128)(2,1)}, u32[]{:S(2)}, u32[]{:S(2)}) collective-permute-start(bf16[512,768]{1,0:T(8,128)(2,1)} %get-tuple-element.131), channel_id=1, source_target_pairs={{0,4},{1,5},{2,6},{3,7},{4,0},{5,1},{6,2},{7,3},{8,12},{9,13},{10,... | collective-permute-start | bytes 2359304 | tf_op jit(solution)/shard_map/ppermute | solution.py:791
  54.5 50.3 %collective-permute-start.8 = (bf16[512,768]{1,0:T(8,128)(2,1)}, bf16[512,768]{1,0:T(8,128)(2,1)}, u32[]{:S(2)}, u32[]{:S(2)}) collective-permute-start(bf16[512,768]{1,0:T(8,128)(2,1)} %get-tuple-element.132), channel_id=1, source_target_pairs={{0,2},{1,3},{2,0},{3,1},{4,6},{5,7},{6,4},{7,5},{8,10},{9,11},{10,... | collective-permute-start | bytes 2359304 | tf_op jit(solution)/shard_map/ppermute | solution.py:791
  105.9 19.6 %collective-permute-start.9 = (bf16[512,768]{1,0:T(8,128)(2,1)}, bf16[512,768]{1,0:T(8,128)(2,1)S(1)}, u32[]{:S(2)}, u32[]{:S(2)}) collective-permute-start(bf16[512,768]{1,0:T(8,128)(2,1)} %add.340), channel_id=1, source_target_pairs={{0,2},{1,3},{2,0},{3,1},{4,6},{5,7},{6,4},{7,5},{8,10},{9,11},{10,... | collective-permute-start | bytes 2359304 | tf_op jit(solution)/shard_map/ppermute | solution.py:791
  107.6 19.3 %collective-permute-start.10 = (bf16[512,768]{1,0:T(8,128)(2,1)S(1)}, bf16[512,768]{1,0:T(8,128)(2,1)S(1)}, u32[]{:S(2)}, u32[]{:S(2)}) collective-permute-start(bf16[512,768]{1,0:T(8,128)(2,1)S(1)} %add.341), channel_id=1, source_target_pairs={{0,4},{1,5},{2,6},{3,7},{4,0},{5,1},{6,2},{7,3},{8,12},{9,13},{10,... | collective-permute-start | bytes 2359304 | tf_op jit(solution)/shard_map/ppermute | solution.py:791
  129.5 462.9 %reduce-scatter.6.cloned.1.call-start = ((), (), s32[]{:S(2)}) async-start(), calls=%async_computation.5 | async-start | bytes 6635520 | tf_op jit(solution)/shard_map/reduce_scatter | solution.py:1104
  129.6 82.0 %collective-permute-start.11 = (bf16[1024,768]{1,0:T(8,128)(2,1)}, bf16[1024,768]{1,0:T(8,128)(2,1)}, u32[]{:S(2)}, u32[]{:S(2)}) collective-permute-start(bf16[1024,768]{1,0:T(8,128)(2,1)} %bitcast.455), channel_id=1, source_target_pairs={{0,4},{1,5},{2,6},{3,7},{4,0},{5,1},{6,2},{7,3},{8,12},{9,13},{10,... | collective-permute-start | bytes 4718600 | tf_op jit(solution)/shard_map/ppermute | solution.py:980
  483.9 164.9 %reduce-scatter.4.cloned.1.call-start = ((), (), s32[]{:S(2)}) async-start(), calls=%async_computation.4 | async-start | bytes 10616832 | tf_op jit(solution)/shard_map/reduce_scatter | solution.py:1108
  484.4 297.1 %reduce-scatter.8.cloned.1.call-start = ((), (), s32[]{:S(2)}) async-start(), calls=%async_computation.6 | async-start | bytes 10616832 | tf_op jit(solution)/shard_map/reduce_scatter | solution.py:1108
  513.2 537.5 %all-reduce.4.cloned.1.call-start = ((), (), s32[]{:S(2)}) async-start(), calls=%async_computation.8 | async-start | bytes 15335424 | tf_op jit(solution)/shard_map/psum | solution.py:1190
  583.1 68.5 %collective-permute-start.24 = (bf16[1024,768]{1,0:T(8,128)(2,1)}, bf16[1024,768]{1,0:T(8,128)(2,1)}, u32[]{:S(2)}, u32[]{:S(2)}) collective-permute-start(bf16[1024,768]{1,0:T(8,128)(2,1)} %multiply_convert_fusion.rest_0_), channel_id=1, source_target_pairs={{0,2},{1,3},{2,0},{3,1},{4,6},{5,7},{6,4},{7,5},{8,10},{9,11},{10,... | collective-permute-start | bytes 4718600 | tf_op jit(solution)/shard_map/ppermute | solution.py:791
  583.1 68.5 %collective-permute-start.25 = (bf16[1024,768]{1,0:T(8,128)(2,1)}, bf16[1024,768]{1,0:T(8,128)(2,1)}, u32[]{:S(2)}, u32[]{:S(2)}) collective-permute-start(bf16[1024,768]{1,0:T(8,128)(2,1)} %multiply_convert_fusion.rest_0_), channel_id=1, source_target_pairs={{0,4},{1,5},{2,6},{3,7},{4,0},{5,1},{6,2},{7,3},{8,12},{9,13},{10,... | collective-permute-start | bytes 4718600 | tf_op jit(solution)/shard_map/ppermute | solution.py:791
  651.6 44.4 %collective-permute-start.30 = (bf16[4,4,96,768]{3,2,1,0:T(8,128)(2,1)}, bf16[4,4,96,768]{3,2,1,0:T(8,128)(2,1)}, u32[]{:S(2)}, u32[]{:S(2)}) collective-permute-start(bf16[4,4,96,768]{3,2,1,0:T(8,128)(2,1)} %bitcast.385), channel_id=1, source_target_pairs={{0,1},{1,0},{2,3},{3,2},{4,5},{5,4},{6,7},{7,6},{8,9},{9,8},{10,11... | collective-permute-start | bytes 7077896 | tf_op jit(solution)/shard_map/ppermute | solution.py:795
  654.8 69.2 %collective-permute-start.28 = (bf16[1024,768]{1,0:T(8,128)(2,1)}, bf16[1024,768]{1,0:T(8,128)(2,1)S(1)}, u32[]{:S(2)}, u32[]{:S(2)}) collective-permute-start(bf16[1024,768]{1,0:T(8,128)(2,1)} %collective-permute-done.24.rest_1_), channel_id=1, source_target_pairs={{0,1},{1,0},{2,3},{3,2},{4,5},{5,4},{6,7},{7,6},{8,9},{9,8},{10,11... | collective-permute-start | bytes 4718600 | tf_op jit(solution)/shard_map/ppermute | solution.py:795
  655.0 69.1 %collective-permute-start.29 = (bf16[1024,768]{1,0:T(8,128)(2,1)}, bf16[1024,768]{1,0:T(8,128)(2,1)S(1)}, u32[]{:S(2)}, u32[]{:S(2)}) collective-permute-start(bf16[1024,768]{1,0:T(8,128)(2,1)} %collective-permute-done.25.rest_2_), channel_id=1, source_target_pairs={{0,1},{1,0},{2,3},{3,2},{4,5},{5,4},{6,7},{7,6},{8,9},{9,8},{10,11... | collective-permute-start | bytes 4718600 | tf_op jit(solution)/shard_map/ppermute | solution.py:795
  655.3 33.7 %collective-permute-start.32 = (bf16[312,768]{1,0:T(8,128)(2,1)S(1)}, bf16[312,768]{1,0:T(8,128)(2,1)S(1)}, u32[]{:S(2)}, u32[]{:S(2)}) collective-permute-start(bf16[312,768]{1,0:T(8,128)(2,1)S(1)} %get-tuple-element.302), channel_id=1, source_target_pairs={{0,16},{8,24},{16,0},{24,8},{1,17},{9,25},{17,1},{25,9},{2,18},{10... | collective-permute-start | bytes 1437704 | tf_op jit(solution)/shard_map/ppermute | solution.py:815
  669.0 25.7 %collective-permute-start.33 = (bf16[312,768]{1,0:T(8,128)(2,1)S(1)}, bf16[312,768]{1,0:T(8,128)(2,1)S(1)}, u32[]{:S(2)}, u32[]{:S(2)}) collective-permute-start(bf16[312,768]{1,0:T(8,128)(2,1)S(1)} %get-tuple-element.301), channel_id=1, source_target_pairs={{0,24},{8,0},{16,8},{24,16},{1,25},{9,1},{17,9},{25,17},{2,26},{10... | collective-permute-start | bytes 1437704 | tf_op jit(solution)/shard_map/ppermute | solution.py:815
  689.0 58.4 %collective-permute-start.34 = (bf16[1024,768]{1,0:T(8,128)(2,1)}, bf16[1024,768]{1,0:T(8,128)(2,1)}, u32[]{:S(2)}, u32[]{:S(2)}) collective-permute-start(bf16[1024,768]{1,0:T(8,128)(2,1)} %multiply_convert_fusion.rest_0_), channel_id=1, source_target_pairs={{0,1},{1,0},{2,3},{3,2},{4,5},{5,4},{6,7},{7,6},{8,9},{9,8},{10,11... | collective-permute-start | bytes 4718600 | tf_op jit(solution)/shard_map/ppermute | solution.py:795
  694.6 29.4 %collective-permute-start.26 = (bf16[512,768]{1,0:T(8,128)(2,1)S(1)}, bf16[512,768]{1,0:T(8,128)(2,1)}, u32[]{:S(2)}, u32[]{:S(2)}) collective-permute-start(bf16[512,768]{1,0:T(8,128)(2,1)S(1)} %slice.482), channel_id=1, source_target_pairs={{0,4},{1,5},{2,6},{3,7},{4,0},{5,1},{6,2},{7,3},{8,12},{9,13},{10,... | collective-permute-start | bytes 2359304 | tf_op jit(solution)/shard_map/ppermute | solution.py:791
  696.0 28.1 %collective-permute-start.27 = (bf16[512,768]{1,0:T(8,128)(2,1)S(1)}, bf16[512,768]{1,0:T(8,128)(2,1)}, u32[]{:S(2)}, u32[]{:S(2)}) collective-permute-start(bf16[512,768]{1,0:T(8,128)(2,1)S(1)} %slice.483), channel_id=1, source_target_pairs={{0,2},{1,3},{2,0},{3,1},{4,6},{5,7},{6,4},{7,5},{8,10},{9,11},{10,... | collective-permute-start | bytes 2359304 | tf_op jit(solution)/shard_map/ppermute | solution.py:791
  724.1 25.4 %collective-permute-start.35 = (bf16[512,768]{1,0:T(8,128)(2,1)}, bf16[512,768]{1,0:T(8,128)(2,1)}, u32[]{:S(2)}, u32[]{:S(2)}) collective-permute-start(bf16[512,768]{1,0:T(8,128)(2,1)} %collective-permute-done.26.rest_3_), channel_id=1, source_target_pairs={{0,1},{1,0},{2,3},{3,2},{4,5},{5,4},{6,7},{7,6},{8,9},{9,8},{10,11... | collective-permute-start | bytes 2359304 | tf_op jit(solution)/shard_map/ppermute | solution.py:795
  724.1 25.8 %collective-permute-start.36 = (bf16[512,768]{1,0:T(8,128)(2,1)}, bf16[512,768]{1,0:T(8,128)(2,1)}, u32[]{:S(2)}, u32[]{:S(2)}) collective-permute-start(bf16[512,768]{1,0:T(8,128)(2,1)} %collective-permute-done.27.rest_4_), channel_id=1, source_target_pairs={{0,1},{1,0},{2,3},{3,2},{4,5},{5,4},{6,7},{7,6},{8,9},{9,8},{10,11... | collective-permute-start | bytes 2359304 | tf_op jit(solution)/shard_map/ppermute | solution.py:795
  725.2 22.8 %collective-permute-start.40 = (bf16[312,768]{1,0:T(8,128)(2,1)S(1)}, bf16[312,768]{1,0:T(8,128)(2,1)}, u32[]{:S(2)}, u32[]{:S(2)}) collective-permute-start(bf16[312,768]{1,0:T(8,128)(2,1)S(1)} %add_convert_fusion.1), channel_id=1, source_target_pairs={{0,8},{8,16},{16,24},{24,0},{1,9},{9,17},{17,25},{25,1},{2,10},{10... | collective-permute-start | bytes 1437704 | tf_op jit(solution)/shard_map/ppermute | solution.py:828
  745.9 33.0 %collective-permute-start.37 = (bf16[4,96,768]{2,1,0:T(8,128)(2,1)}, bf16[4,96,768]{2,1,0:T(8,128)(2,1)}, u32[]{:S(2)}, u32[]{:S(2)}) collective-permute-start(bf16[4,96,768]{2,1,0:T(8,128)(2,1)} %get-tuple-element.298), channel_id=1, source_target_pairs={{0,2},{1,3},{2,0},{3,1},{4,6},{5,7},{6,4},{7,5},{8,10},{9,11},{10,... | collective-permute-start | bytes 1769480 | tf_op jit(solution)/shard_map/ppermute | solution.py:791
  747.4 31.6 %collective-permute-start.38 = (bf16[4,96,768]{2,1,0:T(8,128)(2,1)}, bf16[4,96,768]{2,1,0:T(8,128)(2,1)}, u32[]{:S(2)}, u32[]{:S(2)}) collective-permute-start(bf16[4,96,768]{2,1,0:T(8,128)(2,1)} %get-tuple-element.297), channel_id=1, source_target_pairs={{0,4},{1,5},{2,6},{3,7},{4,0},{5,1},{6,2},{7,3},{8,12},{9,13},{10,... | collective-permute-start | bytes 1769480 | tf_op jit(solution)/shard_map/ppermute | solution.py:791
  748.0 31.0 %collective-permute-start.39 = (bf16[4,96,768]{2,1,0:T(8,128)(2,1)S(1)}, bf16[4,96,768]{2,1,0:T(8,128)(2,1)}, u32[]{:S(2)}, u32[]{:S(2)}) collective-permute-start(bf16[4,96,768]{2,1,0:T(8,128)(2,1)S(1)} %get-tuple-element.296), channel_id=1, source_target_pairs={{0,6},{1,7},{2,4},{3,5},{4,2},{5,3},{6,0},{7,1},{8,14},{9,15},{10,... | collective-permute-start | bytes 1769480 | tf_op jit(solution)/shard_map/ppermute | solution.py:791
  749.4 29.5 %collective-permute-start.41 = (bf16[312,768]{1,0:T(8,128)(2,1)S(1)}, bf16[312,768]{1,0:T(8,128)(2,1)}, u32[]{:S(2)}, u32[]{:S(2)}) collective-permute-start(bf16[312,768]{1,0:T(8,128)(2,1)S(1)} %add_convert_fusion.1), channel_id=1, source_target_pairs={{0,16},{8,24},{16,0},{24,8},{1,17},{9,25},{17,1},{25,9},{2,18},{10... | collective-permute-start | bytes 1437704 | tf_op jit(solution)/shard_map/ppermute | solution.py:828
  750.0 29.0 %collective-permute-start.42 = (bf16[312,768]{1,0:T(8,128)(2,1)S(1)}, bf16[312,768]{1,0:T(8,128)(2,1)}, u32[]{:S(2)}, u32[]{:S(2)}) collective-permute-start(bf16[312,768]{1,0:T(8,128)(2,1)S(1)} %add_convert_fusion.1), channel_id=1, source_target_pairs={{0,24},{8,0},{16,8},{24,16},{1,25},{9,1},{17,9},{25,17},{2,26},{10... | collective-permute-start | bytes 1437704 | tf_op jit(solution)/shard_map/ppermute | solution.py:828
  (110 other events, 1481.5 us)
Sparse Core Ops, SparseCore 0:
  11.6 82.0 all-gather.7
  129.7 75.3 all-gather.5
  484.0 60.0 reduce-scatter.5
  547.5 101.2 reduce-scatter.3
  652.1 87.0 reduce-scatter.7
  781.8 268.8 all-reduce.3

commit v2 on v1

--- a/solution.py
+++ b/solution.py
@@ -63,10 +63,11 @@
     return (key_seg == query_seg) | (key_at == query_at)
 
 
-def head_rows(block, head):
+def head_rows(block):
     empty = jnp.zeros((HD, block.shape[1]), block.dtype)
-    parts = [block[:HD], empty] if head == 0 else [empty, block[HD:]]
-    return jnp.concatenate(parts, axis=0)
+    first = jnp.concatenate([block[:HD], empty], axis=0)
+    second = jnp.concatenate([empty, block[HD:]], axis=0)
+    return jnp.concatenate([first, second], axis=1)
 
 
 def head_lanes(block):
@@ -97,16 +98,20 @@
                 keys = k_ref[0, pl.ds(start, width), :]
                 mask = window_mask(segk_ref, segq_ref, start, width, i * block, block)
                 queries = qt_ref[0, :, columns]
+                scores = dot(keys, head_rows(queries))
+                scores = jnp.where(jnp.concatenate([mask, mask], axis=1), scores, -MASK_FILL)
+                top = jnp.max(scores, axis=0, keepdims=True)
+                exponent = jnp.exp(scores - top)
+                total = jnp.sum(exponent, axis=0, keepdims=True)
+                mixed = dot(vt_ref[0, :, pl.ds(start, width)], exponent.astype(B))
+                inverse = 1.0 / total
+                log_total = top + jnp.log(total)
                 for head in range(2):
                     rows = slice(head * HD, (head + 1) * HD)
-                    scores = jnp.where(mask, dot(keys, head_rows(queries, head)), -MASK_FILL)
-                    top = jnp.max(scores, axis=0, keepdims=True)
-                    exponent = jnp.exp(scores - top)
-                    total = jnp.sum(exponent, axis=0, keepdims=True)
-                    mixed = dot(vt_ref[0, rows, pl.ds(start, width)], exponent.astype(B))
-                    gated = mixed * (gate_ref[2 * pair + head] / total)
+                    lanes = slice(head * block, (head + 1) * block)
+                    gated = mixed[rows, lanes] * (inverse[:, lanes] * gate_ref[2 * pair + head])
                     ot_ref[rows, columns] = gated.astype(B)
-                    lse_ref[0, head : head + 1, columns] = top + jnp.log(total)
+                    lse_ref[0, head : head + 1, columns] = log_total[:, lanes]
 
 
 def attend(windows, gates, tokens, features, key_segments, query_segments):
@@ -183,24 +188,20 @@
                 mask = window_mask(segk_ref, segq_ref, start, width, i * block, block)
                 queries_t = qt_ref[0, :, columns]
                 grads_t = dot_ref[:, columns]
-                all_prob = []
-                all_grad = []
-                for head in range(2):
-                    rows = slice(head * HD, (head + 1) * HD)
-                    scores = jnp.where(mask, dot(keys, head_rows(queries_t, head)), -MASK_FILL)
-                    prob = jnp.exp(scores - lse_ref[0, head : head + 1, columns])
-                    weighted = prob * dot(values, head_rows(grads_t, head))
-                    inner = jnp.sum(weighted, axis=0, keepdims=True)
-                    grad = (weighted - prob * inner).astype(B)
-                    dq_sum[rows, columns] = dot(kt_ref[0, rows, window], grad) * score_scale
-                    all_prob.append(prob.astype(B))
-                    all_grad.append(grad)
-                dv_sum[window, :] += dot(
-                    jnp.concatenate(all_prob, axis=1), head_lanes(do_ref[columns, :])
+                scores = dot(keys, head_rows(queries_t))
+                scores = jnp.where(jnp.concatenate([mask, mask], axis=1), scores, -MASK_FILL)
+                log_total = jnp.concatenate(
+                    [lse_ref[0, 0:1, columns], lse_ref[0, 1:2, columns]], axis=1
                 )
-                dk_sum[window, :] += dot(
-                    jnp.concatenate(all_grad, axis=1), head_lanes(q_ref[0, columns, :])
-                )
+                prob = jnp.exp(scores - log_total)
+                weighted = prob * dot(values, head_rows(grads_t))
+                inner = jnp.sum(weighted, axis=0, keepdims=True)
+                grad = (weighted - prob * inner).astype(B)
+                grad_q = dot(kt_ref[0, :, window], grad) * score_scale
+                dq_sum[:HD, columns] = grad_q[:HD, :block]
+                dq_sum[HD:, columns] = grad_q[HD:, block:]
+                dv_sum[window, :] += dot(prob.astype(B), head_lanes(do_ref[columns, :]))
+                dk_sum[window, :] += dot(grad, head_lanes(q_ref[0, columns, :]))
 
     grad_ref[0] = jnp.transpose(dq_sum[...]).astype(B)
     grad_ref[1] = dk_sum[...].astype(B)
@@ -823,15 +824,17 @@
     for part in parts[1:]:
         total = total + part.astype(F)
     total = total.astype(B)
-    share = total.shape[0]
     found = [total] + [
         lax.ppermute(total, "dp", [(d, (d + step) % size) for d in range(size)])
         for step in range(1, size)
     ]
-    return found, share, at, size
-
-
-def dp_placed(found, share, at, size):
+    return found
+
+
+def dp_placed(found):
+    size = len(found)
+    at = lax.axis_index("dp")
+    share = found[0].shape[0]
     result = jnp.zeros((size * share,) + found[0].shape[1:], found[0].dtype)
     for step, part in enumerate(found):
         result = lax.dynamic_update_slice_in_dim(result, part, (at - step) % size * share, 0)
@@ -1076,7 +1079,6 @@
     grad_picked = both[0]
     for step in range(1, chips):
         grad_picked = grad_picked + across(both[step], step)
-    grad_table = contract(grad_logits, picked_rows, TN)
 
     loss_part = error_part + jnp.sum(own_terms)
     grad_hidden = grad_final + lax.dot_general(
@@ -1090,6 +1092,7 @@
     gain_rows = [None] * norm_params.shape[0]
     feed_parts = [None] * layer_count
     attn_parts = [None] * layer_count
+    later_feeds = []
     for layer_at in reversed(range(layer_count)):
         attn_stored, norm_first, feed_stored, norm_second = stored_layers[layer_at]
         hidden_low, tokens, features, gated_t, log_total = attn_stored
@@ -1105,6 +1108,9 @@
         grad_middle, feed_owned = feed_back(
             grad_result, middle_low, act, slope, feed_low[layer_at], unit_count
         )
+        if layer_at < layer_count - 1:
+            grad_middle, later_feed = together(grad_middle, feed_parts[layer_at + 1])
+            later_feed = dp_scatter(later_feed.reshape(-1, breadth))
         feed_parts[layer_at] = lax.psum_scatter(feed_owned, "unit")
         grad_first, gain_rows[2 + 4 * layer_at], gain_rows[3 + 4 * layer_at] = norm_backward(
             norm_first, norm_params[2 + 4 * layer_at], grad_second + grad_middle
@@ -1123,6 +1129,9 @@
             query_segments,
             log_total,
         )
+        if layer_at < layer_count - 1:
+            grad_proj, later_feed = together(grad_proj, later_feed)
+            later_feeds.append(dp_gather(later_feed))
         grad_input = jnp.einsum("jre,jde->rd", grad_proj, weights[:3], preferred_element_type=F)
         grad_hidden = grad_first + grad_input
         grad_hidden, grad_proj = together(grad_hidden, grad_proj)
@@ -1147,6 +1156,8 @@
                 lax.dynamic_index_in_dim(stack, 1 - core, 2, keepdims=False), 1, 0
             )
 
+    grad_hidden, grad_logits = together(grad_hidden, grad_logits)
+    grad_table = contract(grad_logits, picked_rows, TN)
     grad_looked, gain_rows[0], gain_rows[1] = norm_backward(
         embed_stored, norm_params[0], grad_hidden * hidden_gate
     )
@@ -1154,29 +1165,33 @@
     small = jnp.concatenate(
         [jnp.stack(gain_rows), jnp.broadcast_to(loss_part, (1, breadth))], axis=0
     )
-    pieces = [part.reshape(-1, breadth) for part in feed_parts[1:] + attn_parts[1:]]
-    early = jnp.concatenate(pieces, axis=0)
     same = [(sent, 0), (sent, ROW_BLOCK)]
     other = swapped(sent)
     crossed = [(other, 0), (other, ROW_BLOCK)]
     if chips == 4 and length == 2 * ROW_BLOCK:
         near = [across(sent, 1), across(sent, 2)]
-        near, early, grad_table, attn_theirs = together(near, early, grad_table, attn_theirs)
+        near, later_feeds, later_attn, grad_table, attn_theirs = together(
+            near, later_feeds, attn_parts[1:], grad_table, attn_theirs
+        )
         last = [across(near[0][:ROW_BLOCK], 2), across(near[1][ROW_BLOCK:], 1)]
         near_other = [swapped(part) for part in near]
         attn_chip = chip_sum(attn_mine, swapped(attn_theirs))
-        early = dp_scatter(early)
-        last, near_other, attn_chip, early = together(last, near_other, attn_chip, early)
-        early, *early_place = dp_gather(early)
+        later_attn = [dp_scatter(part.reshape(-1, breadth)) for part in later_attn]
+        last, near_other, attn_chip, later_attn = together(
+            last, near_other, attn_chip, later_attn
+        )
         small = dp_sum(small)
         attn_received = sent_to_owners(attn_chip, chip, range(1, chips))
         last_other = [swapped(part) for part in last]
         for home, parts, ends in ((same, near, last), (crossed, near_other, last_other)):
             home += [(part, at) for part in parts for at in (0, ROW_BLOCK)]
             home += [(part, 0) for part in ends]
+        later_attn = [dp_gather(part) for part in later_attn]
     else:
-        early, *early_place = dp_gather(dp_scatter(early))
         small = dp_sum(small)
+        later_attn = [
+            dp_gather(dp_scatter(part.reshape(-1, breadth))) for part in attn_parts[1:]
+        ]
         attn_chip = chip_sum(attn_mine, swapped(attn_theirs))
         attn_received = sent_to_owners(attn_chip, chip, range(1, chips))
         for step in range(1, chips):
@@ -1184,18 +1199,17 @@
             for home, part in ((same, part), (crossed, swapped(part))):
                 home += [(part, at) for at in range(0, length, ROW_BLOCK)]
     embed_part = spread(all_ids, other_ids, own_place, lists, grad_table, same + crossed)
-    embed_part, attn_received, early, small = together(embed_part, attn_received, early, small)
+    embed_part, attn_received, small, later_attn = together(
+        embed_part, attn_received, small, later_attn
+    )
     attn_parts[0] = owner_total(attn_chip, attn_received, chip)
-    early = dp_placed(early, *early_place)
     embed_sum, feed_first, attn_first = lax.psum((embed_part, feed_parts[0], attn_parts[0]), "dp")
-    feed_sums, attn_sums = [feed_first], [attn_first]
-    cursor = 0
-    for parts, sums in ((feed_parts, feed_sums), (attn_parts, attn_sums)):
-        for part in parts[1:]:
-            rows = part.shape[0] * part.shape[1]
-            sums.append(early[cursor : cursor + rows].reshape(part.shape))
-            cursor += rows
-
+    attn_sums = [attn_first] + [
+        dp_placed(found).reshape(part.shape) for found, part in zip(later_attn, attn_parts[1:])
+    ]
+    feed_sums = [feed_first] + [
+        dp_placed(part).reshape(feed_first.shape) for part in reversed(later_feeds)
+    ]
     row_sums = jnp.concatenate(
         [
             jnp.sum(attention_rows, axis=-1).reshape(-1),

time: 1130 us -> 1070 us (0.947)
  waiting for transfers between devices: 425 us -> 366 us
  Pallas kernels: 373 us -> 355 us
    reduce_scatter x2, waiting for transfers between devices: 56.3 us -> 0.01 us  [local(): feed_parts[layer_at] = lax.psum_scatter(feed_owned, 'unit')]
    ppermute x3 -> x6, waiting for transfers between devices: 33.3 us -> 14.8 us  [dp_scatter(): lax.ppermute(away, 'dp', [(d, (d + step) % size) for d in range(size)])]
    ppermute x25, waiting for transfers between devices: 64.5 us -> 81.3 us  [across(): return lax.ppermute(value, 'unit', pairs)]
    pallas_call x2, Pallas kernels: 51.3 us -> 38.8 us  [attend(): pl.pallas_call(functools.partial(attend_kernel, block=QUERY_BLOCK), grid_...]
  transfers between devices with their start and end apart: 51 -> 57, of which waited for: 23 -> 25; matrix products, arithmetic and copies ran while one was open for 13% -> 17% of each run, Pallas kernels for 22% -> 25%
where the time goes in v2:
time: 1070 us; the launch traced here: 1060 us
  waiting for transfers between devices  366 us (34%)
  Pallas kernels  355 us (33%)
  other arithmetic  121 us (11%)
  matrix products  84.5 us (8%)
  starting transfers between devices  52.2 us (5%)
  local copies, waits for them, and re-layouts  47.3 us (4%)
  between operations  19.4 us (2%)
  blocking collectives  12.2 us (1%)
    psum x1, waiting for transfers between devices, local(): lax.psum((embed_part, feed_parts[0], attn_parts[0]), 'dp')  256 us
    ppermute x25, waiting for transfers between devices, across(): return lax.ppermute(value, 'unit', pairs)  81.3 us
    pallas_call x2, Pallas kernels, attend_back(): pl.pallas_call(functools.partial(attend_back_kernel, block=QUERY_BLOCK, s...  61.2 us
    pallas_call x2, Pallas kernels, feed_back(): pl.pallas_call(feed_back_kernel, grid=(units // block,), in_specs=[whole,...  57.4 us
    pallas_call x2, Pallas kernels, feed(): pl.pallas_call(feed_kernel, grid=(units // block,), in_specs=[pl.BlockSpe...  52.1 us
    pallas_call x2, Pallas kernels, attend(): pl.pallas_call(functools.partial(attend_kernel, block=QUERY_BLOCK), grid_...  38.8 us
    dot_general x8, matrix products, contract(): return lax.dot_general(left, right, dims, preferred_element_type=F)  38.3 us
    pallas_call x3, Pallas kernels, scan_ids(): pl.pallas_call(functools.partial(scan_kernel, vocab=vocab), in_specs=[sme...  36.9 us
  transfers between devices with their start and end apart: 57, of which 25 were waited for; matrix products, arithmetic and copies ran while one was open for 17% of the time, Pallas kernels for 25%

profile of v2, /device:TPU:0, one launch (start us, length us, event | category | flops | bytes accessed | tf_op | source)
XLA Modules:
  0.0 1058.1 jit_solution(3629281140497735952)
XLA Ops:
  20.2 12.3 %scan_ids.3 = (s32[4096]{0:T(1024)}, s32[8]{0:T(128)}) custom-call(s32[4096]{0:T(1024)} %pad_add_fusion.ids, s32[2]{0:T(128)} %pad_add_fusion.2.place), custom_call_target="tpu_custom_call" | custom-call | tf_op jit(solution)/shard_map/scan_ids/pallas_call | solution.py:458
  32.5 19.1 %lookup.1 = (bf16[512,768]{1,0:T(8,128)(2,1)}, bf16[512,768]{1,0:T(8,128)(2,1)}, bf16[512,768]{1,0:T(8,128)(2,1)}, bf16[512,768]{1,0:T(8,128)(2,1)}, bf16[512,76...) custom-call(s32[4096]{0:T(1024)} %pad_add_fusion.ids, ...), custom_call_target="tpu_custom_call" | custom-call | bytes 29884416 | tf_op jit(solution)/shard_map/lookup/pallas_call | solution.py:522
  55.7 7.4 convert_element_type.202
  63.1 10.1 convert_element_type.203.weight_ref
  75.2 12.3 %scan_ids.4 = (s32[4096]{0:T(1024)}, s32[8]{0:T(128)}) custom-call(s32[4096]{0:T(1024)} %pad_add_fusion.ids, s32[2]{0:T(128)} %pad_add_fusion.1.place), custom_call_target="tpu_custom_call" | custom-call | tf_op jit(solution)/shard_map/scan_ids/pallas_call | solution.py:458
  88.7 16.1 %collective-permute-done.7 = bf16[512,768]{1,0:T(8,128)(2,1)} collective-permute-done((bf16[512,768]{1,0:T(8,128)(2,1)}, bf16[512,768]{1,0:T(8,128)(2,1)}, u32[]{:S(2)}, u32[]{:S(2)}) %collective-permute-start.7) | collective-permute-done | bytes 786464 | tf_op jit(solution)/shard_map/ppermute | solution.py:792
  110.0 12.3 %scan_ids.5 = (s32[4096]{0:T(1024)}, s32[8]{0:T(128)}) custom-call(s32[4096]{0:T(1024)} %copy-done.61, s32[2]{0:T(128)} %pad_add_fusion.1.place), custom_call_target="tpu_custom_call" | custom-call | tf_op jit(solution)/shard_map/scan_ids/pallas_call | solution.py:458
  139.4 10.8 %project.2 = (bf16[3,1024,768]{2,1,0:T(8,128)(2,1)}, bf16[3,768,1024]{2,1,0:T(8,128)(2,1)}) custom-call(bf16[1024,768]{1,0:T(8,128)(2,1)} %fusion.11.x_ref, bf16[2,4,768,768]{3,2,1,0:T(8,128)(2,1)} %convert_element_type.203.weight_ref), custom_call_target="tpu_custom_call" | custom-call | flops 7247757312 | bytes 14548992 | tf_op jit(solution)/shard_map/project/pallas_call | solution.py:282
  151.8 19.2 %attend.2 = (bf16[768,1024]{1,0:T(8,128)(2,1)}, f32[6,8,1024]{2,1,0:T(8,128)}) custom-call(s32[8]{0:T(128)} %pad_add_fusion.3.window_ref, f32[12]{0:T(128)} %get-tuple-element.419.gate_ref, bf16[3,1024,768]{2,1,0:T(8,128)(2,1)} %get-tuple-element.166.k_ref.q_ref.v_ref, bf16[3,768,1024]{2,1,0:T(8,128)(2,1)} %get-tuple-element.167.qt_ref.vt_ref.kt_ref, ...), custom_call_target="tpu_custom_call" | custom-call | flops 3221225472 | bytes 6291456 | tf_op jit(solution)/shard_map/attend/pallas_call | solution.py:120
  179.3 26.0 %feed.2 = (bf16[1024,3072]{1,0:T(8,128)(2,1)}, bf16[1024,3072]{1,0:T(8,128)(2,1)}, f32[1024,768]{1,0:T(8,128)}) custom-call(bf16[1024,768]{1,0:T(8,128)(2,1)} %fusion.8.x_ref, bf16[2,3072,768]{2,1,0:T(8,128)(2,1)} %bitcast.450, bf16[2,3072,768]{2,1,0:T(8,128)(2,1)} %bitcast.451, f32[1,1,3072]{2,1,0:T(1,128)} %get-tuple-element.405.scale_ref), custom_call_target="tpu_custom_call" | custom-call | flops 9663676416 | bytes 26738688 | tf_op jit(solution)/shard_map/feed/pallas_call | solution.py:342
  212.4 10.8 %project.3 = (bf16[3,1024,768]{2,1,0:T(8,128)(2,1)}, bf16[3,768,1024]{2,1,0:T(8,128)(2,1)}) custom-call(bf16[1024,768]{1,0:T(8,128)(2,1)} %fusion.9.x_ref, bf16[2,4,768,768]{3,2,1,0:T(8,128)(2,1)} %convert_element_type.203.weight_ref), custom_call_target="tpu_custom_call" | custom-call | flops 7247757312 | bytes 14548992 | tf_op jit(solution)/shard_map/project/pallas_call | solution.py:282
  223.2 19.5 %attend.3 = (bf16[768,1024]{1,0:T(8,128)(2,1)}, f32[6,8,1024]{2,1,0:T(8,128)}) custom-call(s32[8]{0:T(128)} %pad_add_fusion.3.window_ref, f32[12]{0:T(128)} %get-tuple-element.418.gate_ref, bf16[3,1024,768]{2,1,0:T(8,128)(2,1)} %get-tuple-element.171.k_ref.q_ref.v_ref, bf16[3,768,1024]{2,1,0:T(8,128)(2,1)} %get-tuple-element.172.qt_ref.vt_ref.kt_ref, ...), custom_call_target="tpu_custom_call" | custom-call | flops 3221225472 | bytes 6291456 | tf_op jit(solution)/shard_map/attend/pallas_call | solution.py:120
  250.8 26.1 %feed.3 = (bf16[1024,3072]{1,0:T(8,128)(2,1)}, bf16[1024,3072]{1,0:T(8,128)(2,1)}, f32[1024,768]{1,0:T(8,128)}) custom-call(bf16[1024,768]{1,0:T(8,128)(2,1)} %fusion.10.x_ref, bf16[2,3072,768]{2,1,0:T(8,128)(2,1)} %all-gather.6.cloned.1.call-done.up_ref.down_ref, bf16[2,3072,768]{2,1,0:T(8,128)(2,1)} %all-gather.6.cloned.1.call-done.up_ref.down_ref, ...), custom_call_target="tpu_custom_call" | custom-call | flops 9663676416 | bytes 26738688 | tf_op jit(solution)/shard_map/feed/pallas_call | solution.py:342
  300.3 8.5 fusion.65
  334.1 7.3 fusion.68
  363.8 28.6 %feed_back.2 = (f32[1024,768]{1,0:T(8,128)}, bf16[8,2,384,768]{3,2,1,0:T(8,128)(2,1)}) custom-call(bf16[1024,768]{1,0:T(8,128)(2,1)} %get-tuple-element.309.grad_ref, bf16[1024,768]{1,0:T(8,128)(2,1)} %fusion.10.x_ref, bf16[1024,3072]{1,0:T(8,128)(2,1)} %get-tuple-element.186.act_ref, bf16[1024,3072]{1,0:T(8,128)(2,1)} %get-tuple-element.187.slope_ref, ...), custom_call_target="tpu_custom_call" | custom-call | flops 19327352832 | bytes 37748736 | tf_op jit(solution)/shard_map/feed_back/pallas_call | solution.py:405
  393.1 6.0 multiply_reduce_fusion.1
  410.6 30.6 %attend_back.2 = bf16[3,1024,768]{2,1,0:T(8,128)(2,1)} custom-call(s32[8]{0:T(128)} %pad_add_fusion.3.window_ref, bf16[3,1024,768]{2,1,0:T(8,128)(2,1)} %get-tuple-element.171.k_ref.q_ref.v_ref, bf16[3,768,1024]{2,1,0:T(8,128)(2,1)} %get-tuple-element.172.qt_ref.vt_ref.kt_ref, bf16[3,1024,768]{2,1,0:T(8,128)(2,1)} %get-tuple-element.171.k_ref.q_ref.v_ref, ...), custom_call_target="tpu_custom_call" | custom-call | flops 8053063680 | bytes 15728640 | tf_op jit(solution)/shard_map/attend_back/pallas_call | solution.py:223
  441.2 8.3 bitcast_add_fusion.1
  465.1 28.8 %feed_back.3 = (f32[1024,768]{1,0:T(8,128)}, bf16[8,2,384,768]{3,2,1,0:T(8,128)(2,1)}) custom-call(bf16[1024,768]{1,0:T(8,128)(2,1)} %get-tuple-element.193.grad_ref, bf16[1024,768]{1,0:T(8,128)(2,1)} %fusion.8.x_ref, bf16[1024,3072]{1,0:T(8,128)(2,1)} %get-tuple-element.194.act_ref, bf16[1024,3072]{1,0:T(8,128)(2,1)} %get-tuple-element.195.slope_ref, ...), custom_call_target="tpu_custom_call" | custom-call | flops 19327352832 | bytes 37748736 | tf_op jit(solution)/shard_map/feed_back/pallas_call | solution.py:405
  518.0 30.6 %attend_back.3 = bf16[3,1024,768]{2,1,0:T(8,128)(2,1)} custom-call(s32[8]{0:T(128)} %pad_add_fusion.3.window_ref, bf16[3,1024,768]{2,1,0:T(8,128)(2,1)} %get-tuple-element.166.k_ref.q_ref.v_ref, bf16[3,768,1024]{2,1,0:T(8,128)(2,1)} %get-tuple-element.167.qt_ref.vt_ref.kt_ref, bf16[3,1024,768]{2,1,0:T(8,128)(2,1)} %get-tuple-element.166.k_ref.q_ref.v_ref, ...), custom_call_target="tpu_custom_call" | custom-call | flops 8053063680 | bytes 15728640 | tf_op jit(solution)/shard_map/attend_back/pallas_call | solution.py:223
  553.2 6.1 bitcast_add_fusion
  572.0 6.2 fusion.69.begin
  590.7 32.3 %collective-permute-done.27.rest_1_ = bf16[1024,768]{1,0:T(8,128)(2,1)} collective-permute-done((bf16[1024,768]{1,0:T(8,128)(2,1)}, bf16[1024,768]{1,0:T(8,128)(2,1)}, u32[]{:S(2)}, u32[]{:S(2)}) %collective-permute-start.27) | collective-permute-done | bytes 1572896 | tf_op jit(solution)/shard_map/ppermute | solution.py:792
  635.0 7.4 collective-permute-done.38
  661.0 6.9 collective-permute-done.32.rest_3_
  687.4 27.0 %spread.1 = bf16[3840,768]{1,0:T(8,128)(2,1)} custom-call(s32[4096]{0:T(1024)} %pad_add_fusion.ids, s32[4096]{0:T(1024)} %copy-done.61, s32[2]{0:T(128)} %pad_add_fusion.1.place, s32[4096]{0:T(1024)} %get-tuple-element.148.found, s32[8]{0:T(128)} %get-tuple-element.149.ends, s32[4096]{0:T(1024)} %get-tuple-element.156.other_found, ...), custom_call_target="tpu_custom_call" | custom-call | bytes 30277632 | tf_op jit(solution)/shard_map/spread/pallas_call | solution.py:606
  728.8 255.6 %all-reduce.4.cloned.1.call-done = (bf16[3840,768]{1,0:T(8,128)(2,1)}, bf16[4,96,768]{2,1,0:T(8,128)(2,1)}, bf16[2,384,768]{2,1,0:T(8,128)(2,1)}) async-done(((bf16[3840,768]{1,0:T(8,128)(2,1)}, bf16[4,96,768]{2,1,0:T(8,128)(2,1)}, bf16[2,384,768]{2,1,0:T(8,128)(2,1)}), (bf16[3840,768]{1,0:T(8,128)(2,1)}, bf16[4,96,768]{2,1,0:T(8,128)(2,1)}, bf16[2,384,768]{2,1,0:T(8,128)(2,1)})) %all-reduce.4.cloned.1.call-update) | async-done | bytes 7667728 | tf_op jit(solution)/shard_map/psum | solution.py:1206
  984.3 7.2 stats.1
  991.5 12.2 %all-gather.2.parts_ref = f32[8,26,768]{2,1,0:T(8,128)} all-gather(f32[1,26,768]{2,1,0:T(8,128)} %bitcast.412), channel_id=3, replica_groups=mesh['dp'=4,'unit'=8] {'unit'}, dimensions={0}, use_global_device_ids=true | all-gather | bytes 718848 | tf_op jit(solution)/shard_map/all_gather | solution.py:1240
  1012.9 16.6 %renew.4 = (f32[1,3840,768]{2,1,0:T(8,128)}, f32[1,3840,768]{2,1,0:T(8,128)}, f32[1,6,1,640]{3,2,1,0:T(1,128)}) custom-call(f32[3]{0:T(128)} %get-tuple-element.240.scalars_ref, s32[1]{0:T(128)} %constant.213.clone.1.at_ref, f32[14,1,768]{2,1,0:T(1,128)} %broadcast_in_dim.65.factor_ref, f32[1,3840,1]{2,1,0:T(8,128)} %broadcast_in_dim_broadcast_in_dim.8.rows_ref, ...), custom_call_target="tpu_custom_call" | custom-call | tf_op jit(solution)/shard_map/renew/pallas_call | solution.py:760
  1032.7 7.9 renew.6
  (522 shorter events, 302.3 us)
Async XLA Ops:
  7.2 172.1 %all-gather.8.cloned.1.call-start = ((), (), s32[]{:S(2)}) async-start(), calls=%async_computation.7 | async-start | bytes 10616832 | tf_op jit(solution)/shard_map/all_gather | solution.py:982
  11.4 239.4 %all-gather.6.cloned.1.call-start = ((), (), s32[]{:S(2)}) async-start(), calls=%async_computation.3 | async-start | bytes 10616832 | tf_op jit(solution)/shard_map/all_gather | solution.py:982
  11.5 21.1 %collective-permute-start.4 = (f32[3840,768]{1,0:T(8,128)}, f32[3840,768]{1,0:T(8,128)}, u32[]{:S(2)}, u32[]{:S(2)}) collective-permute-start(f32[3840,768]{1,0:T(8,128)} %own.1), channel_id=1, source_target_pairs={{0,1},{1,0},{2,3},{3,2},{4,5},{5,4},{6,7},{7,6},{8,9},{9,8},{10,11... | collective-permute-start | bytes 35389448 | tf_op jit(solution)/shard_map/ppermute | solution.py:796
  51.6 37.1 %collective-permute-start.5 = (bf16[512,768]{1,0:T(8,128)(2,1)}, bf16[512,768]{1,0:T(8,128)(2,1)S(1)}, u32[]{:S(2)}, u32[]{:S(2)}) collective-permute-start(bf16[512,768]{1,0:T(8,128)(2,1)} %get-tuple-element.142), channel_id=1, source_target_pairs={{0,4},{1,5},{2,6},{3,7},{4,0},{5,1},{6,2},{7,3},{8,12},{9,13},{10,... | collective-permute-start | bytes 2359304 | tf_op jit(solution)/shard_map/ppermute | solution.py:792
  51.7 37.0 %collective-permute-start.6 = (bf16[512,768]{1,0:T(8,128)(2,1)}, bf16[512,768]{1,0:T(8,128)(2,1)S(1)}, u32[]{:S(2)}, u32[]{:S(2)}) collective-permute-start(bf16[512,768]{1,0:T(8,128)(2,1)} %get-tuple-element.143), channel_id=1, source_target_pairs={{0,2},{1,3},{2,0},{3,1},{4,6},{5,7},{6,4},{7,5},{8,10},{9,11},{10,... | collective-permute-start | bytes 2359304 | tf_op jit(solution)/shard_map/ppermute | solution.py:792
  51.8 53.0 %collective-permute-start.7 = (bf16[512,768]{1,0:T(8,128)(2,1)}, bf16[512,768]{1,0:T(8,128)(2,1)}, u32[]{:S(2)}, u32[]{:S(2)}) collective-permute-start(bf16[512,768]{1,0:T(8,128)(2,1)} %get-tuple-element.144), channel_id=1, source_target_pairs={{0,4},{1,5},{2,6},{3,7},{4,0},{5,1},{6,2},{7,3},{8,12},{9,13},{10,... | collective-permute-start | bytes 2359304 | tf_op jit(solution)/shard_map/ppermute | solution.py:792
  53.7 51.1 %collective-permute-start.8 = (bf16[512,768]{1,0:T(8,128)(2,1)}, bf16[512,768]{1,0:T(8,128)(2,1)}, u32[]{:S(2)}, u32[]{:S(2)}) collective-permute-start(bf16[512,768]{1,0:T(8,128)(2,1)} %get-tuple-element.145), channel_id=1, source_target_pairs={{0,2},{1,3},{2,0},{3,1},{4,6},{5,7},{6,4},{7,5},{8,10},{9,11},{10,... | collective-permute-start | bytes 2359304 | tf_op jit(solution)/shard_map/ppermute | solution.py:792
  105.9 19.3 %collective-permute-start.9 = (bf16[512,768]{1,0:T(8,128)(2,1)}, bf16[512,768]{1,0:T(8,128)(2,1)S(1)}, u32[]{:S(2)}, u32[]{:S(2)}) collective-permute-start(bf16[512,768]{1,0:T(8,128)(2,1)} %add.383), channel_id=1, source_target_pairs={{0,2},{1,3},{2,0},{3,1},{4,6},{5,7},{6,4},{7,5},{8,10},{9,11},{10,... | collective-permute-start | bytes 2359304 | tf_op jit(solution)/shard_map/ppermute | solution.py:792
  107.5 19.1 %collective-permute-start.10 = (bf16[512,768]{1,0:T(8,128)(2,1)S(1)}, bf16[512,768]{1,0:T(8,128)(2,1)S(1)}, u32[]{:S(2)}, u32[]{:S(2)}) collective-permute-start(bf16[512,768]{1,0:T(8,128)(2,1)S(1)} %add.384), channel_id=1, source_target_pairs={{0,4},{1,5},{2,6},{3,7},{4,0},{5,1},{6,2},{7,3},{8,12},{9,13},{10,... | collective-permute-start | bytes 2359304 | tf_op jit(solution)/shard_map/ppermute | solution.py:792
  129.4 365.4 %reduce-scatter.4.cloned.1.call-start = ((), (), s32[]{:S(2)}) async-start(), calls=%async_computation.4 | async-start | bytes 10616832 | tf_op jit(solution)/shard_map/reduce_scatter | solution.py:1114
  129.4 76.0 %collective-permute-start.11 = (bf16[1024,768]{1,0:T(8,128)(2,1)}, bf16[1024,768]{1,0:T(8,128)(2,1)}, u32[]{:S(2)}, u32[]{:S(2)}) collective-permute-start(bf16[1024,768]{1,0:T(8,128)(2,1)} %bitcast.458), channel_id=1, source_target_pairs={{0,4},{1,5},{2,6},{3,7},{4,0},{5,1},{6,2},{7,3},{8,12},{9,13},{10,... | collective-permute-start | bytes 4718600 | tf_op jit(solution)/shard_map/ppermute | solution.py:983
  392.4 192.4 %reduce-scatter.6.cloned.1.call-start = ((), (), s32[]{:S(2)}) async-start(), calls=%async_computation.5 | async-start | bytes 6635520 | tf_op jit(solution)/shard_map/reduce_scatter | solution.py:1107
  465.0 252.2 %reduce-scatter.8.cloned.1.call-start = ((), (), s32[]{:S(2)}) async-start(), calls=%async_computation.6 | async-start | bytes 10616832 | tf_op jit(solution)/shard_map/reduce_scatter | solution.py:1114
  494.0 490.3 %all-reduce.4.cloned.1.call-start = ((), (), s32[]{:S(2)}) async-start(), calls=%async_computation.8 | async-start | bytes 15335424 | tf_op jit(solution)/shard_map/psum | solution.py:1206
  497.1 53.0 %collective-permute-start.24 = (bf16[192,768]{1,0:T(8,128)(2,1)}, bf16[192,768]{1,0:T(8,128)(2,1)S(1)}, u32[]{:S(2)}, u32[]{:S(2)}) collective-permute-start(bf16[192,768]{1,0:T(8,128)(2,1)} %get-tuple-element.329), channel_id=1, source_target_pairs={{0,8},{8,16},{16,24},{24,0},{1,9},{9,17},{17,25},{25,1},{2,10},{10... | collective-permute-start | bytes 884744 | tf_op jit(solution)/shard_map/ppermute | solution.py:816
  497.5 52.5 %collective-permute-start.25 = (bf16[192,768]{1,0:T(8,128)(2,1)}, bf16[192,768]{1,0:T(8,128)(2,1)S(1)}, u32[]{:S(2)}, u32[]{:S(2)}) collective-permute-start(bf16[192,768]{1,0:T(8,128)(2,1)} %get-tuple-element.328), channel_id=1, source_target_pairs={{0,16},{8,24},{16,0},{24,8},{1,17},{9,25},{17,1},{25,9},{2,18},{10... | collective-permute-start | bytes 884744 | tf_op jit(solution)/shard_map/ppermute | solution.py:816
  501.0 49.1 %collective-permute-start.26 = (bf16[192,768]{1,0:T(8,128)(2,1)}, bf16[192,768]{1,0:T(8,128)(2,1)}, u32[]{:S(2)}, u32[]{:S(2)}) collective-permute-start(bf16[192,768]{1,0:T(8,128)(2,1)} %get-tuple-element.327), channel_id=1, source_target_pairs={{0,24},{8,0},{16,8},{24,16},{1,25},{9,1},{17,9},{25,17},{2,26},{10... | collective-permute-start | bytes 884744 | tf_op jit(solution)/shard_map/ppermute | solution.py:816
  563.9 59.2 %collective-permute-start.27 = (bf16[1024,768]{1,0:T(8,128)(2,1)}, bf16[1024,768]{1,0:T(8,128)(2,1)}, u32[]{:S(2)}, u32[]{:S(2)}) collective-permute-start(bf16[1024,768]{1,0:T(8,128)(2,1)} %multiply_convert_fusion.rest_0_), channel_id=1, source_target_pairs={{0,2},{1,3},{2,0},{3,1},{4,6},{5,7},{6,4},{7,5},{8,10},{9,11},{10,... | collective-permute-start | bytes 4718600 | tf_op jit(solution)/shard_map/ppermute | solution.py:792
  564.4 58.7 %collective-permute-start.28 = (bf16[1024,768]{1,0:T(8,128)(2,1)}, bf16[1024,768]{1,0:T(8,128)(2,1)}, u32[]{:S(2)}, u32[]{:S(2)}) collective-permute-start(bf16[1024,768]{1,0:T(8,128)(2,1)} %multiply_convert_fusion.rest_0_), channel_id=1, source_target_pairs={{0,4},{1,5},{2,6},{3,7},{4,0},{5,1},{6,2},{7,3},{8,12},{9,13},{10,... | collective-permute-start | bytes 4718600 | tf_op jit(solution)/shard_map/ppermute | solution.py:792
  569.4 21.3 %collective-permute-start.30 = (bf16[192,768]{1,0:T(8,128)(2,1)S(1)}, bf16[192,768]{1,0:T(8,128)(2,1)S(1)}, u32[]{:S(2)}, u32[]{:S(2)}) collective-permute-start(bf16[192,768]{1,0:T(8,128)(2,1)S(1)} %add_convert_fusion.1), channel_id=1, source_target_pairs={{0,16},{8,24},{16,0},{24,8},{1,17},{9,25},{17,1},{25,9},{2,18},{10... | collective-permute-start | bytes 884744 | tf_op jit(solution)/shard_map/ppermute | solution.py:828
  570.7 20.0 %collective-permute-start.31 = (bf16[192,768]{1,0:T(8,128)(2,1)S(1)}, bf16[192,768]{1,0:T(8,128)(2,1)S(1)}, u32[]{:S(2)}, u32[]{:S(2)}) collective-permute-start(bf16[192,768]{1,0:T(8,128)(2,1)S(1)} %add_convert_fusion.1), channel_id=1, source_target_pairs={{0,24},{8,0},{16,8},{24,16},{1,25},{9,1},{17,9},{25,17},{2,26},{10... | collective-permute-start | bytes 884744 | tf_op jit(solution)/shard_map/ppermute | solution.py:828
  623.1 27.3 %collective-permute-start.36 = (bf16[4,4,96,768]{3,2,1,0:T(8,128)(2,1)}, bf16[4,4,96,768]{3,2,1,0:T(8,128)(2,1)}, u32[]{:S(2)}, u32[]{:S(2)}) collective-permute-start(bf16[4,4,96,768]{3,2,1,0:T(8,128)(2,1)} %bitcast.400), channel_id=1, source_target_pairs={{0,1},{1,0},{2,3},{3,2},{4,5},{5,4},{6,7},{7,6},{8,9},{9,8},{10,11... | collective-permute-start | bytes 7077896 | tf_op jit(solution)/shard_map/ppermute | solution.py:796
  623.1 45.8 %collective-permute-start.34 = (bf16[1024,768]{1,0:T(8,128)(2,1)}, bf16[1024,768]{1,0:T(8,128)(2,1)}, u32[]{:S(2)}, u32[]{:S(2)}) collective-permute-start(bf16[1024,768]{1,0:T(8,128)(2,1)} %collective-permute-done.27.rest_1_), channel_id=1, source_target_pairs={{0,1},{1,0},{2,3},{3,2},{4,5},{5,4},{6,7},{7,6},{8,9},{9,8},{10,11... | collective-permute-start | bytes 4718600 | tf_op jit(solution)/shard_map/ppermute | solution.py:796
  623.6 45.3 %collective-permute-start.35 = (bf16[1024,768]{1,0:T(8,128)(2,1)}, bf16[1024,768]{1,0:T(8,128)(2,1)}, u32[]{:S(2)}, u32[]{:S(2)}) collective-permute-start(bf16[1024,768]{1,0:T(8,128)(2,1)} %collective-permute-done.28.rest_2_), channel_id=1, source_target_pairs={{0,1},{1,0},{2,3},{3,2},{4,5},{5,4},{6,7},{7,6},{8,9},{9,8},{10,11... | collective-permute-start | bytes 4718600 | tf_op jit(solution)/shard_map/ppermute | solution.py:796
  635.0 47.0 %collective-permute-start.40 = (bf16[1024,768]{1,0:T(8,128)(2,1)}, bf16[1024,768]{1,0:T(8,128)(2,1)}, u32[]{:S(2)}, u32[]{:S(2)}) collective-permute-start(bf16[1024,768]{1,0:T(8,128)(2,1)} %multiply_convert_fusion.rest_0_), channel_id=1, source_target_pairs={{0,1},{1,0},{2,3},{3,2},{4,5},{5,4},{6,7},{7,6},{8,9},{9,8},{10,11... | collective-permute-start | bytes 4718600 | tf_op jit(solution)/shard_map/ppermute | solution.py:796
  649.0 19.0 %collective-permute-start.32 = (bf16[512,768]{1,0:T(8,128)(2,1)}, bf16[512,768]{1,0:T(8,128)(2,1)}, u32[]{:S(2)}, u32[]{:S(2)}) collective-permute-start(bf16[512,768]{1,0:T(8,128)(2,1)} %slice.474), channel_id=1, source_target_pairs={{0,4},{1,5},{2,6},{3,7},{4,0},{5,1},{6,2},{7,3},{8,12},{9,13},{10,... | collective-permute-start | bytes 2359304 | tf_op jit(solution)/shard_map/ppermute | solution.py:792
  650.4 18.5 %collective-permute-start.33 = (bf16[512,768]{1,0:T(8,128)(2,1)S(1)}, bf16[512,768]{1,0:T(8,128)(2,1)}, u32[]{:S(2)}, u32[]{:S(2)}) collective-permute-start(bf16[512,768]{1,0:T(8,128)(2,1)S(1)} %slice.475), channel_id=1, source_target_pairs={{0,2},{1,3},{2,0},{3,1},{4,6},{5,7},{6,4},{7,5},{8,10},{9,11},{10,... | collective-permute-start | bytes 2359304 | tf_op jit(solution)/shard_map/ppermute | solution.py:792
  681.3 33.2 %collective-permute-start.43 = (bf16[4,96,768]{2,1,0:T(8,128)(2,1)}, bf16[4,96,768]{2,1,0:T(8,128)(2,1)}, u32[]{:S(2)}, u32[]{:S(2)}) collective-permute-start(bf16[4,96,768]{2,1,0:T(8,128)(2,1)} %get-tuple-element.324), channel_id=1, source_target_pairs={{0,2},{1,3},{2,0},{3,1},{4,6},{5,7},{6,4},{7,5},{8,10},{9,11},{10,... | collective-permute-start | bytes 1769480 | tf_op jit(solution)/shard_map/ppermute | solution.py:792
  681.9 32.6 %collective-permute-start.44 = (bf16[4,96,768]{2,1,0:T(8,128)(2,1)}, bf16[4,96,768]{2,1,0:T(8,128)(2,1)}, u32[]{:S(2)}, u32[]{:S(2)}) collective-permute-start(bf16[4,96,768]{2,1,0:T(8,128)(2,1)} %get-tuple-element.323), channel_id=1, source_target_pairs={{0,4},{1,5},{2,6},{3,7},{4,0},{5,1},{6,2},{7,3},{8,12},{9,13},{10,... | collective-permute-start | bytes 1769480 | tf_op jit(solution)/shard_map/ppermute | solution.py:792
  683.4 31.1 %collective-permute-start.45 = (bf16[4,96,768]{2,1,0:T(8,128)(2,1)S(1)}, bf16[4,96,768]{2,1,0:T(8,128)(2,1)}, u32[]{:S(2)}, u32[]{:S(2)}) collective-permute-start(bf16[4,96,768]{2,1,0:T(8,128)(2,1)S(1)} %get-tuple-element.322), channel_id=1, source_target_pairs={{0,6},{1,7},{2,4},{3,5},{4,2},{5,3},{6,0},{7,1},{8,14},{9,15},{10,... | collective-permute-start | bytes 1769480 | tf_op jit(solution)/shard_map/ppermute | solution.py:792
  684.8 29.6 %collective-permute-start.49 = (bf16[120,768]{1,0:T(8,128)(2,1)S(1)}, bf16[120,768]{1,0:T(8,128)(2,1)S(1)}, u32[]{:S(2)}, u32[]{:S(2)}) collective-permute-start(bf16[120,768]{1,0:T(8,128)(2,1)S(1)} %add_convert_fusion.2), channel_id=1, source_target_pairs={{0,16},{8,24},{16,0},{24,8},{1,17},{9,25},{17,1},{25,9},{2,18},{10... | collective-permute-start | bytes 552968 | tf_op jit(solution)/shard_map/ppermute | solution.py:828
  684.8 29.6 %collective-permute-start.50 = (bf16[120,768]{1,0:T(8,128)(2,1)S(1)}, bf16[120,768]{1,0:T(8,128)(2,1)S(1)}, u32[]{:S(2)}, u32[]{:S(2)}) collective-permute-start(bf16[120,768]{1,0:T(8,128)(2,1)S(1)} %add_convert_fusion.2), channel_id=1, source_target_pairs={{0,24},{8,0},{16,8},{24,16},{1,25},{9,1},{17,9},{25,17},{2,26},{10... | collective-permute-start | bytes 552968 | tf_op jit(solution)/shard_map/ppermute | solution.py:828
  (129 other events, 2439.8 us)
Sparse Core Ops, SparseCore 0:
  11.5 78.9 all-gather.7
  129.5 75.1 all-gather.5
  392.6 76.8 reduce-scatter.3
  472.8 59.6 reduce-scatter.5
  535.9 101.1 reduce-scatter.7
  717.5 266.7 all-reduce.3

commit v3 on v2

--- a/solution.py
+++ b/solution.py
@@ -1170,25 +1170,22 @@
     crossed = [(other, 0), (other, ROW_BLOCK)]
     if chips == 4 and length == 2 * ROW_BLOCK:
         near = [across(sent, 1), across(sent, 2)]
-        near, later_feeds, later_attn, grad_table, attn_theirs = together(
-            near, later_feeds, attn_parts[1:], grad_table, attn_theirs
+        later_feeds, later_attn = together(later_feeds, attn_parts[1:])
+        later_attn = [dp_scatter(part.reshape(-1, breadth)) for part in later_attn]
+        near, later_attn, grad_table, attn_theirs = together(
+            near, later_attn, grad_table, attn_theirs
         )
         last = [across(near[0][:ROW_BLOCK], 2), across(near[1][ROW_BLOCK:], 1)]
         near_other = [swapped(part) for part in near]
         attn_chip = chip_sum(attn_mine, swapped(attn_theirs))
-        later_attn = [dp_scatter(part.reshape(-1, breadth)) for part in later_attn]
-        last, near_other, attn_chip, later_attn = together(
-            last, near_other, attn_chip, later_attn
-        )
-        small = dp_sum(small)
+        later_attn = [dp_gather(part) for part in later_attn]
+        last, near_other, attn_chip = together(last, near_other, attn_chip)
+        last_other = [swapped(part) for part in last]
         attn_received = sent_to_owners(attn_chip, chip, range(1, chips))
-        last_other = [swapped(part) for part in last]
         for home, parts, ends in ((same, near, last), (crossed, near_other, last_other)):
             home += [(part, at) for part in parts for at in (0, ROW_BLOCK)]
             home += [(part, 0) for part in ends]
-        later_attn = [dp_gather(part) for part in later_attn]
     else:
-        small = dp_sum(small)
         later_attn = [
             dp_gather(dp_scatter(part.reshape(-1, breadth))) for part in attn_parts[1:]
         ]
@@ -1199,9 +1196,8 @@
             for home, part in ((same, part), (crossed, swapped(part))):
                 home += [(part, at) for at in range(0, length, ROW_BLOCK)]
     embed_part = spread(all_ids, other_ids, own_place, lists, grad_table, same + crossed)
-    embed_part, attn_received, small, later_attn = together(
-        embed_part, attn_received, small, later_attn
-    )
+    embed_part, attn_received, later_attn = together(embed_part, attn_received, later_attn)
+    small = dp_sum(small)
     attn_parts[0] = owner_total(attn_chip, attn_received, chip)
     embed_sum, feed_first, attn_first = lax.psum((embed_part, feed_parts[0], attn_parts[0]), "dp")
     attn_sums = [attn_first] + [

time: 1070 us -> 1050 us (0.981)
  waiting for transfers between devices: 366 us -> 345 us
  transfers between devices with their start and end apart: 57 -> 57, of which waited for: 25 -> 28; matrix products, arithmetic and copies ran while one was open for 17% -> 17% of each run, Pallas kernels for 25% -> 25%
where the time goes in v3:
time: 1050 us; the launch traced here: 1040 us
  Pallas kernels  353 us (34%)
  waiting for transfers between devices  345 us (33%)
  other arithmetic  117 us (11%)
  matrix products  85.7 us (8%)
  starting transfers between devices  61.1 us (6%)
  local copies, waits for them, and re-layouts  44 us (4%)
  between operations  19.3 us (2%)
  blocking collectives  12.3 us (1%)
    psum x1, waiting for transfers between devices, local(): lax.psum((embed_part, feed_parts[0], attn_parts[0]), 'dp')  245 us
    ppermute x25, waiting for transfers between devices, across(): return lax.ppermute(value, 'unit', pairs)  74.8 us
    pallas_call x2, Pallas kernels, attend_back(): pl.pallas_call(functools.partial(attend_back_kernel, block=QUERY_BLOCK, s...  61.2 us
    pallas_call x2, Pallas kernels, feed_back(): pl.pallas_call(feed_back_kernel, grid=(units // block,), in_specs=[whole,...  57.5 us
    pallas_call x2, Pallas kernels, feed(): pl.pallas_call(feed_kernel, grid=(units // block,), in_specs=[pl.BlockSpe...  52.1 us
    pallas_call x2, Pallas kernels, attend(): pl.pallas_call(functools.partial(attend_kernel, block=QUERY_BLOCK), grid_...  39.2 us
    dot_general x8, matrix products, contract(): return lax.dot_general(left, right, dims, preferred_element_type=F)  38.4 us
    pallas_call x3, Pallas kernels, scan_ids(): pl.pallas_call(functools.partial(scan_kernel, vocab=vocab), in_specs=[sme...  36.9 us
  transfers between devices with their start and end apart: 57, of which 28 were waited for; matrix products, arithmetic and copies ran while one was open for 17% of the time, Pallas kernels for 25%

profile of v3, /device:TPU:0, one launch (start us, length us, event | category | flops | bytes accessed | tf_op | source)
XLA Modules:
  0.0 1037.8 jit_solution(3959393926815143981)
XLA Ops:
  20.3 12.3 %scan_ids.3 = (s32[4096]{0:T(1024)}, s32[8]{0:T(128)}) custom-call(s32[4096]{0:T(1024)} %pad_add_fusion.ids, s32[2]{0:T(128)} %pad_add_fusion.1.place), custom_call_target="tpu_custom_call" | custom-call | tf_op jit(solution)/shard_map/scan_ids/pallas_call | solution.py:458
  32.6 16.3 %lookup.1 = (bf16[512,768]{1,0:T(8,128)(2,1)}, bf16[512,768]{1,0:T(8,128)(2,1)}, bf16[512,768]{1,0:T(8,128)(2,1)}, bf16[512,768]{1,0:T(8,128)(2,1)}, bf16[512,76...) custom-call(s32[4096]{0:T(1024)} %pad_add_fusion.ids, ...), custom_call_target="tpu_custom_call" | custom-call | bytes 29884416 | tf_op jit(solution)/shard_map/lookup/pallas_call | solution.py:522
  53.7 7.4 convert_element_type.203
  61.1 9.9 convert_element_type.204.weight_ref
  73.0 12.3 %scan_ids.4 = (s32[4096]{0:T(1024)}, s32[8]{0:T(128)}) custom-call(s32[4096]{0:T(1024)} %pad_add_fusion.ids, s32[2]{0:T(128)} %pad_add_fusion.2.place), custom_call_target="tpu_custom_call" | custom-call | tf_op jit(solution)/shard_map/scan_ids/pallas_call | solution.py:458
  88.2 16.6 %collective-permute-done.6 = bf16[512,768]{1,0:T(8,128)(2,1)} collective-permute-done((bf16[512,768]{1,0:T(8,128)(2,1)}, bf16[512,768]{1,0:T(8,128)(2,1)}, u32[]{:S(2)}, u32[]{:S(2)}) %collective-permute-start.6) | collective-permute-done | bytes 786464 | tf_op jit(solution)/shard_map/ppermute | solution.py:792
  110.0 12.3 %scan_ids.5 = (s32[4096]{0:T(1024)}, s32[8]{0:T(128)}) custom-call(s32[4096]{0:T(1024)} %copy-done.49, s32[2]{0:T(128)} %pad_add_fusion.2.place), custom_call_target="tpu_custom_call" | custom-call | tf_op jit(solution)/shard_map/scan_ids/pallas_call | solution.py:458
  139.3 10.8 %project.2 = (bf16[3,1024,768]{2,1,0:T(8,128)(2,1)}, bf16[3,768,1024]{2,1,0:T(8,128)(2,1)}) custom-call(bf16[1024,768]{1,0:T(8,128)(2,1)} %fusion.11.x_ref, bf16[2,4,768,768]{3,2,1,0:T(8,128)(2,1)} %convert_element_type.204.weight_ref), custom_call_target="tpu_custom_call" | custom-call | flops 7247757312 | bytes 14548992 | tf_op jit(solution)/shard_map/project/pallas_call | solution.py:282
  151.7 19.4 %attend.2 = (bf16[768,1024]{1,0:T(8,128)(2,1)}, f32[6,8,1024]{2,1,0:T(8,128)}) custom-call(s32[8]{0:T(128)} %pad_add_fusion.3.window_ref, f32[12]{0:T(128)} %get-tuple-element.417.gate_ref, bf16[3,1024,768]{2,1,0:T(8,128)(2,1)} %get-tuple-element.161.k_ref.q_ref.v_ref, bf16[3,768,1024]{2,1,0:T(8,128)(2,1)} %get-tuple-element.162.qt_ref.vt_ref.kt_ref, ...), custom_call_target="tpu_custom_call" | custom-call | flops 3221225472 | bytes 6291456 | tf_op jit(solution)/shard_map/attend/pallas_call | solution.py:120
  179.6 26.0 %feed.2 = (bf16[1024,3072]{1,0:T(8,128)(2,1)}, bf16[1024,3072]{1,0:T(8,128)(2,1)}, f32[1024,768]{1,0:T(8,128)}) custom-call(bf16[1024,768]{1,0:T(8,128)(2,1)} %fusion.8.x_ref, bf16[2,3072,768]{2,1,0:T(8,128)(2,1)} %bitcast.450, bf16[2,3072,768]{2,1,0:T(8,128)(2,1)} %bitcast.451, f32[1,1,3072]{2,1,0:T(1,128)} %get-tuple-element.403.scale_ref), custom_call_target="tpu_custom_call" | custom-call | flops 9663676416 | bytes 26738688 | tf_op jit(solution)/shard_map/feed/pallas_call | solution.py:342
  212.7 10.8 %project.3 = (bf16[3,1024,768]{2,1,0:T(8,128)(2,1)}, bf16[3,768,1024]{2,1,0:T(8,128)(2,1)}) custom-call(bf16[1024,768]{1,0:T(8,128)(2,1)} %fusion.9.x_ref, bf16[2,4,768,768]{3,2,1,0:T(8,128)(2,1)} %convert_element_type.204.weight_ref), custom_call_target="tpu_custom_call" | custom-call | flops 7247757312 | bytes 14548992 | tf_op jit(solution)/shard_map/project/pallas_call | solution.py:282
  223.4 19.8 %attend.3 = (bf16[768,1024]{1,0:T(8,128)(2,1)}, f32[6,8,1024]{2,1,0:T(8,128)}) custom-call(s32[8]{0:T(128)} %pad_add_fusion.3.window_ref, f32[12]{0:T(128)} %get-tuple-element.416.gate_ref, bf16[3,1024,768]{2,1,0:T(8,128)(2,1)} %get-tuple-element.166.k_ref.q_ref.v_ref, bf16[3,768,1024]{2,1,0:T(8,128)(2,1)} %get-tuple-element.167.qt_ref.vt_ref.kt_ref, ...), custom_call_target="tpu_custom_call" | custom-call | flops 3221225472 | bytes 6291456 | tf_op jit(solution)/shard_map/attend/pallas_call | solution.py:120
  251.2 26.1 %feed.3 = (bf16[1024,3072]{1,0:T(8,128)(2,1)}, bf16[1024,3072]{1,0:T(8,128)(2,1)}, f32[1024,768]{1,0:T(8,128)}) custom-call(bf16[1024,768]{1,0:T(8,128)(2,1)} %fusion.10.x_ref, bf16[2,3072,768]{2,1,0:T(8,128)(2,1)} %all-gather.6.cloned.1.call-done.up_ref.down_ref, bf16[2,3072,768]{2,1,0:T(8,128)(2,1)} %all-gather.6.cloned.1.call-done.up_ref.down_ref, ...), custom_call_target="tpu_custom_call" | custom-call | flops 9663676416 | bytes 26738688 | tf_op jit(solution)/shard_map/feed/pallas_call | solution.py:342
  300.6 8.5 fusion.65
  334.6 7.3 fusion.68
  364.3 28.6 %feed_back.2 = (f32[1024,768]{1,0:T(8,128)}, bf16[8,2,384,768]{3,2,1,0:T(8,128)(2,1)}) custom-call(bf16[1024,768]{1,0:T(8,128)(2,1)} %get-tuple-element.307.grad_ref, bf16[1024,768]{1,0:T(8,128)(2,1)} %fusion.10.x_ref, bf16[1024,3072]{1,0:T(8,128)(2,1)} %get-tuple-element.181.act_ref, bf16[1024,3072]{1,0:T(8,128)(2,1)} %get-tuple-element.182.slope_ref, ...), custom_call_target="tpu_custom_call" | custom-call | flops 19327352832 | bytes 37748736 | tf_op jit(solution)/shard_map/feed_back/pallas_call | solution.py:405
  393.7 6.0 multiply_reduce_fusion.2
  411.2 30.5 %attend_back.2 = bf16[3,1024,768]{2,1,0:T(8,128)(2,1)} custom-call(s32[8]{0:T(128)} %pad_add_fusion.3.window_ref, bf16[3,1024,768]{2,1,0:T(8,128)(2,1)} %get-tuple-element.166.k_ref.q_ref.v_ref, bf16[3,768,1024]{2,1,0:T(8,128)(2,1)} %get-tuple-element.167.qt_ref.vt_ref.kt_ref, bf16[3,1024,768]{2,1,0:T(8,128)(2,1)} %get-tuple-element.166.k_ref.q_ref.v_ref, ...), custom_call_target="tpu_custom_call" | custom-call | flops 8053063680 | bytes 15728640 | tf_op jit(solution)/shard_map/attend_back/pallas_call | solution.py:223
  441.7 8.3 bitcast_add_fusion.1
  465.2 28.9 %feed_back.3 = (f32[1024,768]{1,0:T(8,128)}, bf16[8,2,384,768]{3,2,1,0:T(8,128)(2,1)}) custom-call(bf16[1024,768]{1,0:T(8,128)(2,1)} %get-tuple-element.188.grad_ref, bf16[1024,768]{1,0:T(8,128)(2,1)} %fusion.8.x_ref, bf16[1024,3072]{1,0:T(8,128)(2,1)} %get-tuple-element.189.act_ref, bf16[1024,3072]{1,0:T(8,128)(2,1)} %get-tuple-element.190.slope_ref, ...), custom_call_target="tpu_custom_call" | custom-call | flops 19327352832 | bytes 37748736 | tf_op jit(solution)/shard_map/feed_back/pallas_call | solution.py:405
  518.1 30.7 %attend_back.3 = bf16[3,1024,768]{2,1,0:T(8,128)(2,1)} custom-call(s32[8]{0:T(128)} %pad_add_fusion.3.window_ref, bf16[3,1024,768]{2,1,0:T(8,128)(2,1)} %get-tuple-element.161.k_ref.q_ref.v_ref, bf16[3,768,1024]{2,1,0:T(8,128)(2,1)} %get-tuple-element.162.qt_ref.vt_ref.kt_ref, bf16[3,1024,768]{2,1,0:T(8,128)(2,1)} %get-tuple-element.161.k_ref.q_ref.v_ref, ...), custom_call_target="tpu_custom_call" | custom-call | flops 8053063680 | bytes 15728640 | tf_op jit(solution)/shard_map/attend_back/pallas_call | solution.py:223
  578.9 6.3 fusion.69.begin
  585.2 6.1 collective-permute-done.32
  592.5 7.9 collective-permute-start.34
  610.7 13.4 %collective-permute-done.29.rest_1_ = bf16[1024,768]{1,0:T(8,128)(2,1)} collective-permute-done((bf16[1024,768]{1,0:T(8,128)(2,1)}, bf16[1024,768]{1,0:T(8,128)(2,1)}, u32[]{:S(2)}, u32[]{:S(2)}) %collective-permute-start.29) | collective-permute-done | bytes 1572896 | tf_op jit(solution)/shard_map/ppermute | solution.py:792
  634.3 17.9 %collective-permute-done.37.rest_3_ = bf16[512,768]{1,0:T(8,128)(2,1)S(1)} collective-permute-done((bf16[512,768]{1,0:T(8,128)(2,1)S(1)}, bf16[512,768]{1,0:T(8,128)(2,1)S(1)}, u32[]{:S(2)}, u32[]{:S(2)}) %collective-permute-start.37) | collective-permute-done | bytes 786464 | tf_op jit(solution)/shard_map/ppermute | solution.py:792
  665.1 26.8 %spread.1 = bf16[3840,768]{1,0:T(8,128)(2,1)} custom-call(s32[4096]{0:T(1024)} %pad_add_fusion.ids, s32[4096]{0:T(1024)} %copy-done.49, s32[2]{0:T(128)} %pad_add_fusion.2.place, s32[4096]{0:T(1024)} %get-tuple-element.200.found, s32[8]{0:T(128)} %get-tuple-element.201.ends, s32[4096]{0:T(1024)} %get-tuple-element.202.other_found, ...), custom_call_target="tpu_custom_call" | custom-call | bytes 30277632 | tf_op jit(solution)/shard_map/spread/pallas_call | solution.py:606
  718.9 245.1 %all-reduce.4.cloned.1.call-done = (bf16[3840,768]{1,0:T(8,128)(2,1)}, bf16[4,96,768]{2,1,0:T(8,128)(2,1)}, bf16[2,384,768]{2,1,0:T(8,128)(2,1)}) async-done(((bf16[3840,768]{1,0:T(8,128)(2,1)}, bf16[4,96,768]{2,1,0:T(8,128)(2,1)}, bf16[2,384,768]{2,1,0:T(8,128)(2,1)}), (bf16[3840,768]{1,0:T(8,128)(2,1)}, bf16[4,96,768]{2,1,0:T(8,128)(2,1)}, bf16[2,384,768]{2,1,0:T(8,128)(2,1)})) %all-reduce.4.cloned.1.call-update) | async-done | bytes 7667728 | tf_op jit(solution)/shard_map/psum | solution.py:1202
  964.0 7.2 stats.1
  971.2 12.3 %all-gather.2.parts_ref = f32[8,26,768]{2,1,0:T(8,128)} all-gather(f32[1,26,768]{2,1,0:T(8,128)} %bitcast.412), channel_id=3, replica_groups=mesh['dp'=4,'unit'=8] {'unit'}, dimensions={0}, use_global_device_ids=true | all-gather | bytes 718848 | tf_op jit(solution)/shard_map/all_gather | solution.py:1236
  992.6 16.5 %renew.4 = (f32[1,3840,768]{2,1,0:T(8,128)}, f32[1,3840,768]{2,1,0:T(8,128)}, f32[1,6,1,640]{3,2,1,0:T(1,128)}) custom-call(f32[3]{0:T(128)} %get-tuple-element.238.scalars_ref, s32[1]{0:T(128)} %constant.213.clone.1.at_ref, f32[14,1,768]{2,1,0:T(1,128)} %broadcast_in_dim.65.factor_ref, f32[1,3840,1]{2,1,0:T(8,128)} %broadcast_in_dim_broadcast_in_dim.8.rows_ref, ...), custom_call_target="tpu_custom_call" | custom-call | tf_op jit(solution)/shard_map/renew/pallas_call | solution.py:760
  1012.3 7.9 renew.6
  (502 shorter events, 302.0 us)
Async XLA Ops:
  7.2 172.4 %all-gather.8.cloned.1.call-start = ((), (), s32[]{:S(2)}) async-start(), calls=%async_computation.7 | async-start | bytes 10616832 | tf_op jit(solution)/shard_map/all_gather | solution.py:982
  11.4 239.8 %all-gather.6.cloned.1.call-start = ((), (), s32[]{:S(2)}) async-start(), calls=%async_computation.3 | async-start | bytes 10616832 | tf_op jit(solution)/shard_map/all_gather | solution.py:982
  11.5 21.1 %collective-permute-start.3 = (f32[3840,768]{1,0:T(8,128)}, f32[3840,768]{1,0:T(8,128)}, u32[]{:S(2)}, u32[]{:S(2)}) collective-permute-start(f32[3840,768]{1,0:T(8,128)} %own.1), channel_id=1, source_target_pairs={{0,1},{1,0},{2,3},{3,2},{4,5},{5,4},{6,7},{7,6},{8,9},{9,8},{10,11... | collective-permute-start | bytes 35389448 | tf_op jit(solution)/shard_map/ppermute | solution.py:796
  48.9 37.7 %collective-permute-start.4 = (bf16[512,768]{1,0:T(8,128)(2,1)}, bf16[512,768]{1,0:T(8,128)(2,1)S(1)}, u32[]{:S(2)}, u32[]{:S(2)}) collective-permute-start(bf16[512,768]{1,0:T(8,128)(2,1)} %get-tuple-element.142), channel_id=1, source_target_pairs={{0,4},{1,5},{2,6},{3,7},{4,0},{5,1},{6,2},{7,3},{8,12},{9,13},{10,... | collective-permute-start | bytes 2359304 | tf_op jit(solution)/shard_map/ppermute | solution.py:792
  51.2 37.0 %collective-permute-start.5 = (bf16[512,768]{1,0:T(8,128)(2,1)}, bf16[512,768]{1,0:T(8,128)(2,1)S(1)}, u32[]{:S(2)}, u32[]{:S(2)}) collective-permute-start(bf16[512,768]{1,0:T(8,128)(2,1)} %get-tuple-element.143), channel_id=1, source_target_pairs={{0,2},{1,3},{2,0},{3,1},{4,6},{5,7},{6,4},{7,5},{8,10},{9,11},{10,... | collective-permute-start | bytes 2359304 | tf_op jit(solution)/shard_map/ppermute | solution.py:792
  53.5 51.3 %collective-permute-start.6 = (bf16[512,768]{1,0:T(8,128)(2,1)}, bf16[512,768]{1,0:T(8,128)(2,1)}, u32[]{:S(2)}, u32[]{:S(2)}) collective-permute-start(bf16[512,768]{1,0:T(8,128)(2,1)} %get-tuple-element.144), channel_id=1, source_target_pairs={{0,4},{1,5},{2,6},{3,7},{4,0},{5,1},{6,2},{7,3},{8,12},{9,13},{10,... | collective-permute-start | bytes 2359304 | tf_op jit(solution)/shard_map/ppermute | solution.py:792
  53.6 51.3 %collective-permute-start.7 = (bf16[512,768]{1,0:T(8,128)(2,1)}, bf16[512,768]{1,0:T(8,128)(2,1)}, u32[]{:S(2)}, u32[]{:S(2)}) collective-permute-start(bf16[512,768]{1,0:T(8,128)(2,1)} %get-tuple-element.145), channel_id=1, source_target_pairs={{0,2},{1,3},{2,0},{3,1},{4,6},{5,7},{6,4},{7,5},{8,10},{9,11},{10,... | collective-permute-start | bytes 2359304 | tf_op jit(solution)/shard_map/ppermute | solution.py:792
  105.9 19.5 %collective-permute-start.8 = (bf16[512,768]{1,0:T(8,128)(2,1)}, bf16[512,768]{1,0:T(8,128)(2,1)S(1)}, u32[]{:S(2)}, u32[]{:S(2)}) collective-permute-start(bf16[512,768]{1,0:T(8,128)(2,1)} %add.384), channel_id=1, source_target_pairs={{0,2},{1,3},{2,0},{3,1},{4,6},{5,7},{6,4},{7,5},{8,10},{9,11},{10,... | collective-permute-start | bytes 2359304 | tf_op jit(solution)/shard_map/ppermute | solution.py:792
  107.6 19.1 %collective-permute-start.9 = (bf16[512,768]{1,0:T(8,128)(2,1)S(1)}, bf16[512,768]{1,0:T(8,128)(2,1)S(1)}, u32[]{:S(2)}, u32[]{:S(2)}) collective-permute-start(bf16[512,768]{1,0:T(8,128)(2,1)S(1)} %add.385), channel_id=1, source_target_pairs={{0,4},{1,5},{2,6},{3,7},{4,0},{5,1},{6,2},{7,3},{8,12},{9,13},{10,... | collective-permute-start | bytes 2359304 | tf_op jit(solution)/shard_map/ppermute | solution.py:792
  129.4 365.4 %reduce-scatter.4.cloned.1.call-start = ((), (), s32[]{:S(2)}) async-start(), calls=%async_computation.4 | async-start | bytes 10616832 | tf_op jit(solution)/shard_map/reduce_scatter | solution.py:1114
  129.4 76.2 %collective-permute-start.11 = (bf16[1024,768]{1,0:T(8,128)(2,1)}, bf16[1024,768]{1,0:T(8,128)(2,1)}, u32[]{:S(2)}, u32[]{:S(2)}) collective-permute-start(bf16[1024,768]{1,0:T(8,128)(2,1)} %bitcast.458), channel_id=1, source_target_pairs={{0,4},{1,5},{2,6},{3,7},{4,0},{5,1},{6,2},{7,3},{8,12},{9,13},{10,... | collective-permute-start | bytes 4718600 | tf_op jit(solution)/shard_map/ppermute | solution.py:983
  392.9 192.2 %reduce-scatter.6.cloned.1.call-start = ((), (), s32[]{:S(2)}) async-start(), calls=%async_computation.5 | async-start | bytes 6635520 | tf_op jit(solution)/shard_map/reduce_scatter | solution.py:1107
  465.2 229.3 %reduce-scatter.8.cloned.1.call-start = ((), (), s32[]{:S(2)}) async-start(), calls=%async_computation.6 | async-start | bytes 10616832 | tf_op jit(solution)/shard_map/reduce_scatter | solution.py:1114
  494.2 469.8 %all-reduce.4.cloned.1.call-start = ((), (), s32[]{:S(2)}) async-start(), calls=%async_computation.8 | async-start | bytes 15335424 | tf_op jit(solution)/shard_map/psum | solution.py:1202
  497.6 53.7 %collective-permute-start.24 = (bf16[192,768]{1,0:T(8,128)(2,1)}, bf16[192,768]{1,0:T(8,128)(2,1)S(1)}, u32[]{:S(2)}, u32[]{:S(2)}) collective-permute-start(bf16[192,768]{1,0:T(8,128)(2,1)} %get-tuple-element.327), channel_id=1, source_target_pairs={{0,8},{8,16},{16,24},{24,0},{1,9},{9,17},{17,25},{25,1},{2,10},{10... | collective-permute-start | bytes 884744 | tf_op jit(solution)/shard_map/ppermute | solution.py:816
  499.1 52.1 %collective-permute-start.25 = (bf16[192,768]{1,0:T(8,128)(2,1)}, bf16[192,768]{1,0:T(8,128)(2,1)S(1)}, u32[]{:S(2)}, u32[]{:S(2)}) collective-permute-start(bf16[192,768]{1,0:T(8,128)(2,1)} %get-tuple-element.326), channel_id=1, source_target_pairs={{0,16},{8,24},{16,0},{24,8},{1,17},{9,25},{17,1},{25,9},{2,18},{10... | collective-permute-start | bytes 884744 | tf_op jit(solution)/shard_map/ppermute | solution.py:816
  500.8 50.4 %collective-permute-start.26 = (bf16[192,768]{1,0:T(8,128)(2,1)}, bf16[192,768]{1,0:T(8,128)(2,1)}, u32[]{:S(2)}, u32[]{:S(2)}) collective-permute-start(bf16[192,768]{1,0:T(8,128)(2,1)} %get-tuple-element.325), channel_id=1, source_target_pairs={{0,24},{8,0},{16,8},{24,16},{1,25},{9,1},{17,9},{25,17},{2,26},{10... | collective-permute-start | bytes 884744 | tf_op jit(solution)/shard_map/ppermute | solution.py:816
  564.1 60.0 %collective-permute-start.29 = (bf16[1024,768]{1,0:T(8,128)(2,1)}, bf16[1024,768]{1,0:T(8,128)(2,1)}, u32[]{:S(2)}, u32[]{:S(2)}) collective-permute-start(bf16[1024,768]{1,0:T(8,128)(2,1)} %multiply_convert_fusion.rest_0_), channel_id=1, source_target_pairs={{0,2},{1,3},{2,0},{3,1},{4,6},{5,7},{6,4},{7,5},{8,10},{9,11},{10,... | collective-permute-start | bytes 4718600 | tf_op jit(solution)/shard_map/ppermute | solution.py:792
  566.7 57.5 %collective-permute-start.30 = (bf16[1024,768]{1,0:T(8,128)(2,1)}, bf16[1024,768]{1,0:T(8,128)(2,1)}, u32[]{:S(2)}, u32[]{:S(2)}) collective-permute-start(bf16[1024,768]{1,0:T(8,128)(2,1)} %multiply_convert_fusion.rest_0_), channel_id=1, source_target_pairs={{0,4},{1,5},{2,6},{3,7},{4,0},{5,1},{6,2},{7,3},{8,12},{9,13},{10,... | collective-permute-start | bytes 4718600 | tf_op jit(solution)/shard_map/ppermute | solution.py:792
  570.6 14.6 %collective-permute-start.31 = (bf16[192,768]{1,0:T(8,128)(2,1)}, bf16[192,768]{1,0:T(8,128)(2,1)}, u32[]{:S(2)}, u32[]{:S(2)}) collective-permute-start(bf16[192,768]{1,0:T(8,128)(2,1)} %add_convert_fusion.1), channel_id=1, source_target_pairs={{0,8},{8,16},{16,24},{24,0},{1,9},{9,17},{17,25},{25,1},{2,10},{10... | collective-permute-start | bytes 884744 | tf_op jit(solution)/shard_map/ppermute | solution.py:828
  570.6 20.7 %collective-permute-start.32 = (bf16[192,768]{1,0:T(8,128)(2,1)}, bf16[192,768]{1,0:T(8,128)(2,1)}, u32[]{:S(2)}, u32[]{:S(2)}) collective-permute-start(bf16[192,768]{1,0:T(8,128)(2,1)} %add_convert_fusion.1), channel_id=1, source_target_pairs={{0,16},{8,24},{16,0},{24,8},{1,17},{9,25},{17,1},{25,9},{2,18},{10... | collective-permute-start | bytes 884744 | tf_op jit(solution)/shard_map/ppermute | solution.py:828
  571.0 20.3 %collective-permute-start.33 = (bf16[192,768]{1,0:T(8,128)(2,1)}, bf16[192,768]{1,0:T(8,128)(2,1)}, u32[]{:S(2)}, u32[]{:S(2)}) collective-permute-start(bf16[192,768]{1,0:T(8,128)(2,1)} %add_convert_fusion.1), channel_id=1, source_target_pairs={{0,24},{8,0},{16,8},{24,16},{1,25},{9,1},{17,9},{25,17},{2,26},{10... | collective-permute-start | bytes 884744 | tf_op jit(solution)/shard_map/ppermute | solution.py:828
  624.3 28.0 %collective-permute-start.39 = (bf16[1024,768]{1,0:T(8,128)(2,1)}, bf16[1024,768]{1,0:T(8,128)(2,1)}, u32[]{:S(2)}, u32[]{:S(2)}) collective-permute-start(bf16[1024,768]{1,0:T(8,128)(2,1)} %collective-permute-done.29.rest_1_), channel_id=1, source_target_pairs={{0,1},{1,0},{2,3},{3,2},{4,5},{5,4},{6,7},{7,6},{8,9},{9,8},{10,11... | collective-permute-start | bytes 4718600 | tf_op jit(solution)/shard_map/ppermute | solution.py:796
  624.8 27.5 %collective-permute-start.40 = (bf16[1024,768]{1,0:T(8,128)(2,1)}, bf16[1024,768]{1,0:T(8,128)(2,1)}, u32[]{:S(2)}, u32[]{:S(2)}) collective-permute-start(bf16[1024,768]{1,0:T(8,128)(2,1)} %collective-permute-done.30.rest_2_), channel_id=1, source_target_pairs={{0,1},{1,0},{2,3},{3,2},{4,5},{5,4},{6,7},{7,6},{8,9},{9,8},{10,11... | collective-permute-start | bytes 4718600 | tf_op jit(solution)/shard_map/ppermute | solution.py:796
  624.8 32.6 %collective-permute-start.42 = (bf16[1024,768]{1,0:T(8,128)(2,1)}, bf16[1024,768]{1,0:T(8,128)(2,1)}, u32[]{:S(2)}, u32[]{:S(2)}) collective-permute-start(bf16[1024,768]{1,0:T(8,128)(2,1)} %multiply_convert_fusion.rest_0_), channel_id=1, source_target_pairs={{0,1},{1,0},{2,3},{3,2},{4,5},{5,4},{6,7},{7,6},{8,9},{9,8},{10,11... | collective-permute-start | bytes 4718600 | tf_op jit(solution)/shard_map/ppermute | solution.py:796
  627.7 24.5 %collective-permute-start.37 = (bf16[512,768]{1,0:T(8,128)(2,1)S(1)}, bf16[512,768]{1,0:T(8,128)(2,1)S(1)}, u32[]{:S(2)}, u32[]{:S(2)}) collective-permute-start(bf16[512,768]{1,0:T(8,128)(2,1)S(1)} %slice.476), channel_id=1, source_target_pairs={{0,4},{1,5},{2,6},{3,7},{4,0},{5,1},{6,2},{7,3},{8,12},{9,13},{10,... | collective-permute-start | bytes 2359304 | tf_op jit(solution)/shard_map/ppermute | solution.py:792
  632.1 20.2 %collective-permute-start.38 = (bf16[512,768]{1,0:T(8,128)(2,1)S(1)}, bf16[512,768]{1,0:T(8,128)(2,1)}, u32[]{:S(2)}, u32[]{:S(2)}) collective-permute-start(bf16[512,768]{1,0:T(8,128)(2,1)S(1)} %slice.477), channel_id=1, source_target_pairs={{0,2},{1,3},{2,0},{3,1},{4,6},{5,7},{6,4},{7,5},{8,10},{9,11},{10,... | collective-permute-start | bytes 2359304 | tf_op jit(solution)/shard_map/ppermute | solution.py:792
  655.9 36.0 %collective-permute-start.45 = (bf16[4,96,768]{2,1,0:T(8,128)(2,1)}, bf16[4,96,768]{2,1,0:T(8,128)(2,1)}, u32[]{:S(2)}, u32[]{:S(2)}) collective-permute-start(bf16[4,96,768]{2,1,0:T(8,128)(2,1)} %get-tuple-element.322), channel_id=1, source_target_pairs={{0,2},{1,3},{2,0},{3,1},{4,6},{5,7},{6,4},{7,5},{8,10},{9,11},{10,... | collective-permute-start | bytes 1769480 | tf_op jit(solution)/shard_map/ppermute | solution.py:792
  657.4 34.6 %collective-permute-start.46 = (bf16[4,96,768]{2,1,0:T(8,128)(2,1)}, bf16[4,96,768]{2,1,0:T(8,128)(2,1)}, u32[]{:S(2)}, u32[]{:S(2)}) collective-permute-start(bf16[4,96,768]{2,1,0:T(8,128)(2,1)} %get-tuple-element.321), channel_id=1, source_target_pairs={{0,4},{1,5},{2,6},{3,7},{4,0},{5,1},{6,2},{7,3},{8,12},{9,13},{10,... | collective-permute-start | bytes 1769480 | tf_op jit(solution)/shard_map/ppermute | solution.py:792
  661.6 30.3 %collective-permute-start.47 = (bf16[4,96,768]{2,1,0:T(8,128)(2,1)}, bf16[4,96,768]{2,1,0:T(8,128)(2,1)}, u32[]{:S(2)}, u32[]{:S(2)}) collective-permute-start(bf16[4,96,768]{2,1,0:T(8,128)(2,1)} %get-tuple-element.320), channel_id=1, source_target_pairs={{0,6},{1,7},{2,4},{3,5},{4,2},{5,3},{6,0},{7,1},{8,14},{9,15},{10,... | collective-permute-start | bytes 1769480 | tf_op jit(solution)/shard_map/ppermute | solution.py:792
  663.1 28.8 %collective-permute-start.49 = (bf16[120,768]{1,0:T(8,128)(2,1)S(1)}, bf16[120,768]{1,0:T(8,128)(2,1)}, u32[]{:S(2)}, u32[]{:S(2)}) collective-permute-start(bf16[120,768]{1,0:T(8,128)(2,1)S(1)} %add_convert_fusion.2), channel_id=1, source_target_pairs={{0,16},{8,24},{16,0},{24,8},{1,17},{9,25},{17,1},{25,9},{2,18},{10... | collective-permute-start | bytes 552968 | tf_op jit(solution)/shard_map/ppermute | solution.py:828
  663.7 28.2 %collective-permute-start.50 = (bf16[120,768]{1,0:T(8,128)(2,1)S(1)}, bf16[120,768]{1,0:T(8,128)(2,1)}, u32[]{:S(2)}, u32[]{:S(2)}) collective-permute-start(bf16[120,768]{1,0:T(8,128)(2,1)S(1)} %add_convert_fusion.2), channel_id=1, source_target_pairs={{0,24},{8,0},{16,8},{24,16},{1,25},{9,1},{17,9},{25,17},{2,26},{10... | collective-permute-start | bytes 552968 | tf_op jit(solution)/shard_map/ppermute | solution.py:828
  (119 other events, 1899.9 us)
Sparse Core Ops, SparseCore 0:
  11.6 81.3 all-gather.7
  129.5 75.1 all-gather.5
  393.0 76.2 reduce-scatter.3
  472.7 59.6 reduce-scatter.5
  535.7 105.8 reduce-scatter.7
  694.8 269.1 all-reduce.3

commit v4 on v3

--- a/solution.py
+++ b/solution.py
@@ -15,6 +15,8 @@
 QUERY_BLOCK = 256
 ROW_BLOCK = 512
 UNIT_BLOCK = 768
+FEED_BLOCK = 1536
+FEED_PART = 512
 
 LN_EPS = 1e-06
 ADA_EPS = 1e-30
@@ -156,7 +158,6 @@
     qt_ref,
     v_ref,
     do_ref,
-    dot_ref,
     segk_ref,
     segq_ref,
     lse_ref,
@@ -164,12 +165,14 @@
     dq_sum,
     dk_sum,
     dv_sum,
+    do_t,
     *,
     block,
     score_scale,
 ):
     length = k_ref.shape[1]
     count = length // block
+    do_t[...] = jnp.transpose(do_ref[...].astype(F)).astype(B)
     dk_sum[...] = jnp.zeros_like(dk_sum)
     dv_sum[...] = jnp.zeros_like(dv_sum)
     for i in range(count):
@@ -187,7 +190,7 @@
                 values = v_ref[0, window, :]
                 mask = window_mask(segk_ref, segq_ref, start, width, i * block, block)
                 queries_t = qt_ref[0, :, columns]
-                grads_t = dot_ref[:, columns]
+                grads_t = do_t[:, columns]
                 scores = dot(keys, head_rows(queries_t))
                 scores = jnp.where(jnp.concatenate([mask, mask], axis=1), scores, -MASK_FILL)
                 log_total = jnp.concatenate(
@@ -209,7 +212,7 @@
 
 
 def attend_back(
-    windows, tokens, features, grads, grads_t, key_segments, query_segments, log_total
+    windows, tokens, features, grads, key_segments, query_segments, log_total
 ):
     _, length, breadth = tokens.shape
     pairs = breadth // PAIR
@@ -234,7 +237,6 @@
                 feature_spec(0),
                 token_spec(2),
                 pl.BlockSpec((length, PAIR), lambda p, *_: (0, p)),
-                pl.BlockSpec((PAIR, length), lambda p, *_: (p, 0)),
                 pl.BlockSpec((length, KEY_BLOCK), lambda p, *_: (0, 0)),
                 pl.BlockSpec((8, length), lambda p, *_: (0, 0)),
                 pl.BlockSpec((1, 8, length), lambda p, *_: (p, 0, 0)),
@@ -244,6 +246,7 @@
                 pltpu.VMEM((PAIR, length), F),
                 pltpu.VMEM((length, PAIR), F),
                 pltpu.VMEM((length, PAIR), F),
+                pltpu.VMEM((PAIR, length), B),
             ],
         ),
         out_shape=jax.ShapeDtypeStruct((3, length, breadth), B),
@@ -262,7 +265,6 @@
         features,
         tokens,
         grads,
-        grads_t,
         key_segments,
         query_segments,
         log_total,
@@ -319,12 +321,20 @@
 
 def feed_kernel(x_ref, up_ref, down_ref, scale_ref, act_ref, slope_ref, out_ref):
     first = pl.program_id(0) == 0
-    scale = scale_ref[0]
-    act, slope = gelu_and_slope(contract(x_ref[...], up_ref[...], NT))
-    act = (act * scale).astype(B)
-    act_ref[...] = act
-    slope_ref[...] = (slope * scale).astype(B)
-    part = dot(act, down_ref[...])
+    parts = [slice(at, at + FEED_PART) for at in range(0, up_ref.shape[0], FEED_PART)]
+    ahead = contract(x_ref[...], up_ref[parts[0], :], NT)
+    part = None
+    for k, lanes in enumerate(parts):
+        before = ahead
+        if k + 1 < len(parts):
+            ahead = contract(x_ref[...], up_ref[parts[k + 1], :], NT)
+        act, slope = gelu_and_slope(before)
+        scale = scale_ref[0, :, lanes]
+        act = (act * scale).astype(B)
+        act_ref[:, lanes] = act
+        slope_ref[:, lanes] = (slope * scale).astype(B)
+        term = dot(act, down_ref[lanes, :])
+        part = term if part is None else part + term
 
     @pl.when(first)
     def _():
@@ -338,7 +348,7 @@
 def feed(x, weights, scale):
     length, breadth = x.shape
     units = weights.shape[1]
-    block = UNIT_BLOCK
+    block = FEED_BLOCK
     return pl.pallas_call(
         feed_kernel,
         grid=(units // block,),
@@ -1118,13 +1128,11 @@
         grad_branch = (grad_first * layer_gate[layer_at, 0] * hidden_gate).astype(B)
         scale = head_scale[layer_at]
         grad_mixed = (contract(grad_branch, weights[3], NT) * scale).astype(B)
-        grad_mixed_t = (contract(weights[3], grad_branch, NT) * scale[:, None]).astype(B)
         grad_proj = attend_back(
             windows,
             tokens,
             features,
             grad_mixed,
-            grad_mixed_t,
             key_segments,
             query_segments,
             log_total,

time: 1050 us -> 1040 us (level)
  waiting for transfers between devices: 345 us -> 356 us
    dot_general x8 -> x6, matrix products: 38.4 us -> 33.1 us  [contract(): return lax.dot_general(left, right, dims, preferred_element_type=F)]
  transfers between devices with their start and end apart: 57 -> 57, of which waited for: 28 -> 27; matrix products, arithmetic and copies ran while one was open for 17% -> 16% of each run, Pallas kernels for 25% -> 25%
where the time goes in v4:
time: 1040 us; the launch traced here: 1030 us
  waiting for transfers between devices  356 us (34%)
  Pallas kernels  351 us (34%)
  other arithmetic  111 us (11%)
  matrix products  83 us (8%)
  starting transfers between devices  59.1 us (6%)
  local copies, waits for them, and re-layouts  41.4 us (4%)
  between operations  19.2 us (2%)
  blocking collectives  12.2 us (1%)
    psum x1, waiting for transfers between devices, local(): lax.psum((embed_part, feed_parts[0], attn_parts[0]), 'dp')  245 us
    ppermute x25, waiting for transfers between devices, across(): return lax.ppermute(value, 'unit', pairs)  84.8 us
    pallas_call x2, Pallas kernels, attend_back(): pl.pallas_call(functools.partial(attend_back_kernel, block=QUERY_BLOCK, s...  63.3 us
    pallas_call x2, Pallas kernels, feed_back(): pl.pallas_call(feed_back_kernel, grid=(units // block,), in_specs=[whole,...  57.4 us
    pallas_call x2, Pallas kernels, feed(): pl.pallas_call(feed_kernel, grid=(units // block,), in_specs=[pl.BlockSpe...  48.2 us
    pallas_call x2, Pallas kernels, attend(): pl.pallas_call(functools.partial(attend_kernel, block=QUERY_BLOCK), grid_...  39.2 us
    pallas_call x3, Pallas kernels, scan_ids(): pl.pallas_call(functools.partial(scan_kernel, vocab=vocab), in_specs=[sme...  36.9 us
    ppermute x25, starting transfers between devices, across(): return lax.ppermute(value, 'unit', pairs)  33.5 us
  transfers between devices with their start and end apart: 57, of which 27 were waited for; matrix products, arithmetic and copies ran while one was open for 16% of the time, Pallas kernels for 25%

profile of v4, /device:TPU:0, one launch (start us, length us, event | category | flops | bytes accessed | tf_op | source)
XLA Modules:
  0.0 1032.7 jit_solution(8857259351821087943)
XLA Ops:
  20.2 12.3 %scan_ids.3 = (s32[4096]{0:T(1024)}, s32[8]{0:T(128)}) custom-call(s32[4096]{0:T(1024)} %pad_add_fusion.ids, s32[2]{0:T(128)} %pad_add_fusion.1.place), custom_call_target="tpu_custom_call" | custom-call | tf_op jit(solution)/shard_map/scan_ids/pallas_call | solution.py:468
  32.5 16.6 %lookup.1 = (bf16[512,768]{1,0:T(8,128)(2,1)}, bf16[512,768]{1,0:T(8,128)(2,1)}, bf16[512,768]{1,0:T(8,128)(2,1)}, bf16[512,768]{1,0:T(8,128)(2,1)}, bf16[512,76...) custom-call(s32[4096]{0:T(1024)} %pad_add_fusion.ids, ...), custom_call_target="tpu_custom_call" | custom-call | bytes 29884416 | tf_op jit(solution)/shard_map/lookup/pallas_call | solution.py:532
  54.0 7.4 convert_element_type.197
  61.4 9.9 convert_element_type.198.weight_ref
  73.2 12.3 %scan_ids.4 = (s32[4096]{0:T(1024)}, s32[8]{0:T(128)}) custom-call(s32[4096]{0:T(1024)} %pad_add_fusion.ids, s32[2]{0:T(128)} %pad_add_fusion.2.place), custom_call_target="tpu_custom_call" | custom-call | tf_op jit(solution)/shard_map/scan_ids/pallas_call | solution.py:468
  88.6 16.2 %collective-permute-done.6 = bf16[512,768]{1,0:T(8,128)(2,1)} collective-permute-done((bf16[512,768]{1,0:T(8,128)(2,1)}, bf16[512,768]{1,0:T(8,128)(2,1)}, u32[]{:S(2)}, u32[]{:S(2)}) %collective-permute-start.6) | collective-permute-done | bytes 786464 | tf_op jit(solution)/shard_map/ppermute | solution.py:802
  110.0 12.3 %scan_ids.5 = (s32[4096]{0:T(1024)}, s32[8]{0:T(128)}) custom-call(s32[4096]{0:T(1024)} %copy-done.48, s32[2]{0:T(128)} %pad_add_fusion.2.place), custom_call_target="tpu_custom_call" | custom-call | tf_op jit(solution)/shard_map/scan_ids/pallas_call | solution.py:468
  138.0 11.0 %project.2 = (bf16[3,1024,768]{2,1,0:T(8,128)(2,1)}, bf16[3,768,1024]{2,1,0:T(8,128)(2,1)}) custom-call(bf16[1024,768]{1,0:T(8,128)(2,1)} %fusion.11.x_ref, bf16[2,4,768,768]{3,2,1,0:T(8,128)(2,1)} %convert_element_type.198.weight_ref), custom_call_target="tpu_custom_call" | custom-call | flops 7247757312 | bytes 14548992 | tf_op jit(solution)/shard_map/project/pallas_call | solution.py:284
  150.6 19.7 %attend.2 = (bf16[768,1024]{1,0:T(8,128)(2,1)}, f32[6,8,1024]{2,1,0:T(8,128)}) custom-call(s32[8]{0:T(128)} %pad_add_fusion.3.window_ref, f32[12]{0:T(128)} %get-tuple-element.413.gate_ref, bf16[3,1024,768]{2,1,0:T(8,128)(2,1)} %get-tuple-element.161.k_ref.q_ref.v_ref, bf16[3,768,1024]{2,1,0:T(8,128)(2,1)} %get-tuple-element.162.qt_ref.vt_ref.kt_ref, ...), custom_call_target="tpu_custom_call" | custom-call | flops 3221225472 | bytes 6291456 | tf_op jit(solution)/shard_map/attend/pallas_call | solution.py:122
  179.2 24.3 %feed.2 = (bf16[1024,3072]{1,0:T(8,128)(2,1)}, bf16[1024,3072]{1,0:T(8,128)(2,1)}, f32[1024,768]{1,0:T(8,128)}) custom-call(bf16[1024,768]{1,0:T(8,128)(2,1)} %fusion.8.x_ref, bf16[2,3072,768]{2,1,0:T(8,128)(2,1)} %bitcast.439, bf16[2,3072,768]{2,1,0:T(8,128)(2,1)} %bitcast.440, f32[1,1,3072]{2,1,0:T(1,128)} %get-tuple-element.399.scale_ref), custom_call_target="tpu_custom_call" | custom-call | flops 9663676416 | bytes 26738688 | tf_op jit(solution)/shard_map/feed/pallas_call | solution.py:352
  210.5 10.8 %project.3 = (bf16[3,1024,768]{2,1,0:T(8,128)(2,1)}, bf16[3,768,1024]{2,1,0:T(8,128)(2,1)}) custom-call(bf16[1024,768]{1,0:T(8,128)(2,1)} %fusion.9.x_ref, bf16[2,4,768,768]{3,2,1,0:T(8,128)(2,1)} %convert_element_type.198.weight_ref), custom_call_target="tpu_custom_call" | custom-call | flops 7247757312 | bytes 14548992 | tf_op jit(solution)/shard_map/project/pallas_call | solution.py:284
  221.3 19.5 %attend.3 = (bf16[768,1024]{1,0:T(8,128)(2,1)}, f32[6,8,1024]{2,1,0:T(8,128)}) custom-call(s32[8]{0:T(128)} %pad_add_fusion.3.window_ref, f32[12]{0:T(128)} %get-tuple-element.412.gate_ref, bf16[3,1024,768]{2,1,0:T(8,128)(2,1)} %get-tuple-element.166.k_ref.q_ref.v_ref, bf16[3,768,1024]{2,1,0:T(8,128)(2,1)} %get-tuple-element.167.qt_ref.vt_ref.kt_ref, ...), custom_call_target="tpu_custom_call" | custom-call | flops 3221225472 | bytes 6291456 | tf_op jit(solution)/shard_map/attend/pallas_call | solution.py:122
  248.8 24.0 %feed.3 = (bf16[1024,3072]{1,0:T(8,128)(2,1)}, bf16[1024,3072]{1,0:T(8,128)(2,1)}, f32[1024,768]{1,0:T(8,128)}) custom-call(bf16[1024,768]{1,0:T(8,128)(2,1)} %fusion.10.x_ref, bf16[2,3072,768]{2,1,0:T(8,128)(2,1)} %all-gather.6.cloned.1.call-done.up_ref.down_ref, bf16[2,3072,768]{2,1,0:T(8,128)(2,1)} %all-gather.6.cloned.1.call-done.up_ref.down_ref, ...), custom_call_target="tpu_custom_call" | custom-call | flops 9663676416 | bytes 26738688 | tf_op jit(solution)/shard_map/feed/pallas_call | solution.py:352
  295.8 8.5 fusion.61
  330.2 7.3 fusion.64
  359.7 28.6 %feed_back.2 = (f32[1024,768]{1,0:T(8,128)}, bf16[8,2,384,768]{3,2,1,0:T(8,128)(2,1)}) custom-call(bf16[1024,768]{1,0:T(8,128)(2,1)} %get-tuple-element.303.grad_ref, bf16[1024,768]{1,0:T(8,128)(2,1)} %fusion.10.x_ref, bf16[1024,3072]{1,0:T(8,128)(2,1)} %get-tuple-element.181.act_ref, bf16[1024,3072]{1,0:T(8,128)(2,1)} %get-tuple-element.182.slope_ref, ...), custom_call_target="tpu_custom_call" | custom-call | flops 19327352832 | bytes 37748736 | tf_op jit(solution)/shard_map/feed_back/pallas_call | solution.py:415
  400.6 31.7 %attend_back.2 = bf16[3,1024,768]{2,1,0:T(8,128)(2,1)} custom-call(s32[8]{0:T(128)} %pad_add_fusion.3.window_ref, bf16[3,1024,768]{2,1,0:T(8,128)(2,1)} %get-tuple-element.166.k_ref.q_ref.v_ref, bf16[3,768,1024]{2,1,0:T(8,128)(2,1)} %get-tuple-element.167.qt_ref.vt_ref.kt_ref, bf16[3,1024,768]{2,1,0:T(8,128)(2,1)} %get-tuple-element.166.k_ref.q_ref.v_ref, ...), custom_call_target="tpu_custom_call" | custom-call | flops 8053063680 | bytes 15728640 | tf_op jit(solution)/shard_map/attend_back/pallas_call | solution.py:226
  432.3 8.4 bitcast_add_fusion.1
  456.6 28.8 %feed_back.3 = (f32[1024,768]{1,0:T(8,128)}, bf16[8,2,384,768]{3,2,1,0:T(8,128)(2,1)}) custom-call(bf16[1024,768]{1,0:T(8,128)(2,1)} %get-tuple-element.188.grad_ref, bf16[1024,768]{1,0:T(8,128)(2,1)} %fusion.8.x_ref, bf16[1024,3072]{1,0:T(8,128)(2,1)} %get-tuple-element.189.act_ref, bf16[1024,3072]{1,0:T(8,128)(2,1)} %get-tuple-element.190.slope_ref, ...), custom_call_target="tpu_custom_call" | custom-call | flops 19327352832 | bytes 37748736 | tf_op jit(solution)/shard_map/feed_back/pallas_call | solution.py:415
  502.4 31.6 %attend_back.3 = bf16[3,1024,768]{2,1,0:T(8,128)(2,1)} custom-call(s32[8]{0:T(128)} %pad_add_fusion.3.window_ref, bf16[3,1024,768]{2,1,0:T(8,128)(2,1)} %get-tuple-element.161.k_ref.q_ref.v_ref, bf16[3,768,1024]{2,1,0:T(8,128)(2,1)} %get-tuple-element.162.qt_ref.vt_ref.kt_ref, bf16[3,1024,768]{2,1,0:T(8,128)(2,1)} %get-tuple-element.161.k_ref.q_ref.v_ref, ...), custom_call_target="tpu_custom_call" | custom-call | flops 8053063680 | bytes 15728640 | tf_op jit(solution)/shard_map/attend_back/pallas_call | solution.py:226
  537.4 6.5 bitcast_add_fusion
  564.4 6.3 fusion.65.begin
  575.3 7.0 collective-permute-start.34
  589.0 6.1 collective-permute-done.35
  595.1 14.5 %collective-permute-done.29.rest_1_ = bf16[1024,768]{1,0:T(8,128)(2,1)} collective-permute-done((bf16[1024,768]{1,0:T(8,128)(2,1)}, bf16[1024,768]{1,0:T(8,128)(2,1)}, u32[]{:S(2)}, u32[]{:S(2)}) %collective-permute-start.29) | collective-permute-done | bytes 1572896 | tf_op jit(solution)/shard_map/ppermute | solution.py:802
  620.0 25.2 %collective-permute-done.37.rest_3_ = bf16[512,768]{1,0:T(8,128)(2,1)S(1)} collective-permute-done((bf16[512,768]{1,0:T(8,128)(2,1)S(1)}, bf16[512,768]{1,0:T(8,128)(2,1)S(1)}, u32[]{:S(2)}, u32[]{:S(2)}) %collective-permute-start.37) | collective-permute-done | bytes 786464 | tf_op jit(solution)/shard_map/ppermute | solution.py:802
  660.1 26.7 %spread.1 = bf16[3840,768]{1,0:T(8,128)(2,1)} custom-call(s32[4096]{0:T(1024)} %pad_add_fusion.ids, s32[4096]{0:T(1024)} %copy-done.48, s32[2]{0:T(128)} %pad_add_fusion.2.place, s32[4096]{0:T(1024)} %get-tuple-element.200.found, s32[8]{0:T(128)} %get-tuple-element.201.ends, s32[4096]{0:T(1024)} %get-tuple-element.202.other_found, ...), custom_call_target="tpu_custom_call" | custom-call | bytes 30277632 | tf_op jit(solution)/shard_map/spread/pallas_call | solution.py:616
  714.0 245.1 %all-reduce.4.cloned.1.call-done = (bf16[3840,768]{1,0:T(8,128)(2,1)}, bf16[4,96,768]{2,1,0:T(8,128)(2,1)}, bf16[2,384,768]{2,1,0:T(8,128)(2,1)}) async-done(((bf16[3840,768]{1,0:T(8,128)(2,1)}, bf16[4,96,768]{2,1,0:T(8,128)(2,1)}, bf16[2,384,768]{2,1,0:T(8,128)(2,1)}), (bf16[3840,768]{1,0:T(8,128)(2,1)}, bf16[4,96,768]{2,1,0:T(8,128)(2,1)}, bf16[2,384,768]{2,1,0:T(8,128)(2,1)})) %all-reduce.4.cloned.1.call-update) | async-done | bytes 7667728 | tf_op jit(solution)/shard_map/psum | solution.py:1210
  959.0 7.2 stats.1
  966.3 12.2 %all-gather.2.parts_ref = f32[8,26,768]{2,1,0:T(8,128)} all-gather(f32[1,26,768]{2,1,0:T(8,128)} %bitcast.402), channel_id=3, replica_groups=mesh['dp'=4,'unit'=8] {'unit'}, dimensions={0}, use_global_device_ids=true | all-gather | bytes 718848 | tf_op jit(solution)/shard_map/all_gather | solution.py:1244
  987.7 16.5 %renew.4 = (f32[1,3840,768]{2,1,0:T(8,128)}, f32[1,3840,768]{2,1,0:T(8,128)}, f32[1,6,1,640]{3,2,1,0:T(1,128)}) custom-call(f32[3]{0:T(128)} %get-tuple-element.238.scalars_ref, s32[1]{0:T(128)} %constant.213.clone.1.at_ref, f32[14,1,768]{2,1,0:T(1,128)} %broadcast_in_dim.65.factor_ref, f32[1,3840,1]{2,1,0:T(8,128)} %broadcast_in_dim_broadcast_in_dim.8.rows_ref, ...), custom_call_target="tpu_custom_call" | custom-call | tf_op jit(solution)/shard_map/renew/pallas_call | solution.py:770
  1007.3 7.9 renew.6
  (476 shorter events, 290.9 us)
Async XLA Ops:
  7.2 172.0 %all-gather.8.cloned.1.call-start = ((), (), s32[]{:S(2)}) async-start(), calls=%async_computation.7 | async-start | bytes 10616832 | tf_op jit(solution)/shard_map/all_gather | solution.py:992
  11.4 237.4 %all-gather.6.cloned.1.call-start = ((), (), s32[]{:S(2)}) async-start(), calls=%async_computation.3 | async-start | bytes 10616832 | tf_op jit(solution)/shard_map/all_gather | solution.py:992
  11.4 21.1 %collective-permute-start.3 = (f32[3840,768]{1,0:T(8,128)}, f32[3840,768]{1,0:T(8,128)}, u32[]{:S(2)}, u32[]{:S(2)}) collective-permute-start(f32[3840,768]{1,0:T(8,128)} %own.1), channel_id=1, source_target_pairs={{0,1},{1,0},{2,3},{3,2},{4,5},{5,4},{6,7},{7,6},{8,9},{9,8},{10,11... | collective-permute-start | bytes 35389448 | tf_op jit(solution)/shard_map/ppermute | solution.py:806
  49.2 38.2 %collective-permute-start.4 = (bf16[512,768]{1,0:T(8,128)(2,1)}, bf16[512,768]{1,0:T(8,128)(2,1)S(1)}, u32[]{:S(2)}, u32[]{:S(2)}) collective-permute-start(bf16[512,768]{1,0:T(8,128)(2,1)} %get-tuple-element.142), channel_id=1, source_target_pairs={{0,4},{1,5},{2,6},{3,7},{4,0},{5,1},{6,2},{7,3},{8,12},{9,13},{10,... | collective-permute-start | bytes 2359304 | tf_op jit(solution)/shard_map/ppermute | solution.py:802
  51.9 36.7 %collective-permute-start.5 = (bf16[512,768]{1,0:T(8,128)(2,1)}, bf16[512,768]{1,0:T(8,128)(2,1)S(1)}, u32[]{:S(2)}, u32[]{:S(2)}) collective-permute-start(bf16[512,768]{1,0:T(8,128)(2,1)} %get-tuple-element.143), channel_id=1, source_target_pairs={{0,2},{1,3},{2,0},{3,1},{4,6},{5,7},{6,4},{7,5},{8,10},{9,11},{10,... | collective-permute-start | bytes 2359304 | tf_op jit(solution)/shard_map/ppermute | solution.py:802
  51.9 52.9 %collective-permute-start.6 = (bf16[512,768]{1,0:T(8,128)(2,1)}, bf16[512,768]{1,0:T(8,128)(2,1)}, u32[]{:S(2)}, u32[]{:S(2)}) collective-permute-start(bf16[512,768]{1,0:T(8,128)(2,1)} %get-tuple-element.144), channel_id=1, source_target_pairs={{0,4},{1,5},{2,6},{3,7},{4,0},{5,1},{6,2},{7,3},{8,12},{9,13},{10,... | collective-permute-start | bytes 2359304 | tf_op jit(solution)/shard_map/ppermute | solution.py:802
  52.1 52.7 %collective-permute-start.7 = (bf16[512,768]{1,0:T(8,128)(2,1)}, bf16[512,768]{1,0:T(8,128)(2,1)}, u32[]{:S(2)}, u32[]{:S(2)}) collective-permute-start(bf16[512,768]{1,0:T(8,128)(2,1)} %get-tuple-element.145), channel_id=1, source_target_pairs={{0,2},{1,3},{2,0},{3,1},{4,6},{5,7},{6,4},{7,5},{8,10},{9,11},{10,... | collective-permute-start | bytes 2359304 | tf_op jit(solution)/shard_map/ppermute | solution.py:802
  105.9 19.2 %collective-permute-start.8 = (bf16[512,768]{1,0:T(8,128)(2,1)}, bf16[512,768]{1,0:T(8,128)(2,1)S(1)}, u32[]{:S(2)}, u32[]{:S(2)}) collective-permute-start(bf16[512,768]{1,0:T(8,128)(2,1)} %add.384), channel_id=1, source_target_pairs={{0,2},{1,3},{2,0},{3,1},{4,6},{5,7},{6,4},{7,5},{8,10},{9,11},{10,... | collective-permute-start | bytes 2359304 | tf_op jit(solution)/shard_map/ppermute | solution.py:802
  107.5 19.1 %collective-permute-start.9 = (bf16[512,768]{1,0:T(8,128)(2,1)S(1)}, bf16[512,768]{1,0:T(8,128)(2,1)S(1)}, u32[]{:S(2)}, u32[]{:S(2)}) collective-permute-start(bf16[512,768]{1,0:T(8,128)(2,1)S(1)} %add.385), channel_id=1, source_target_pairs={{0,4},{1,5},{2,6},{3,7},{4,0},{5,1},{6,2},{7,3},{8,12},{9,13},{10,... | collective-permute-start | bytes 2359304 | tf_op jit(solution)/shard_map/ppermute | solution.py:802
  129.3 356.9 %reduce-scatter.4.cloned.1.call-start = ((), (), s32[]{:S(2)}) async-start(), calls=%async_computation.4 | async-start | bytes 10616832 | tf_op jit(solution)/shard_map/reduce_scatter | solution.py:1124
  129.3 74.2 %collective-permute-start.11 = (bf16[1024,768]{1,0:T(8,128)(2,1)}, bf16[1024,768]{1,0:T(8,128)(2,1)}, u32[]{:S(2)}, u32[]{:S(2)}) collective-permute-start(bf16[1024,768]{1,0:T(8,128)(2,1)} %bitcast.447), channel_id=1, source_target_pairs={{0,4},{1,5},{2,6},{3,7},{4,0},{5,1},{6,2},{7,3},{8,12},{9,13},{10,... | collective-permute-start | bytes 4718600 | tf_op jit(solution)/shard_map/ppermute | solution.py:993
  388.4 182.3 %reduce-scatter.6.cloned.1.call-start = ((), (), s32[]{:S(2)}) async-start(), calls=%async_computation.5 | async-start | bytes 6635520 | tf_op jit(solution)/shard_map/reduce_scatter | solution.py:1117
  456.6 232.9 %reduce-scatter.8.cloned.1.call-start = ((), (), s32[]{:S(2)}) async-start(), calls=%async_computation.6 | async-start | bytes 10616832 | tf_op jit(solution)/shard_map/reduce_scatter | solution.py:1124
  485.5 473.6 %all-reduce.4.cloned.1.call-start = ((), (), s32[]{:S(2)}) async-start(), calls=%async_computation.8 | async-start | bytes 15335424 | tf_op jit(solution)/shard_map/psum | solution.py:1210
  488.6 48.7 %collective-permute-start.24 = (bf16[192,768]{1,0:T(8,128)(2,1)}, bf16[192,768]{1,0:T(8,128)(2,1)}, u32[]{:S(2)}, u32[]{:S(2)}) collective-permute-start(bf16[192,768]{1,0:T(8,128)(2,1)} %get-tuple-element.323), channel_id=1, source_target_pairs={{0,8},{8,16},{16,24},{24,0},{1,9},{9,17},{17,25},{25,1},{2,10},{10... | collective-permute-start | bytes 884744 | tf_op jit(solution)/shard_map/ppermute | solution.py:826
  490.0 47.4 %collective-permute-start.25 = (bf16[192,768]{1,0:T(8,128)(2,1)}, bf16[192,768]{1,0:T(8,128)(2,1)}, u32[]{:S(2)}, u32[]{:S(2)}) collective-permute-start(bf16[192,768]{1,0:T(8,128)(2,1)} %get-tuple-element.322), channel_id=1, source_target_pairs={{0,16},{8,24},{16,0},{24,8},{1,17},{9,25},{17,1},{25,9},{2,18},{10... | collective-permute-start | bytes 884744 | tf_op jit(solution)/shard_map/ppermute | solution.py:826
  490.0 47.4 %collective-permute-start.26 = (bf16[192,768]{1,0:T(8,128)(2,1)}, bf16[192,768]{1,0:T(8,128)(2,1)}, u32[]{:S(2)}, u32[]{:S(2)}) collective-permute-start(bf16[192,768]{1,0:T(8,128)(2,1)} %get-tuple-element.321), channel_id=1, source_target_pairs={{0,24},{8,0},{16,8},{24,16},{1,25},{9,1},{17,9},{25,17},{2,26},{10... | collective-permute-start | bytes 884744 | tf_op jit(solution)/shard_map/ppermute | solution.py:826
  548.3 61.3 %collective-permute-start.29 = (bf16[1024,768]{1,0:T(8,128)(2,1)}, bf16[1024,768]{1,0:T(8,128)(2,1)}, u32[]{:S(2)}, u32[]{:S(2)}) collective-permute-start(bf16[1024,768]{1,0:T(8,128)(2,1)} %multiply_convert_fusion.rest_0_), channel_id=1, source_target_pairs={{0,2},{1,3},{2,0},{3,1},{4,6},{5,7},{6,4},{7,5},{8,10},{9,11},{10,... | collective-permute-start | bytes 4718600 | tf_op jit(solution)/shard_map/ppermute | solution.py:802
  554.1 55.6 %collective-permute-start.30 = (bf16[1024,768]{1,0:T(8,128)(2,1)}, bf16[1024,768]{1,0:T(8,128)(2,1)}, u32[]{:S(2)}, u32[]{:S(2)}) collective-permute-start(bf16[1024,768]{1,0:T(8,128)(2,1)} %multiply_convert_fusion.rest_0_), channel_id=1, source_target_pairs={{0,4},{1,5},{2,6},{3,7},{4,0},{5,1},{6,2},{7,3},{8,12},{9,13},{10,... | collective-permute-start | bytes 4718600 | tf_op jit(solution)/shard_map/ppermute | solution.py:802
  556.1 14.6 %collective-permute-start.31 = (bf16[192,768]{1,0:T(8,128)(2,1)}, bf16[192,768]{1,0:T(8,128)(2,1)}, u32[]{:S(2)}, u32[]{:S(2)}) collective-permute-start(bf16[192,768]{1,0:T(8,128)(2,1)} %add_convert_fusion.1), channel_id=1, source_target_pairs={{0,8},{8,16},{16,24},{24,0},{1,9},{9,17},{17,25},{25,1},{2,10},{10... | collective-permute-start | bytes 884744 | tf_op jit(solution)/shard_map/ppermute | solution.py:838
  556.1 18.0 %collective-permute-start.32 = (bf16[192,768]{1,0:T(8,128)(2,1)}, bf16[192,768]{1,0:T(8,128)(2,1)}, u32[]{:S(2)}, u32[]{:S(2)}) collective-permute-start(bf16[192,768]{1,0:T(8,128)(2,1)} %add_convert_fusion.1), channel_id=1, source_target_pairs={{0,16},{8,24},{16,0},{24,8},{1,17},{9,25},{17,1},{25,9},{2,18},{10... | collective-permute-start | bytes 884744 | tf_op jit(solution)/shard_map/ppermute | solution.py:838
  556.1 18.0 %collective-permute-start.33 = (bf16[192,768]{1,0:T(8,128)(2,1)}, bf16[192,768]{1,0:T(8,128)(2,1)}, u32[]{:S(2)}, u32[]{:S(2)}) collective-permute-start(bf16[192,768]{1,0:T(8,128)(2,1)} %add_convert_fusion.1), channel_id=1, source_target_pairs={{0,24},{8,0},{16,8},{24,16},{1,25},{9,1},{17,9},{25,17},{2,26},{10... | collective-permute-start | bytes 884744 | tf_op jit(solution)/shard_map/ppermute | solution.py:838
  609.6 37.7 %collective-permute-start.39 = (bf16[1024,768]{1,0:T(8,128)(2,1)}, bf16[1024,768]{1,0:T(8,128)(2,1)}, u32[]{:S(2)}, u32[]{:S(2)}) collective-permute-start(bf16[1024,768]{1,0:T(8,128)(2,1)} %collective-permute-done.29.rest_1_), channel_id=1, source_target_pairs={{0,1},{1,0},{2,3},{3,2},{4,5},{5,4},{6,7},{7,6},{8,9},{9,8},{10,11... | collective-permute-start | bytes 4718600 | tf_op jit(solution)/shard_map/ppermute | solution.py:806
  610.2 37.2 %collective-permute-start.40 = (bf16[1024,768]{1,0:T(8,128)(2,1)}, bf16[1024,768]{1,0:T(8,128)(2,1)}, u32[]{:S(2)}, u32[]{:S(2)}) collective-permute-start(bf16[1024,768]{1,0:T(8,128)(2,1)} %collective-permute-done.30.rest_2_), channel_id=1, source_target_pairs={{0,1},{1,0},{2,3},{3,2},{4,5},{5,4},{6,7},{7,6},{8,9},{9,8},{10,11... | collective-permute-start | bytes 4718600 | tf_op jit(solution)/shard_map/ppermute | solution.py:806
  610.2 41.3 %collective-permute-start.42 = (bf16[1024,768]{1,0:T(8,128)(2,1)}, bf16[1024,768]{1,0:T(8,128)(2,1)}, u32[]{:S(2)}, u32[]{:S(2)}) collective-permute-start(bf16[1024,768]{1,0:T(8,128)(2,1)} %multiply_convert_fusion.rest_0_), channel_id=1, source_target_pairs={{0,1},{1,0},{2,3},{3,2},{4,5},{5,4},{6,7},{7,6},{8,9},{9,8},{10,11... | collective-permute-start | bytes 4718600 | tf_op jit(solution)/shard_map/ppermute | solution.py:806
  613.0 32.2 %collective-permute-start.37 = (bf16[512,768]{1,0:T(8,128)(2,1)S(1)}, bf16[512,768]{1,0:T(8,128)(2,1)S(1)}, u32[]{:S(2)}, u32[]{:S(2)}) collective-permute-start(bf16[512,768]{1,0:T(8,128)(2,1)S(1)} %slice.474), channel_id=1, source_target_pairs={{0,4},{1,5},{2,6},{3,7},{4,0},{5,1},{6,2},{7,3},{8,12},{9,13},{10,... | collective-permute-start | bytes 2359304 | tf_op jit(solution)/shard_map/ppermute | solution.py:802
  617.5 29.8 %collective-permute-start.38 = (bf16[512,768]{1,0:T(8,128)(2,1)S(1)}, bf16[512,768]{1,0:T(8,128)(2,1)}, u32[]{:S(2)}, u32[]{:S(2)}) collective-permute-start(bf16[512,768]{1,0:T(8,128)(2,1)S(1)} %slice.475), channel_id=1, source_target_pairs={{0,2},{1,3},{2,0},{3,1},{4,6},{5,7},{6,4},{7,5},{8,10},{9,11},{10,... | collective-permute-start | bytes 2359304 | tf_op jit(solution)/shard_map/ppermute | solution.py:802
  650.9 36.0 %collective-permute-start.45 = (bf16[4,96,768]{2,1,0:T(8,128)(2,1)}, bf16[4,96,768]{2,1,0:T(8,128)(2,1)}, u32[]{:S(2)}, u32[]{:S(2)}) collective-permute-start(bf16[4,96,768]{2,1,0:T(8,128)(2,1)} %get-tuple-element.318), channel_id=1, source_target_pairs={{0,2},{1,3},{2,0},{3,1},{4,6},{5,7},{6,4},{7,5},{8,10},{9,11},{10,... | collective-permute-start | bytes 1769480 | tf_op jit(solution)/shard_map/ppermute | solution.py:802
  651.5 35.4 %collective-permute-start.46 = (bf16[4,96,768]{2,1,0:T(8,128)(2,1)}, bf16[4,96,768]{2,1,0:T(8,128)(2,1)}, u32[]{:S(2)}, u32[]{:S(2)}) collective-permute-start(bf16[4,96,768]{2,1,0:T(8,128)(2,1)} %get-tuple-element.317), channel_id=1, source_target_pairs={{0,4},{1,5},{2,6},{3,7},{4,0},{5,1},{6,2},{7,3},{8,12},{9,13},{10,... | collective-permute-start | bytes 1769480 | tf_op jit(solution)/shard_map/ppermute | solution.py:802
  656.6 30.3 %collective-permute-start.47 = (bf16[4,96,768]{2,1,0:T(8,128)(2,1)}, bf16[4,96,768]{2,1,0:T(8,128)(2,1)}, u32[]{:S(2)}, u32[]{:S(2)}) collective-permute-start(bf16[4,96,768]{2,1,0:T(8,128)(2,1)} %get-tuple-element.316), channel_id=1, source_target_pairs={{0,6},{1,7},{2,4},{3,5},{4,2},{5,3},{6,0},{7,1},{8,14},{9,15},{10,... | collective-permute-start | bytes 1769480 | tf_op jit(solution)/shard_map/ppermute | solution.py:802
  658.1 28.8 %collective-permute-start.49 = (bf16[120,768]{1,0:T(8,128)(2,1)S(1)}, bf16[120,768]{1,0:T(8,128)(2,1)}, u32[]{:S(2)}, u32[]{:S(2)}) collective-permute-start(bf16[120,768]{1,0:T(8,128)(2,1)S(1)} %add_convert_fusion.2), channel_id=1, source_target_pairs={{0,16},{8,24},{16,0},{24,8},{1,17},{9,25},{17,1},{25,9},{2,18},{10... | collective-permute-start | bytes 552968 | tf_op jit(solution)/shard_map/ppermute | solution.py:838
  658.7 28.2 %collective-permute-start.50 = (bf16[120,768]{1,0:T(8,128)(2,1)S(1)}, bf16[120,768]{1,0:T(8,128)(2,1)}, u32[]{:S(2)}, u32[]{:S(2)}) collective-permute-start(bf16[120,768]{1,0:T(8,128)(2,1)S(1)} %add_convert_fusion.2), channel_id=1, source_target_pairs={{0,24},{8,0},{16,8},{24,16},{1,25},{9,1},{17,9},{25,17},{2,26},{10... | collective-permute-start | bytes 552968 | tf_op jit(solution)/shard_map/ppermute | solution.py:838
  (107 other events, 1522.4 us)
Sparse Core Ops, SparseCore 0:
  11.5 80.1 all-gather.7
  129.4 75.0 all-gather.5
  388.5 76.2 reduce-scatter.3
  468.1 59.6 reduce-scatter.5
  531.1 113.3 reduce-scatter.7
  689.7 269.2 all-reduce.3
